TPU v7x, 32 devices: a whole 2x2x4 slice. The times are simulated.
32 devices in a mesh: items: 2 (over core), seq: 16 (over z, y, x).
Axes of the slice: x: 2, y: 2, z: 4, core: 2. Of those that a mesh axis runs over, the one named last changes fastest.
Arguments:
- frames: bfloat16 [2, 4096, 1024], P('items', 'seq'), may hold values from -6 to 6
- lengths: int32 [2, 3], P('items'), may hold values from 128 to 3712, as said below
- w_qkv: bfloat16 [1024, 3072], replicated, may hold values from -0.1875 to 0.1875
- w_out: bfloat16 [1024, 1024], replicated, may hold values from -3 to 3
- w_up: bfloat16 [1024, 4096], replicated, may hold values from -0.1875 to 0.1875
- w_down: bfloat16 [4096, 1024], replicated, may hold values from -0.09375 to 0.09375
- gain_one: float32 [1024], replicated, may hold values from 0.1 to 1.9
- gain_two: float32 [1024], replicated, may hold values from 0.1 to 1.9
- cotangent: bfloat16 [2, 4096, 1024], P('items', 'seq'), may hold values from -6 to 6
Outputs:
- output: bfloat16 [2, 4096, 1024], P('items', 'seq')
- grad_frames: float32 [2, 4096, 1024], P('items', 'seq')
- grad_qkv: float32 [1024, 3072], P('seq')
- grad_out: float32 [1024, 1024], P('seq')
- grad_up: float32 [1024, 4096], P('seq')
- grad_down: float32 [4096, 1024], P('seq')
- grad_gain_one: float32 [1024], P('seq')
- grad_gain_two: float32 [1024], P('seq')
Inputs may be any that keep to these rules, and one draw needn't show every extreme that they name: Each row holds a first utterance of more than 128 and fewer than 256 frames, then one of exactly 3712 frames, then one of exactly 128 frames; the lengths sum to less than 4096 and the frames after their sum are padding.
All inputs are finite; a program needn't handle non-finite values.
Results may differ from a plain program's by a relative error of at most 0.023.
Values may be sent and summed in bfloat16 or wider, within the bound.
No kernel may reach another device: no remote copies, remote signals or barrier semaphores. Data moves between devices by JAX's collectives and lax.ppermute only.
A program may use at most 320 MiB of HBM per device.

v0:
```python
import jax
import jax.numpy as jnp
from jax import lax
from jax.sharding import PartitionSpec as P

HEADS = 16
HEAD_DIM = 64


eps = 1e-05
masked = -1e30


def passed_along(array, axis, by):
    count = lax.axis_size(axis)
    return lax.ppermute(array, axis, [(i, (i + by) % count) for i in range(count)])


def norm_scaled(inputs, gain):
    centred = inputs - jnp.mean(inputs, axis=-1, keepdims=True)
    spread = jnp.mean(centred * centred, axis=-1, keepdims=True)
    return centred * lax.rsqrt(spread + eps) * gain


def labels_at(places, utter_ends):
    return jnp.sum((places[:, None] >= utter_ends[None, :]).astype(jnp.int32), axis=1)


def frame_ids(utter_ends, offset, row_count):
    places = offset + jnp.arange(row_count, dtype=jnp.int32)
    return (labels_at(places, utter_ends), places)


def needed(row_labels, row_places, col_labels, col_places):
    return (
        (row_places[-1] >= col_places[0])
        & (row_labels[-1] >= col_labels[0])
        & (row_labels[0] <= col_labels[-1])
    )


def visible(row_labels, row_places, col_labels, col_places):
    return (
        (row_labels[:, None] == col_labels[None, :]) & (row_places[:, None] >= col_places[None, :])
    )[:, None, :]


def forward_piece(state, queries, labels, places, key_rows, value_rows, key_labels, key_places):
    key_count = key_rows.shape[0]
    key_heads = key_rows.reshape(key_count, -1, HEAD_DIM)
    value_heads = value_rows.reshape(key_count, -1, HEAD_DIM)
    score_scale = HEAD_DIM ** (-0.5)

    def forward_update(current):
        running, row_peak, weight_sum = current
        scores = (
            jnp.einsum("qhd,khd->qhk", queries, key_heads, preferred_element_type=jnp.float32)
            * score_scale
        )
        allowed = visible(labels, places, key_labels, key_places)
        scores = jnp.where(allowed, scores, masked)
        new_peak = jnp.maximum(row_peak, jnp.max(scores, axis=-1, keepdims=True))
        weights = jnp.where(allowed, jnp.exp(scores - new_peak), 0.0)
        running = jnp.einsum(
            "qhk,khd->qhd",
            weights.astype(jnp.bfloat16),
            value_heads,
            preferred_element_type=jnp.float32,
        )
        weight_sum = jnp.sum(weights, axis=-1, keepdims=True)
        return (running, new_peak, weight_sum)

    return lax.cond(
        needed(labels, places, key_labels, key_places),
        forward_update,
        lambda kept_state: kept_state,
        state,
    )


def backward_piece(
    grad_query,
    queries,
    grad_heads,
    log_mass,
    row_delta,
    labels,
    places,
    key_rows,
    value_rows,
    key_labels,
    key_places,
):
    key_count = key_rows.shape[0]
    key_heads = key_rows.reshape(key_count, -1, HEAD_DIM)
    value_heads = value_rows.reshape(key_count, -1, HEAD_DIM)
    score_scale = HEAD_DIM ** (-0.5)

    def backward_update(current):
        scores = (
            jnp.einsum("qhd,khd->qhk", queries, key_heads, preferred_element_type=jnp.float32)
            * score_scale
        )
        allowed = visible(labels, places, key_labels, key_places)
        attn_probs = jnp.where(allowed, jnp.exp(scores - log_mass), 0.0)
        grad_probs = jnp.einsum(
            "qhd,khd->qhk", grad_heads, value_heads, preferred_element_type=jnp.float32
        )
        grad_scores = (attn_probs * (grad_probs - row_delta)).astype(jnp.bfloat16)
        current = current + jnp.einsum(
            "qhk,khd->qhd", grad_scores, key_heads, preferred_element_type=jnp.float32
        )
        grad_keys = jnp.einsum(
            "qhk,qhd->khd", grad_scores, queries, preferred_element_type=jnp.float32
        )
        grad_values = jnp.einsum(
            "qhk,qhd->khd",
            attn_probs.astype(jnp.bfloat16),
            grad_heads,
            preferred_element_type=jnp.float32,
        )
        return (current, grad_keys.reshape(key_count, -1), grad_values.reshape(key_count, -1))

    def skipped(current):
        nothing = jnp.zeros((key_count, key_rows.shape[1]), jnp.float32)
        return (current, nothing, nothing)

    return lax.cond(
        needed(labels, places, key_labels, key_places), backward_update, skipped, grad_query
    )


def on_device(frames, lengths, w_qkv, w_out, w_up, w_down, gain_one, gain_two, cotangent):
    row_count = frames.shape[1]
    feature_count = frames.shape[2]
    cycle_size = lax.axis_size("seq")
    my_index = lax.axis_index("seq")
    first_row = my_index * row_count
    utter_ends = jnp.cumsum(lengths[0])
    labels, places = frame_ids(utter_ends, first_row, row_count)
    present = (labels < lengths.shape[1]).astype(jnp.float32)[:, None]
    score_scale = HEAD_DIM ** (-0.5)
    inputs = frames[0].astype(jnp.float32)
    normed_one, pull_one = jax.vjp(norm_scaled, inputs, gain_one)
    low_one = normed_one.astype(jnp.bfloat16)
    packed = jnp.dot(low_one, w_qkv, preferred_element_type=jnp.float32).astype(jnp.bfloat16)
    query_rows = packed[:, :feature_count]
    queries = query_rows.reshape(row_count, HEADS, HEAD_DIM)
    key_rows = packed[:, feature_count : 2 * feature_count]
    value_rows = packed[:, 2 * feature_count :]
    start_state = (
        jnp.zeros((row_count, HEADS, HEAD_DIM), jnp.float32),
        jnp.full((row_count, HEADS, 1), masked, jnp.float32),
        jnp.zeros((row_count, HEADS, 1), jnp.float32),
    )
    pieces = (
        lax.all_gather(key_rows, "seq", axis=0, tiled=True),
        lax.all_gather(value_rows, "seq", axis=0, tiled=True),
    )
    key_labels, key_places = frame_ids(utter_ends, jnp.int32(0), pieces[0].shape[0])
    running, row_peak, weight_sum = forward_piece(
        start_state, queries, labels, places, pieces[0], pieces[1], key_labels, key_places
    )
    attended = running / weight_sum * present[:, :, None]
    log_mass = row_peak + jnp.log(weight_sum)
    attended_low = attended.reshape(row_count, feature_count).astype(jnp.bfloat16)
    middle = inputs + jnp.dot(attended_low, w_out, preferred_element_type=jnp.float32)
    normed_two, pull_two = jax.vjp(norm_scaled, middle, gain_two)
    low_two = normed_two.astype(jnp.bfloat16)
    hidden = jnp.dot(low_two, w_up, preferred_element_type=jnp.float32)
    activated, pull_gelu = jax.vjp(jax.nn.gelu, hidden)
    act_low = activated.astype(jnp.bfloat16)
    mixed = jnp.dot(act_low, w_down, preferred_element_type=jnp.float32)
    result = (present * (middle + mixed)).astype(jnp.bfloat16)
    grad_mixed = cotangent[0].astype(jnp.float32) * present
    grad_mixed_low = grad_mixed.astype(jnp.bfloat16)
    grad_down = jnp.einsum("tf,td->fd", act_low, grad_mixed_low, preferred_element_type=jnp.float32)
    grad_act = jnp.einsum("td,fd->tf", grad_mixed_low, w_down, preferred_element_type=jnp.float32)
    grad_hidden = pull_gelu(grad_act)[0].astype(jnp.bfloat16)
    grad_up = jnp.einsum("td,tf->df", low_two, grad_hidden, preferred_element_type=jnp.float32)
    grad_normed_two = jnp.einsum("tf,df->td", grad_hidden, w_up, preferred_element_type=jnp.float32)
    grad_middle_norm, grad_gain_two = pull_two(grad_normed_two)
    grad_middle = grad_mixed + grad_middle_norm
    grad_branch = grad_middle.astype(jnp.bfloat16)
    grad_out = jnp.einsum(
        "td,te->de", attended_low, grad_branch, preferred_element_type=jnp.float32
    )
    grad_attended = jnp.einsum(
        "te,de->td", grad_branch, w_out, preferred_element_type=jnp.float32
    ).astype(jnp.bfloat16) * present.astype(jnp.bfloat16)
    grad_heads = grad_attended.reshape(row_count, HEADS, HEAD_DIM)
    row_delta = jnp.sum(grad_heads.astype(jnp.float32) * attended, axis=-1, keepdims=True)
    empty_rows = jnp.zeros((row_count, feature_count), jnp.float32)
    begin = (
        key_rows,
        value_rows,
        empty_rows,
        empty_rows,
        jnp.zeros((row_count, HEADS, HEAD_DIM), jnp.float32),
    )

    def cycle_turn(turn, current):
        keys_here, values_here, keys_sum, values_sum, grad_query = current
        owner = (my_index + turn) % cycle_size
        key_labels, key_places = frame_ids(utter_ends, owner * row_count, row_count)
        grad_query, grad_key_block, grad_value_block = backward_piece(
            grad_query,
            queries,
            grad_heads,
            log_mass,
            row_delta,
            labels,
            places,
            keys_here,
            values_here,
            key_labels,
            key_places,
        )
        moved_keys, moved_values = passed_along((keys_here, values_here), "seq", -1)
        moved_sums = (
            passed_along((keys_sum + grad_key_block).astype(jnp.bfloat16), "seq", -1).astype(
                jnp.float32
            ),
            passed_along((values_sum + grad_value_block).astype(jnp.bfloat16), "seq", -1).astype(
                jnp.float32
            ),
        )
        return (moved_keys, moved_values, moved_sums[0], moved_sums[1], grad_query)

    final = lax.fori_loop(0, cycle_size, cycle_turn, begin)
    grad_keys = final[2]
    grad_values = final[3]
    grad_query = final[4].reshape(row_count, feature_count)
    grad_packed = jnp.concatenate(
        [grad_query * score_scale, grad_keys * score_scale, grad_values], axis=1
    ).astype(jnp.bfloat16)
    grad_qkv = jnp.einsum("td,te->de", low_one, grad_packed, preferred_element_type=jnp.float32)
    grad_normed_one = jnp.einsum(
        "te,de->td", grad_packed, w_qkv, preferred_element_type=jnp.float32
    )
    grad_inputs_norm, grad_gain_one = pull_one(grad_normed_one)
    grad_inputs = grad_middle + grad_inputs_norm
    summed = (
        lax.psum_scatter(
            grad_qkv.astype(jnp.bfloat16), "seq", scatter_dimension=0, tiled=True
        ).astype(jnp.float32),
        lax.psum_scatter(
            grad_out.astype(jnp.bfloat16), "seq", scatter_dimension=0, tiled=True
        ).astype(jnp.float32),
        lax.psum_scatter(
            grad_up.astype(jnp.bfloat16), "seq", scatter_dimension=0, tiled=True
        ).astype(jnp.float32),
        lax.psum_scatter(
            grad_down.astype(jnp.bfloat16), "seq", scatter_dimension=0, tiled=True
        ).astype(jnp.float32),
        lax.psum_scatter(
            grad_gain_one.astype(jnp.bfloat16), "seq", scatter_dimension=0, tiled=True
        ).astype(jnp.float32),
        lax.psum_scatter(
            grad_gain_two.astype(jnp.bfloat16), "seq", scatter_dimension=0, tiled=True
        ).astype(jnp.float32),
    )
    summed = (
        lax.psum(summed[0].astype(jnp.bfloat16), "items").astype(jnp.float32),
        lax.psum(summed[1].astype(jnp.bfloat16), "items").astype(jnp.float32),
        lax.psum(summed[2].astype(jnp.bfloat16), "items").astype(jnp.float32),
        lax.psum(summed[3].astype(jnp.bfloat16), "items").astype(jnp.float32),
        lax.psum(summed[4].astype(jnp.bfloat16), "items").astype(jnp.float32),
        lax.psum(summed[5].astype(jnp.bfloat16), "items").astype(jnp.float32),
    )
    summed_qkv, summed_out, summed_up, summed_down, summed_gain_one, summed_gain_two = summed
    return (
        result[None],
        grad_inputs[None],
        summed_qkv,
        summed_out,
        summed_up,
        summed_down,
        summed_gain_one,
        summed_gain_two,
    )


def solution(mesh):
    return jax.shard_map(
        on_device,
        mesh=mesh,
        in_specs=(
            P("items", "seq", None),
            P("items", None),
            P(),
            P(),
            P(),
            P(),
            P(),
            P(),
            P("items", "seq", None),
        ),
        out_specs=(
            P("items", "seq", None),
            P("items", "seq", None),
            P("seq", None),
            P("seq", None),
            P("seq", None),
            P("seq", None),
            P("seq"),
            P("seq"),
        ),
        check_vma=False,
    )
```

profile of v0, /device:TPU:0, one launch (start us, length us, event | category | flops | bytes accessed | tf_op | source)
XLA Modules:
  0.0 1952.5 jit_solution(12190190093098558019)
XLA Ops:
  26.8 105.5 %all-gather.3.cloned.1.call-done = bf16[4096,1024]{1,0:T(8,128)(2,1)} async-done(((bf16[256,1024]{1,0:T(8,128)(2,1)}), bf16[4096,1024]{1,0:T(8,128)(2,1)}) %all-gather.3.cloned.1.call-update) | async-done | bytes 8388624 | tf_op jit(solution)/shard_map/all_gather | solution.py:157
  132.3 114.4 %all-gather.5.cloned.1.call-done = bf16[4096,1024]{1,0:T(8,128)(2,1)} async-done(((bf16[256,1024]{1,0:T(8,128)(2,1)}), bf16[4096,1024]{1,0:T(8,128)(2,1)}) %all-gather.5.cloned.1.call-update) | async-done | bytes 8388624 | tf_op jit(solution)/shard_map/all_gather | solution.py:158
  246.7 106.3 %conditional.2 = (f32[256,16,64]{0,2,1:T(8,128)}, f32[256,16,1]{0,1,2:T(8,128)S(1)}, f32[256,16,1]{0,1,2:T(8,128)S(1)}) conditional(s32[]{:T(128)} %bitcast.20, () %tuple.53, (s32[256]{0:T(256)S(1)}, s32[4096]{0:T(1024)S(1)}, s32[256]{0:T(256)S(1)}, s32[4096]{0:T(1024)S(1)}, bf16[4096,1024]{1,0:T(8,128)(2,1)}, ...), branch_computations={%region_5.6_spmd.clone, %region_6.9_spmd.clone} | conditional | flops 4516220928 | bytes 257738848 | solution.py:73
  251.1 11.3 copy.67
  262.4 29.0 %fusion.16 = (f32[256,16]{0,1:T(8,128)S(1)}, f32[16,4096,256]{2,1,0:T(8,128)}) fusion(pred[256,4096]{0,1:T(8,128)(4,1)} %compare_and_fusion.1, bf16[4096,16,64]{0,2,1:T(8,128)(2,1)} %bitcast.151, bf16[256,16,64]{0,2,1:T(8,128)(2,1)S(1)} %get-tuple-element.559), kind=kOutput, calls=%fused_computation.25 | convolution fusion | flops 2197811200 | bytes 77086720 | tf_op jit(solution)/shard_map/cond/branch_1_fun/qhd,khd->qhk/dot_general | solution.py:57
  291.4 22.0 %fusion.17 = f32[256,16]{0,1:T(8,128)S(1)} fusion(f32[16,4096,256]{2,1,0:T(8,128)} %get-tuple-element.611, f32[256,16]{0,1:T(8,128)S(1)} %broadcast_maximum_fusion, pred[256,4096]{0,1:T(8,128)(4,1)} %compare_and_fusion.1), kind=kLoop, calls=%fused_computation.26 | loop fusion | flops 83881984 | bytes 68190208 | tf_op jit(solution)/shard_map/cond/branch_1_fun/reduce_sum | solution.py:70
  313.5 11.3 copy.68
  324.8 28.1 %fusion.22 = f32[256,16,64]{0,2,1:T(8,128)} fusion(bf16[4096,16,64]{0,2,1:T(8,128)(2,1)} %bitcast.152, f32[16,4096,256]{2,1,0:T(8,128)} %get-tuple-element.611, f32[256,16]{0,1:T(8,128)S(1)} %broadcast_maximum_fusion, pred[256,4096]{0,1:T(8,128)(4,1)} %compare_and_fusion.1), kind=kOutput, calls=%fused_computation.31 | convolution fusion | flops 2231369728 | bytes 77611008 | tf_op jit(solution)/shard_map/cond/branch_1_fun/qhk,khd->qhd/dot_general | solution.py:64
  364.6 11.3 fusion.34
  390.7 970.8 %while.27 = (s32[]{:T(128)}, bf16[256,1024]{0,1:T(8,128)(2,1)S(1)}, bf16[256,1024]{0,1:T(8,128)(2,1)S(1)}, f32[256,1024]{0,1:T(8,128)}, f32[256,1024]{0,1:T(8,12...) while((s32[]{:T(128)}, bf16[256,1024]{0,1:T(8,128)(2,1)S(1)}, ...), condition=%wide.region_18.19_spmd.clone, body=%wide.region_14.0_spmd.clone.sunk | while | flops 684132608 | bytes 54255336 | solution.py:230
  423.1 10.1 collective-permute-done.3
  434.2 10.2 collective-permute-done
  444.4 10.6 collective-permute-done.1
  464.6 13.3 collective-permute-start.2
  480.2 10.4 collective-permute-done.2
  491.7 10.1 collective-permute-done.3
  502.9 10.1 collective-permute-done
  512.9 13.0 collective-permute-done.1
  535.6 12.7 collective-permute-start.2
  550.6 10.4 collective-permute-done.2
  562.1 10.1 collective-permute-done.3
  573.3 11.3 collective-permute-done
  603.9 12.6 collective-permute-start.2
  618.7 10.4 collective-permute-done.2
  630.3 10.1 collective-permute-done.3
  641.5 10.1 collective-permute-done
  668.4 12.6 collective-permute-start.2
  683.2 10.4 collective-permute-done.2
  694.8 10.1 collective-permute-done.3
  706.0 10.1 collective-permute-done
  732.0 12.6 collective-permute-start.2
  746.8 10.4 collective-permute-done.2
  758.4 10.1 collective-permute-done.3
  769.6 9.8 collective-permute-done
  794.7 12.6 collective-permute-start.2
  809.5 10.4 collective-permute-done.2
  821.1 10.1 collective-permute-done.3
  856.5 12.6 collective-permute-start.2
  871.3 10.4 collective-permute-done.2
  882.9 10.1 collective-permute-done.3
  917.3 12.6 collective-permute-start.2
  932.2 10.4 collective-permute-done.2
  943.7 10.1 collective-permute-done.3
  977.3 12.6 collective-permute-start.2
  992.1 10.4 collective-permute-done.2
  1003.7 10.1 collective-permute-done.3
  1036.3 12.6 collective-permute-start.2
  1051.1 10.4 collective-permute-done.2
  1062.7 10.1 collective-permute-done.3
  1094.4 12.6 collective-permute-start.2
  1109.2 10.4 collective-permute-done.2
  1120.8 9.9 collective-permute-done.3
  1151.6 12.6 collective-permute-start.2
  1166.4 10.4 collective-permute-done.2
  1207.8 12.6 collective-permute-start.2
  1222.7 10.4 collective-permute-done.2
  1263.2 12.6 collective-permute-start.2
  1278.0 10.4 collective-permute-done.2
  1317.6 12.6 collective-permute-start.2
  1332.4 10.4 collective-permute-done.2
  1397.8 121.1 %reduce-scatter.5.cloned.1.call-done = bf16[64,3072]{1,0:T(8,128)(2,1)} async-done(((bf16[1024,3072]{1,0:T(8,128)(2,1)}), bf16[64,3072]{1,0:T(8,128)(2,1)}) %reduce-scatter.5.cloned.1.call-update) | async-done | bytes 393232 | tf_op jit(solution)/shard_map/reduce_scatter | solution.py:244
  1518.9 179.2 %reduce-scatter.9.cloned.1.call-done = bf16[64,4096]{1,0:T(8,128)(2,1)} async-done(((bf16[1024,4096]{1,0:T(8,128)(2,1)}), bf16[64,4096]{1,0:T(8,128)(2,1)}) %reduce-scatter.9.cloned.1.call-update) | async-done | bytes 524304 | tf_op jit(solution)/shard_map/reduce_scatter | solution.py:250
  1698.1 182.4 %reduce-scatter.11.cloned.1.call-done = bf16[256,1024]{1,0:T(8,128)(2,1)} async-done(((bf16[4096,1024]{1,0:T(8,128)(2,1)}), bf16[256,1024]{1,0:T(8,128)(2,1)}) %reduce-scatter.11.cloned.1.call-update) | async-done | bytes 524304 | tf_op jit(solution)/shard_map/reduce_scatter | solution.py:253
  1882.3 42.4 %all-reduce.2 = (bf16[1024]{0:T(1024)(128)(2,1)S(1)}, bf16[1024]{0:T(1024)(128)(2,1)S(1)}) all-reduce(bf16[1024]{0:T(1024)(128)(2,1)S(1)} %get-tuple-element.566, bf16[1024]{0:T(1024)(128)(2,1)S(1)} %get-tuple-element.564), channel_id=6, replica_groups=mesh['items'=2,'seq'=16] {'seq'}, use_global_device_ids=true, to_apply=%region_30.31.clone | all-reduce | flops 2048 | bytes 8192
  (526 shorter events, 471.6 us)
Async XLA Ops:
  7.2 125.1 %all-gather.3.cloned.1.call-start = ((), (), s32[]{:S(2)}) async-start(), calls=%async_computation.4 | async-start | bytes 8912896 | tf_op jit(solution)/shard_map/all_gather | solution.py:157
  16.6 230.1 %all-gather.5.cloned.1.call-start = ((), (), s32[]{:S(2)}) async-start(), calls=%async_computation.5 | async-start | bytes 8912896 | tf_op jit(solution)/shard_map/all_gather | solution.py:158
  17.4 1380.4 %reduce-scatter.7.cloned.1.call-start = ((), (), s32[]{:S(2)}) async-start(), calls=%async_computation.7 | async-start | bytes 2228224 | tf_op jit(solution)/shard_map/reduce_scatter | solution.py:247
  389.4 1129.6 %reduce-scatter.5.cloned.1.call-start = ((), (), s32[]{:S(2)}) async-start(), calls=%async_computation.6 | async-start | bytes 6684672 | tf_op jit(solution)/shard_map/reduce_scatter | solution.py:244
  408.8 24.4 %collective-permute-start.3 = (bf16[256,1024]{0,1:T(8,128)(2,1)}, bf16[256,1024]{0,1:T(8,128)(2,1)S(1)}, u32[]{:S(2)}, u32[]{:S(2)}) collective-permute-start(bf16[256,1024]{0,1:T(8,128)(2,1)} %fusion.111), channel_id=1, source_target_pairs={{0,15},{1,0},{2,1},{3,2},{4,3},{5,4},{6,5},{7,6},{8,7},{9,8},{10,9... | collective-permute-start | bytes 1572872 | tf_op jit(solution)/shard_map/while/body/eval_jaxpr/ppermute | solution.py:16
  410.3 34.2 %collective-permute-start = (bf16[256,1024]{0,1:T(8,128)(2,1)S(1)}, bf16[256,1024]{0,1:T(8,128)(2,1)S(1)}, u32[]{:S(2)}, u32[]{:S(2)}) collective-permute-start(bf16[256,1024]{0,1:T(8,128)(2,1)S(1)} %copy.88), channel_id=1, source_target_pairs={{0,15},{1,0},{2,1},{3,2},{4,3},{5,4},{6,5},{7,6},{8,7},{9,8},{10,9... | collective-permute-start | bytes 1572872 | tf_op jit(solution)/shard_map/while/body/eval_jaxpr/ppermute | solution.py:16
  411.5 43.5 %collective-permute-start.1 = (bf16[256,1024]{0,1:T(8,128)(2,1)}, bf16[256,1024]{0,1:T(8,128)(2,1)S(1)}, u32[]{:S(2)}, u32[]{:S(2)}) collective-permute-start(bf16[256,1024]{0,1:T(8,128)(2,1)} %copy.89), channel_id=1, source_target_pairs={{0,15},{1,0},{2,1},{3,2},{4,3},{5,4},{6,5},{7,6},{8,7},{9,8},{10,9... | collective-permute-start | bytes 1572872 | tf_op jit(solution)/shard_map/while/body/eval_jaxpr/ppermute | solution.py:16
  464.6 25.9 %collective-permute-start.2 = (bf16[256,1024]{0,1:T(8,128)(2,1)}, bf16[256,1024]{0,1:T(8,128)(2,1)S(1)}, u32[]{:S(2)}, u32[]{:S(2)}) collective-permute-start(bf16[256,1024]{0,1:T(8,128)(2,1)} %fusion.110), channel_id=1, source_target_pairs={{0,15},{1,0},{2,1},{3,2},{4,3},{5,4},{6,5},{7,6},{8,7},{9,8},{10,9... | collective-permute-start | bytes 1572872 | tf_op jit(solution)/shard_map/while/body/eval_jaxpr/ppermute | solution.py:16
  480.1 32.8 %collective-permute-start = (bf16[256,1024]{0,1:T(8,128)(2,1)S(1)}, bf16[256,1024]{0,1:T(8,128)(2,1)S(1)}, u32[]{:S(2)}, u32[]{:S(2)}) collective-permute-start(bf16[256,1024]{0,1:T(8,128)(2,1)S(1)} %copy.88), channel_id=1, source_target_pairs={{0,15},{1,0},{2,1},{3,2},{4,3},{5,4},{6,5},{7,6},{8,7},{9,8},{10,9... | collective-permute-start | bytes 1572872 | tf_op jit(solution)/shard_map/while/body/eval_jaxpr/ppermute | solution.py:16
  480.1 45.8 %collective-permute-start.1 = (bf16[256,1024]{0,1:T(8,128)(2,1)}, bf16[256,1024]{0,1:T(8,128)(2,1)S(1)}, u32[]{:S(2)}, u32[]{:S(2)}) collective-permute-start(bf16[256,1024]{0,1:T(8,128)(2,1)} %copy.89), channel_id=1, source_target_pairs={{0,15},{1,0},{2,1},{3,2},{4,3},{5,4},{6,5},{7,6},{8,7},{9,8},{10,9... | collective-permute-start | bytes 1572872 | tf_op jit(solution)/shard_map/while/body/eval_jaxpr/ppermute | solution.py:16
  535.6 25.4 %collective-permute-start.2 = (bf16[256,1024]{0,1:T(8,128)(2,1)}, bf16[256,1024]{0,1:T(8,128)(2,1)S(1)}, u32[]{:S(2)}, u32[]{:S(2)}) collective-permute-start(bf16[256,1024]{0,1:T(8,128)(2,1)} %fusion.110), channel_id=1, source_target_pairs={{0,15},{1,0},{2,1},{3,2},{4,3},{5,4},{6,5},{7,6},{8,7},{9,8},{10,9... | collective-permute-start | bytes 1572872 | tf_op jit(solution)/shard_map/while/body/eval_jaxpr/ppermute | solution.py:16
  550.5 21.8 %collective-permute-start.3 = (bf16[256,1024]{0,1:T(8,128)(2,1)}, bf16[256,1024]{0,1:T(8,128)(2,1)S(1)}, u32[]{:S(2)}, u32[]{:S(2)}) collective-permute-start(bf16[256,1024]{0,1:T(8,128)(2,1)} %fusion.111), channel_id=1, source_target_pairs={{0,15},{1,0},{2,1},{3,2},{4,3},{5,4},{6,5},{7,6},{8,7},{9,8},{10,9... | collective-permute-start | bytes 1572872 | tf_op jit(solution)/shard_map/while/body/eval_jaxpr/ppermute | solution.py:16
  550.5 34.1 %collective-permute-start = (bf16[256,1024]{0,1:T(8,128)(2,1)S(1)}, bf16[256,1024]{0,1:T(8,128)(2,1)S(1)}, u32[]{:S(2)}, u32[]{:S(2)}) collective-permute-start(bf16[256,1024]{0,1:T(8,128)(2,1)S(1)} %copy.88), channel_id=1, source_target_pairs={{0,15},{1,0},{2,1},{3,2},{4,3},{5,4},{6,5},{7,6},{8,7},{9,8},{10,9... | collective-permute-start | bytes 1572872 | tf_op jit(solution)/shard_map/while/body/eval_jaxpr/ppermute | solution.py:16
  550.5 43.7 %collective-permute-start.1 = (bf16[256,1024]{0,1:T(8,128)(2,1)}, bf16[256,1024]{0,1:T(8,128)(2,1)S(1)}, u32[]{:S(2)}, u32[]{:S(2)}) collective-permute-start(bf16[256,1024]{0,1:T(8,128)(2,1)} %copy.89), channel_id=1, source_target_pairs={{0,15},{1,0},{2,1},{3,2},{4,3},{5,4},{6,5},{7,6},{8,7},{9,8},{10,9... | collective-permute-start | bytes 1572872 | tf_op jit(solution)/shard_map/while/body/eval_jaxpr/ppermute | solution.py:16
  603.9 25.3 %collective-permute-start.2 = (bf16[256,1024]{0,1:T(8,128)(2,1)}, bf16[256,1024]{0,1:T(8,128)(2,1)S(1)}, u32[]{:S(2)}, u32[]{:S(2)}) collective-permute-start(bf16[256,1024]{0,1:T(8,128)(2,1)} %fusion.110), channel_id=1, source_target_pairs={{0,15},{1,0},{2,1},{3,2},{4,3},{5,4},{6,5},{7,6},{8,7},{9,8},{10,9... | collective-permute-start | bytes 1572872 | tf_op jit(solution)/shard_map/while/body/eval_jaxpr/ppermute | solution.py:16
  618.6 21.8 %collective-permute-start.3 = (bf16[256,1024]{0,1:T(8,128)(2,1)}, bf16[256,1024]{0,1:T(8,128)(2,1)S(1)}, u32[]{:S(2)}, u32[]{:S(2)}) collective-permute-start(bf16[256,1024]{0,1:T(8,128)(2,1)} %fusion.111), channel_id=1, source_target_pairs={{0,15},{1,0},{2,1},{3,2},{4,3},{5,4},{6,5},{7,6},{8,7},{9,8},{10,9... | collective-permute-start | bytes 1572872 | tf_op jit(solution)/shard_map/while/body/eval_jaxpr/ppermute | solution.py:16
  618.6 32.9 %collective-permute-start = (bf16[256,1024]{0,1:T(8,128)(2,1)S(1)}, bf16[256,1024]{0,1:T(8,128)(2,1)S(1)}, u32[]{:S(2)}, u32[]{:S(2)}) collective-permute-start(bf16[256,1024]{0,1:T(8,128)(2,1)S(1)} %copy.88), channel_id=1, source_target_pairs={{0,15},{1,0},{2,1},{3,2},{4,3},{5,4},{6,5},{7,6},{8,7},{9,8},{10,9... | collective-permute-start | bytes 1572872 | tf_op jit(solution)/shard_map/while/body/eval_jaxpr/ppermute | solution.py:16
  618.7 40.1 %collective-permute-start.1 = (bf16[256,1024]{0,1:T(8,128)(2,1)}, bf16[256,1024]{0,1:T(8,128)(2,1)S(1)}, u32[]{:S(2)}, u32[]{:S(2)}) collective-permute-start(bf16[256,1024]{0,1:T(8,128)(2,1)} %copy.89), channel_id=1, source_target_pairs={{0,15},{1,0},{2,1},{3,2},{4,3},{5,4},{6,5},{7,6},{8,7},{9,8},{10,9... | collective-permute-start | bytes 1572872 | tf_op jit(solution)/shard_map/while/body/eval_jaxpr/ppermute | solution.py:16
  668.4 25.3 %collective-permute-start.2 = (bf16[256,1024]{0,1:T(8,128)(2,1)}, bf16[256,1024]{0,1:T(8,128)(2,1)S(1)}, u32[]{:S(2)}, u32[]{:S(2)}) collective-permute-start(bf16[256,1024]{0,1:T(8,128)(2,1)} %fusion.110), channel_id=1, source_target_pairs={{0,15},{1,0},{2,1},{3,2},{4,3},{5,4},{6,5},{7,6},{8,7},{9,8},{10,9... | collective-permute-start | bytes 1572872 | tf_op jit(solution)/shard_map/while/body/eval_jaxpr/ppermute | solution.py:16
  683.2 21.8 %collective-permute-start.3 = (bf16[256,1024]{0,1:T(8,128)(2,1)}, bf16[256,1024]{0,1:T(8,128)(2,1)S(1)}, u32[]{:S(2)}, u32[]{:S(2)}) collective-permute-start(bf16[256,1024]{0,1:T(8,128)(2,1)} %fusion.111), channel_id=1, source_target_pairs={{0,15},{1,0},{2,1},{3,2},{4,3},{5,4},{6,5},{7,6},{8,7},{9,8},{10,9... | collective-permute-start | bytes 1572872 | tf_op jit(solution)/shard_map/while/body/eval_jaxpr/ppermute | solution.py:16
  683.2 32.9 %collective-permute-start = (bf16[256,1024]{0,1:T(8,128)(2,1)S(1)}, bf16[256,1024]{0,1:T(8,128)(2,1)S(1)}, u32[]{:S(2)}, u32[]{:S(2)}) collective-permute-start(bf16[256,1024]{0,1:T(8,128)(2,1)S(1)} %copy.88), channel_id=1, source_target_pairs={{0,15},{1,0},{2,1},{3,2},{4,3},{5,4},{6,5},{7,6},{8,7},{9,8},{10,9... | collective-permute-start | bytes 1572872 | tf_op jit(solution)/shard_map/while/body/eval_jaxpr/ppermute | solution.py:16
  683.2 39.2 %collective-permute-start.1 = (bf16[256,1024]{0,1:T(8,128)(2,1)}, bf16[256,1024]{0,1:T(8,128)(2,1)S(1)}, u32[]{:S(2)}, u32[]{:S(2)}) collective-permute-start(bf16[256,1024]{0,1:T(8,128)(2,1)} %copy.89), channel_id=1, source_target_pairs={{0,15},{1,0},{2,1},{3,2},{4,3},{5,4},{6,5},{7,6},{8,7},{9,8},{10,9... | collective-permute-start | bytes 1572872 | tf_op jit(solution)/shard_map/while/body/eval_jaxpr/ppermute | solution.py:16
  732.0 25.3 %collective-permute-start.2 = (bf16[256,1024]{0,1:T(8,128)(2,1)}, bf16[256,1024]{0,1:T(8,128)(2,1)S(1)}, u32[]{:S(2)}, u32[]{:S(2)}) collective-permute-start(bf16[256,1024]{0,1:T(8,128)(2,1)} %fusion.110), channel_id=1, source_target_pairs={{0,15},{1,0},{2,1},{3,2},{4,3},{5,4},{6,5},{7,6},{8,7},{9,8},{10,9... | collective-permute-start | bytes 1572872 | tf_op jit(solution)/shard_map/while/body/eval_jaxpr/ppermute | solution.py:16
  746.8 21.8 %collective-permute-start.3 = (bf16[256,1024]{0,1:T(8,128)(2,1)}, bf16[256,1024]{0,1:T(8,128)(2,1)S(1)}, u32[]{:S(2)}, u32[]{:S(2)}) collective-permute-start(bf16[256,1024]{0,1:T(8,128)(2,1)} %fusion.111), channel_id=1, source_target_pairs={{0,15},{1,0},{2,1},{3,2},{4,3},{5,4},{6,5},{7,6},{8,7},{9,8},{10,9... | collective-permute-start | bytes 1572872 | tf_op jit(solution)/shard_map/while/body/eval_jaxpr/ppermute | solution.py:16
  746.8 32.6 %collective-permute-start = (bf16[256,1024]{0,1:T(8,128)(2,1)S(1)}, bf16[256,1024]{0,1:T(8,128)(2,1)S(1)}, u32[]{:S(2)}, u32[]{:S(2)}) collective-permute-start(bf16[256,1024]{0,1:T(8,128)(2,1)S(1)} %copy.88), channel_id=1, source_target_pairs={{0,15},{1,0},{2,1},{3,2},{4,3},{5,4},{6,5},{7,6},{8,7},{9,8},{10,9... | collective-permute-start | bytes 1572872 | tf_op jit(solution)/shard_map/while/body/eval_jaxpr/ppermute | solution.py:16
  746.8 38.3 %collective-permute-start.1 = (bf16[256,1024]{0,1:T(8,128)(2,1)}, bf16[256,1024]{0,1:T(8,128)(2,1)S(1)}, u32[]{:S(2)}, u32[]{:S(2)}) collective-permute-start(bf16[256,1024]{0,1:T(8,128)(2,1)} %copy.89), channel_id=1, source_target_pairs={{0,15},{1,0},{2,1},{3,2},{4,3},{5,4},{6,5},{7,6},{8,7},{9,8},{10,9... | collective-permute-start | bytes 1572872 | tf_op jit(solution)/shard_map/while/body/eval_jaxpr/ppermute | solution.py:16
  794.7 25.3 %collective-permute-start.2 = (bf16[256,1024]{0,1:T(8,128)(2,1)}, bf16[256,1024]{0,1:T(8,128)(2,1)S(1)}, u32[]{:S(2)}, u32[]{:S(2)}) collective-permute-start(bf16[256,1024]{0,1:T(8,128)(2,1)} %fusion.110), channel_id=1, source_target_pairs={{0,15},{1,0},{2,1},{3,2},{4,3},{5,4},{6,5},{7,6},{8,7},{9,8},{10,9... | collective-permute-start | bytes 1572872 | tf_op jit(solution)/shard_map/while/body/eval_jaxpr/ppermute | solution.py:16
  809.4 21.8 %collective-permute-start.3 = (bf16[256,1024]{0,1:T(8,128)(2,1)}, bf16[256,1024]{0,1:T(8,128)(2,1)S(1)}, u32[]{:S(2)}, u32[]{:S(2)}) collective-permute-start(bf16[256,1024]{0,1:T(8,128)(2,1)} %fusion.111), channel_id=1, source_target_pairs={{0,15},{1,0},{2,1},{3,2},{4,3},{5,4},{6,5},{7,6},{8,7},{9,8},{10,9... | collective-permute-start | bytes 1572872 | tf_op jit(solution)/shard_map/while/body/eval_jaxpr/ppermute | solution.py:16
  809.5 31.7 %collective-permute-start = (bf16[256,1024]{0,1:T(8,128)(2,1)S(1)}, bf16[256,1024]{0,1:T(8,128)(2,1)S(1)}, u32[]{:S(2)}, u32[]{:S(2)}) collective-permute-start(bf16[256,1024]{0,1:T(8,128)(2,1)S(1)} %copy.88), channel_id=1, source_target_pairs={{0,15},{1,0},{2,1},{3,2},{4,3},{5,4},{6,5},{7,6},{8,7},{9,8},{10,9... | collective-permute-start | bytes 1572872 | tf_op jit(solution)/shard_map/while/body/eval_jaxpr/ppermute | solution.py:16
  809.5 37.3 %collective-permute-start.1 = (bf16[256,1024]{0,1:T(8,128)(2,1)}, bf16[256,1024]{0,1:T(8,128)(2,1)S(1)}, u32[]{:S(2)}, u32[]{:S(2)}) collective-permute-start(bf16[256,1024]{0,1:T(8,128)(2,1)} %copy.89), channel_id=1, source_target_pairs={{0,15},{1,0},{2,1},{3,2},{4,3},{5,4},{6,5},{7,6},{8,7},{9,8},{10,9... | collective-permute-start | bytes 1572872 | tf_op jit(solution)/shard_map/while/body/eval_jaxpr/ppermute | solution.py:16
  856.5 25.3 %collective-permute-start.2 = (bf16[256,1024]{0,1:T(8,128)(2,1)}, bf16[256,1024]{0,1:T(8,128)(2,1)S(1)}, u32[]{:S(2)}, u32[]{:S(2)}) collective-permute-start(bf16[256,1024]{0,1:T(8,128)(2,1)} %fusion.110), channel_id=1, source_target_pairs={{0,15},{1,0},{2,1},{3,2},{4,3},{5,4},{6,5},{7,6},{8,7},{9,8},{10,9... | collective-permute-start | bytes 1572872 | tf_op jit(solution)/shard_map/while/body/eval_jaxpr/ppermute | solution.py:16
  871.2 21.8 %collective-permute-start.3 = (bf16[256,1024]{0,1:T(8,128)(2,1)}, bf16[256,1024]{0,1:T(8,128)(2,1)S(1)}, u32[]{:S(2)}, u32[]{:S(2)}) collective-permute-start(bf16[256,1024]{0,1:T(8,128)(2,1)} %fusion.111), channel_id=1, source_target_pairs={{0,15},{1,0},{2,1},{3,2},{4,3},{5,4},{6,5},{7,6},{8,7},{9,8},{10,9... | collective-permute-start | bytes 1572872 | tf_op jit(solution)/shard_map/while/body/eval_jaxpr/ppermute | solution.py:16
  871.2 30.8 %collective-permute-start = (bf16[256,1024]{0,1:T(8,128)(2,1)S(1)}, bf16[256,1024]{0,1:T(8,128)(2,1)S(1)}, u32[]{:S(2)}, u32[]{:S(2)}) collective-permute-start(bf16[256,1024]{0,1:T(8,128)(2,1)S(1)} %copy.88), channel_id=1, source_target_pairs={{0,15},{1,0},{2,1},{3,2},{4,3},{5,4},{6,5},{7,6},{8,7},{9,8},{10,9... | collective-permute-start | bytes 1572872 | tf_op jit(solution)/shard_map/while/body/eval_jaxpr/ppermute | solution.py:16
  871.3 36.4 %collective-permute-start.1 = (bf16[256,1024]{0,1:T(8,128)(2,1)}, bf16[256,1024]{0,1:T(8,128)(2,1)S(1)}, u32[]{:S(2)}, u32[]{:S(2)}) collective-permute-start(bf16[256,1024]{0,1:T(8,128)(2,1)} %copy.89), channel_id=1, source_target_pairs={{0,15},{1,0},{2,1},{3,2},{4,3},{5,4},{6,5},{7,6},{8,7},{9,8},{10,9... | collective-permute-start | bytes 1572872 | tf_op jit(solution)/shard_map/while/body/eval_jaxpr/ppermute | solution.py:16
  917.3 25.3 %collective-permute-start.2 = (bf16[256,1024]{0,1:T(8,128)(2,1)}, bf16[256,1024]{0,1:T(8,128)(2,1)S(1)}, u32[]{:S(2)}, u32[]{:S(2)}) collective-permute-start(bf16[256,1024]{0,1:T(8,128)(2,1)} %fusion.110), channel_id=1, source_target_pairs={{0,15},{1,0},{2,1},{3,2},{4,3},{5,4},{6,5},{7,6},{8,7},{9,8},{10,9... | collective-permute-start | bytes 1572872 | tf_op jit(solution)/shard_map/while/body/eval_jaxpr/ppermute | solution.py:16
  932.1 21.8 %collective-permute-start.3 = (bf16[256,1024]{0,1:T(8,128)(2,1)}, bf16[256,1024]{0,1:T(8,128)(2,1)S(1)}, u32[]{:S(2)}, u32[]{:S(2)}) collective-permute-start(bf16[256,1024]{0,1:T(8,128)(2,1)} %fusion.111), channel_id=1, source_target_pairs={{0,15},{1,0},{2,1},{3,2},{4,3},{5,4},{6,5},{7,6},{8,7},{9,8},{10,9... | collective-permute-start | bytes 1572872 | tf_op jit(solution)/shard_map/while/body/eval_jaxpr/ppermute | solution.py:16
  932.1 29.8 %collective-permute-start = (bf16[256,1024]{0,1:T(8,128)(2,1)S(1)}, bf16[256,1024]{0,1:T(8,128)(2,1)S(1)}, u32[]{:S(2)}, u32[]{:S(2)}) collective-permute-start(bf16[256,1024]{0,1:T(8,128)(2,1)S(1)} %copy.88), channel_id=1, source_target_pairs={{0,15},{1,0},{2,1},{3,2},{4,3},{5,4},{6,5},{7,6},{8,7},{9,8},{10,9... | collective-permute-start | bytes 1572872 | tf_op jit(solution)/shard_map/while/body/eval_jaxpr/ppermute | solution.py:16
  932.1 35.5 %collective-permute-start.1 = (bf16[256,1024]{0,1:T(8,128)(2,1)}, bf16[256,1024]{0,1:T(8,128)(2,1)S(1)}, u32[]{:S(2)}, u32[]{:S(2)}) collective-permute-start(bf16[256,1024]{0,1:T(8,128)(2,1)} %copy.89), channel_id=1, source_target_pairs={{0,15},{1,0},{2,1},{3,2},{4,3},{5,4},{6,5},{7,6},{8,7},{9,8},{10,9... | collective-permute-start | bytes 1572872 | tf_op jit(solution)/shard_map/while/body/eval_jaxpr/ppermute | solution.py:16
  977.3 25.3 %collective-permute-start.2 = (bf16[256,1024]{0,1:T(8,128)(2,1)}, bf16[256,1024]{0,1:T(8,128)(2,1)S(1)}, u32[]{:S(2)}, u32[]{:S(2)}) collective-permute-start(bf16[256,1024]{0,1:T(8,128)(2,1)} %fusion.110), channel_id=1, source_target_pairs={{0,15},{1,0},{2,1},{3,2},{4,3},{5,4},{6,5},{7,6},{8,7},{9,8},{10,9... | collective-permute-start | bytes 1572872 | tf_op jit(solution)/shard_map/while/body/eval_jaxpr/ppermute | solution.py:16
  992.0 21.8 %collective-permute-start.3 = (bf16[256,1024]{0,1:T(8,128)(2,1)}, bf16[256,1024]{0,1:T(8,128)(2,1)S(1)}, u32[]{:S(2)}, u32[]{:S(2)}) collective-permute-start(bf16[256,1024]{0,1:T(8,128)(2,1)} %fusion.111), channel_id=1, source_target_pairs={{0,15},{1,0},{2,1},{3,2},{4,3},{5,4},{6,5},{7,6},{8,7},{9,8},{10,9... | collective-permute-start | bytes 1572872 | tf_op jit(solution)/shard_map/while/body/eval_jaxpr/ppermute | solution.py:16
  992.1 28.9 %collective-permute-start = (bf16[256,1024]{0,1:T(8,128)(2,1)S(1)}, bf16[256,1024]{0,1:T(8,128)(2,1)S(1)}, u32[]{:S(2)}, u32[]{:S(2)}) collective-permute-start(bf16[256,1024]{0,1:T(8,128)(2,1)S(1)} %copy.88), channel_id=1, source_target_pairs={{0,15},{1,0},{2,1},{3,2},{4,3},{5,4},{6,5},{7,6},{8,7},{9,8},{10,9... | collective-permute-start | bytes 1572872 | tf_op jit(solution)/shard_map/while/body/eval_jaxpr/ppermute | solution.py:16
  992.1 34.6 %collective-permute-start.1 = (bf16[256,1024]{0,1:T(8,128)(2,1)}, bf16[256,1024]{0,1:T(8,128)(2,1)S(1)}, u32[]{:S(2)}, u32[]{:S(2)}) collective-permute-start(bf16[256,1024]{0,1:T(8,128)(2,1)} %copy.89), channel_id=1, source_target_pairs={{0,15},{1,0},{2,1},{3,2},{4,3},{5,4},{6,5},{7,6},{8,7},{9,8},{10,9... | collective-permute-start | bytes 1572872 | tf_op jit(solution)/shard_map/while/body/eval_jaxpr/ppermute | solution.py:16
  1036.3 25.3 %collective-permute-start.2 = (bf16[256,1024]{0,1:T(8,128)(2,1)}, bf16[256,1024]{0,1:T(8,128)(2,1)S(1)}, u32[]{:S(2)}, u32[]{:S(2)}) collective-permute-start(bf16[256,1024]{0,1:T(8,128)(2,1)} %fusion.110), channel_id=1, source_target_pairs={{0,15},{1,0},{2,1},{3,2},{4,3},{5,4},{6,5},{7,6},{8,7},{9,8},{10,9... | collective-permute-start | bytes 1572872 | tf_op jit(solution)/shard_map/while/body/eval_jaxpr/ppermute | solution.py:16
  1051.1 21.8 %collective-permute-start.3 = (bf16[256,1024]{0,1:T(8,128)(2,1)}, bf16[256,1024]{0,1:T(8,128)(2,1)S(1)}, u32[]{:S(2)}, u32[]{:S(2)}) collective-permute-start(bf16[256,1024]{0,1:T(8,128)(2,1)} %fusion.111), channel_id=1, source_target_pairs={{0,15},{1,0},{2,1},{3,2},{4,3},{5,4},{6,5},{7,6},{8,7},{9,8},{10,9... | collective-permute-start | bytes 1572872 | tf_op jit(solution)/shard_map/while/body/eval_jaxpr/ppermute | solution.py:16
  1051.1 28.0 %collective-permute-start = (bf16[256,1024]{0,1:T(8,128)(2,1)S(1)}, bf16[256,1024]{0,1:T(8,128)(2,1)S(1)}, u32[]{:S(2)}, u32[]{:S(2)}) collective-permute-start(bf16[256,1024]{0,1:T(8,128)(2,1)S(1)} %copy.88), channel_id=1, source_target_pairs={{0,15},{1,0},{2,1},{3,2},{4,3},{5,4},{6,5},{7,6},{8,7},{9,8},{10,9... | collective-permute-start | bytes 1572872 | tf_op jit(solution)/shard_map/while/body/eval_jaxpr/ppermute | solution.py:16
  1051.1 33.7 %collective-permute-start.1 = (bf16[256,1024]{0,1:T(8,128)(2,1)}, bf16[256,1024]{0,1:T(8,128)(2,1)S(1)}, u32[]{:S(2)}, u32[]{:S(2)}) collective-permute-start(bf16[256,1024]{0,1:T(8,128)(2,1)} %copy.89), channel_id=1, source_target_pairs={{0,15},{1,0},{2,1},{3,2},{4,3},{5,4},{6,5},{7,6},{8,7},{9,8},{10,9... | collective-permute-start | bytes 1572872 | tf_op jit(solution)/shard_map/while/body/eval_jaxpr/ppermute | solution.py:16
  1094.4 25.3 %collective-permute-start.2 = (bf16[256,1024]{0,1:T(8,128)(2,1)}, bf16[256,1024]{0,1:T(8,128)(2,1)S(1)}, u32[]{:S(2)}, u32[]{:S(2)}) collective-permute-start(bf16[256,1024]{0,1:T(8,128)(2,1)} %fusion.110), channel_id=1, source_target_pairs={{0,15},{1,0},{2,1},{3,2},{4,3},{5,4},{6,5},{7,6},{8,7},{9,8},{10,9... | collective-permute-start | bytes 1572872 | tf_op jit(solution)/shard_map/while/body/eval_jaxpr/ppermute | solution.py:16
  1109.2 27.1 %collective-permute-start = (bf16[256,1024]{0,1:T(8,128)(2,1)S(1)}, bf16[256,1024]{0,1:T(8,128)(2,1)S(1)}, u32[]{:S(2)}, u32[]{:S(2)}) collective-permute-start(bf16[256,1024]{0,1:T(8,128)(2,1)S(1)} %copy.88), channel_id=1, source_target_pairs={{0,15},{1,0},{2,1},{3,2},{4,3},{5,4},{6,5},{7,6},{8,7},{9,8},{10,9... | collective-permute-start | bytes 1572872 | tf_op jit(solution)/shard_map/while/body/eval_jaxpr/ppermute | solution.py:16
  1109.2 32.7 %collective-permute-start.1 = (bf16[256,1024]{0,1:T(8,128)(2,1)}, bf16[256,1024]{0,1:T(8,128)(2,1)S(1)}, u32[]{:S(2)}, u32[]{:S(2)}) collective-permute-start(bf16[256,1024]{0,1:T(8,128)(2,1)} %copy.89), channel_id=1, source_target_pairs={{0,15},{1,0},{2,1},{3,2},{4,3},{5,4},{6,5},{7,6},{8,7},{9,8},{10,9... | collective-permute-start | bytes 1572872 | tf_op jit(solution)/shard_map/while/body/eval_jaxpr/ppermute | solution.py:16
  1151.6 25.3 %collective-permute-start.2 = (bf16[256,1024]{0,1:T(8,128)(2,1)}, bf16[256,1024]{0,1:T(8,128)(2,1)S(1)}, u32[]{:S(2)}, u32[]{:S(2)}) collective-permute-start(bf16[256,1024]{0,1:T(8,128)(2,1)} %fusion.110), channel_id=1, source_target_pairs={{0,15},{1,0},{2,1},{3,2},{4,3},{5,4},{6,5},{7,6},{8,7},{9,8},{10,9... | collective-permute-start | bytes 1572872 | tf_op jit(solution)/shard_map/while/body/eval_jaxpr/ppermute | solution.py:16
  1166.3 26.1 %collective-permute-start = (bf16[256,1024]{0,1:T(8,128)(2,1)S(1)}, bf16[256,1024]{0,1:T(8,128)(2,1)S(1)}, u32[]{:S(2)}, u32[]{:S(2)}) collective-permute-start(bf16[256,1024]{0,1:T(8,128)(2,1)S(1)} %copy.88), channel_id=1, source_target_pairs={{0,15},{1,0},{2,1},{3,2},{4,3},{5,4},{6,5},{7,6},{8,7},{9,8},{10,9... | collective-permute-start | bytes 1572872 | tf_op jit(solution)/shard_map/while/body/eval_jaxpr/ppermute | solution.py:16
  1166.4 31.8 %collective-permute-start.1 = (bf16[256,1024]{0,1:T(8,128)(2,1)}, bf16[256,1024]{0,1:T(8,128)(2,1)S(1)}, u32[]{:S(2)}, u32[]{:S(2)}) collective-permute-start(bf16[256,1024]{0,1:T(8,128)(2,1)} %copy.89), channel_id=1, source_target_pairs={{0,15},{1,0},{2,1},{3,2},{4,3},{5,4},{6,5},{7,6},{8,7},{9,8},{10,9... | collective-permute-start | bytes 1572872 | tf_op jit(solution)/shard_map/while/body/eval_jaxpr/ppermute | solution.py:16
  1207.8 25.3 %collective-permute-start.2 = (bf16[256,1024]{0,1:T(8,128)(2,1)}, bf16[256,1024]{0,1:T(8,128)(2,1)S(1)}, u32[]{:S(2)}, u32[]{:S(2)}) collective-permute-start(bf16[256,1024]{0,1:T(8,128)(2,1)} %fusion.110), channel_id=1, source_target_pairs={{0,15},{1,0},{2,1},{3,2},{4,3},{5,4},{6,5},{7,6},{8,7},{9,8},{10,9... | collective-permute-start | bytes 1572872 | tf_op jit(solution)/shard_map/while/body/eval_jaxpr/ppermute | solution.py:16
  1222.6 25.2 %collective-permute-start = (bf16[256,1024]{0,1:T(8,128)(2,1)S(1)}, bf16[256,1024]{0,1:T(8,128)(2,1)S(1)}, u32[]{:S(2)}, u32[]{:S(2)}) collective-permute-start(bf16[256,1024]{0,1:T(8,128)(2,1)S(1)} %copy.88), channel_id=1, source_target_pairs={{0,15},{1,0},{2,1},{3,2},{4,3},{5,4},{6,5},{7,6},{8,7},{9,8},{10,9... | collective-permute-start | bytes 1572872 | tf_op jit(solution)/shard_map/while/body/eval_jaxpr/ppermute | solution.py:16
  1222.6 30.9 %collective-permute-start.1 = (bf16[256,1024]{0,1:T(8,128)(2,1)}, bf16[256,1024]{0,1:T(8,128)(2,1)S(1)}, u32[]{:S(2)}, u32[]{:S(2)}) collective-permute-start(bf16[256,1024]{0,1:T(8,128)(2,1)} %copy.89), channel_id=1, source_target_pairs={{0,15},{1,0},{2,1},{3,2},{4,3},{5,4},{6,5},{7,6},{8,7},{9,8},{10,9... | collective-permute-start | bytes 1572872 | tf_op jit(solution)/shard_map/while/body/eval_jaxpr/ppermute | solution.py:16
  1263.2 25.3 %collective-permute-start.2 = (bf16[256,1024]{0,1:T(8,128)(2,1)}, bf16[256,1024]{0,1:T(8,128)(2,1)S(1)}, u32[]{:S(2)}, u32[]{:S(2)}) collective-permute-start(bf16[256,1024]{0,1:T(8,128)(2,1)} %fusion.110), channel_id=1, source_target_pairs={{0,15},{1,0},{2,1},{3,2},{4,3},{5,4},{6,5},{7,6},{8,7},{9,8},{10,9... | collective-permute-start | bytes 1572872 | tf_op jit(solution)/shard_map/while/body/eval_jaxpr/ppermute | solution.py:16
  1278.0 24.3 %collective-permute-start = (bf16[256,1024]{0,1:T(8,128)(2,1)S(1)}, bf16[256,1024]{0,1:T(8,128)(2,1)S(1)}, u32[]{:S(2)}, u32[]{:S(2)}) collective-permute-start(bf16[256,1024]{0,1:T(8,128)(2,1)S(1)} %copy.88), channel_id=1, source_target_pairs={{0,15},{1,0},{2,1},{3,2},{4,3},{5,4},{6,5},{7,6},{8,7},{9,8},{10,9... | collective-permute-start | bytes 1572872 | tf_op jit(solution)/shard_map/while/body/eval_jaxpr/ppermute | solution.py:16
  1278.0 30.0 %collective-permute-start.1 = (bf16[256,1024]{0,1:T(8,128)(2,1)}, bf16[256,1024]{0,1:T(8,128)(2,1)S(1)}, u32[]{:S(2)}, u32[]{:S(2)}) collective-permute-start(bf16[256,1024]{0,1:T(8,128)(2,1)} %copy.89), channel_id=1, source_target_pairs={{0,15},{1,0},{2,1},{3,2},{4,3},{5,4},{6,5},{7,6},{8,7},{9,8},{10,9... | collective-permute-start | bytes 1572872 | tf_op jit(solution)/shard_map/while/body/eval_jaxpr/ppermute | solution.py:16
  1317.6 25.3 %collective-permute-start.2 = (bf16[256,1024]{0,1:T(8,128)(2,1)}, bf16[256,1024]{0,1:T(8,128)(2,1)S(1)}, u32[]{:S(2)}, u32[]{:S(2)}) collective-permute-start(bf16[256,1024]{0,1:T(8,128)(2,1)} %fusion.110), channel_id=1, source_target_pairs={{0,15},{1,0},{2,1},{3,2},{4,3},{5,4},{6,5},{7,6},{8,7},{9,8},{10,9... | collective-permute-start | bytes 1572872 | tf_op jit(solution)/shard_map/while/body/eval_jaxpr/ppermute | solution.py:16
  1332.4 23.4 %collective-permute-start = (bf16[256,1024]{0,1:T(8,128)(2,1)S(1)}, bf16[256,1024]{0,1:T(8,128)(2,1)S(1)}, u32[]{:S(2)}, u32[]{:S(2)}) collective-permute-start(bf16[256,1024]{0,1:T(8,128)(2,1)S(1)} %copy.88), channel_id=1, source_target_pairs={{0,15},{1,0},{2,1},{3,2},{4,3},{5,4},{6,5},{7,6},{8,7},{9,8},{10,9... | collective-permute-start | bytes 1572872 | tf_op jit(solution)/shard_map/while/body/eval_jaxpr/ppermute | solution.py:16
  1332.4 29.0 %collective-permute-start.1 = (bf16[256,1024]{0,1:T(8,128)(2,1)}, bf16[256,1024]{0,1:T(8,128)(2,1)S(1)}, u32[]{:S(2)}, u32[]{:S(2)}) collective-permute-start(bf16[256,1024]{0,1:T(8,128)(2,1)} %copy.89), channel_id=1, source_target_pairs={{0,15},{1,0},{2,1},{3,2},{4,3},{5,4},{6,5},{7,6},{8,7},{9,8},{10,9... | collective-permute-start | bytes 1572872 | tf_op jit(solution)/shard_map/while/body/eval_jaxpr/ppermute | solution.py:16
  1371.4 326.7 %reduce-scatter.9.cloned.1.call-start = ((), (), s32[]{:S(2)}) async-start(), calls=%async_computation.8 | async-start | bytes 8912896 | tf_op jit(solution)/shard_map/reduce_scatter | solution.py:250
  1380.0 500.5 %reduce-scatter.11.cloned.1.call-start = ((), (), s32[]{:S(2)}) async-start(), calls=%async_computation.9 | async-start | bytes 8912896 | tf_op jit(solution)/shard_map/reduce_scatter | solution.py:253
  1389.6 548.9 %all-reduce.7.cloned.1.call-start = ((), (), s32[]{:S(2)}) async-start(), calls=%async_computation.10 | async-start | bytes 3145728 | tf_op jit(solution)/shard_map/psum | solution.py:264
  (70 other events, 1591.5 us)
Sparse Core Ops, SparseCore 0:
  16.7 115.5 all-gather.2
  135.6 111.0 all-gather.4
  389.5 207.5 reduce-scatter.6
  1371.5 147.3 reduce-scatter.4
  1521.1 176.9 reduce-scatter.8
  1700.3 180.2 reduce-scatter.10
  1883.1 22.8 all-reduce.6
where the time goes:
time: 1960 us; the launch traced here: 1950 us
  waiting for transfers between devices  1250 us (64%)
  starting transfers between devices  197 us (10%)
  other arithmetic  159 us (8%)
  matrix products  131 us (7%)
  local copies, waits for them, and re-layouts  91 us (5%)
  loops' own time  60.7 us (3%)
  blocking collectives  44.9 us (2%)
    ppermute x64, waiting for transfers between devices, passed_along(): lax.ppermute(array, axis, [(i, (i + by) % count) for i in range(count)])  547 us
    ppermute x64, starting transfers between devices, passed_along(): lax.ppermute(array, axis, [(i, (i + by) % count) for i in range(count)])  196 us
    reduce_scatter x1, waiting for transfers between devices, on_device(): lax.psum_scatter(grad_down.astype(jnp.bfloat16), 'seq', scatter_dimension...  182 us
    reduce_scatter x1, waiting for transfers between devices, on_device(): lax.psum_scatter(grad_up.astype(jnp.bfloat16), 'seq', scatter_dimension=0...  179 us
    reduce_scatter x1, waiting for transfers between devices, on_device(): lax.psum_scatter(grad_qkv.astype(jnp.bfloat16), 'seq', scatter_dimension=...  121 us
    all_gather x1, waiting for transfers between devices, on_device(): lax.all_gather(value_rows, 'seq', axis=0, tiled=True)  114 us
    all_gather x1, waiting for transfers between devices, on_device(): lax.all_gather(key_rows, 'seq', axis=0, tiled=True)  105 us
    another operation x1, loops' own time, on_device(): final = lax.fori_loop(0, cycle_size, cycle_turn, begin)  59.5 us
  transfers between devices with their start and end apart: 71, of which 69 were waited for; matrix products, arithmetic and copies ran while one was open for 11% of the time, Pallas kernels for 0%

commit v1 on v0

v1 whole, which is shorter than its diff:
```python
import functools

import jax
import jax.numpy as jnp
from jax import lax
from jax.experimental import pallas as pl
from jax.experimental.pallas import tpu as pltpu
from jax.sharding import PartitionSpec as P

HEADS = 16
HEAD_DIM = 64
eps = 1e-05
masked = -1e30
log2e = 1.4426950408889634
vmem_bytes = 56 * 2**20
GAIN_ROWS = 16
low = jnp.bfloat16
full = jnp.float32


def lane_labels(ends_ref, utterances, start, rows, count):
    place = start + lax.broadcasted_iota(jnp.int32, (rows, count), 1)
    label = jnp.zeros((rows, count), jnp.int32)
    for u in range(utterances):
        label = label + (place >= ends_ref[u]).astype(jnp.int32)
    return label


def stage_scores(ends_ref, rows_ref, source, utterances, query_s, key_s):
    frames = rows_ref.shape[2]
    label = lane_labels(ends_ref, utterances, source * frames, HEAD_DIM, frames)
    row = lax.broadcasted_iota(jnp.int32, (HEAD_DIM, frames), 0)
    own = jnp.where(row == label, 1.0, 0.0).astype(low)
    barred = jnp.where((row != label) & (row <= utterances), masked, 0.0).astype(low)
    span = pl.ds(source * frames, frames)
    query_s[0:HEAD_DIM, span] = rows_ref[source, 0:HEAD_DIM, :]
    query_s[HEAD_DIM:, span] = own
    key_s[span, :] = jnp.concatenate([rows_ref[source, HEAD_DIM : 2 * HEAD_DIM, :], barred], axis=0).T


def causal(scores, key_start, query_start):
    key_place = key_start + lax.broadcasted_iota(jnp.int32, scores.shape, 0)
    query_place = query_start + lax.broadcasted_iota(jnp.int32, scores.shape, 1)
    return jnp.where(key_place <= query_place, scores, masked)


def forward_kernel(ends_ref, rows_ref, out_ref, mass_ref, query_s, key_s, value_s, *, block, copies):
    sources, _, frames = rows_ref.shape
    utterances = ends_ref.shape[0] - 1
    share = ends_ref[utterances]
    power = HEAD_DIM**-0.5 * log2e
    total = sources * frames
    for source in range(sources):
        stage_scores(ends_ref, rows_ref, source, utterances, query_s, key_s)
        span = pl.ds(source * frames, frames)
        value_s[0:HEAD_DIM, span] = rows_ref[source, 2 * HEAD_DIM :, :]
        row = lax.broadcasted_iota(jnp.int32, (value_s.shape[0] - HEAD_DIM, frames), 0)
        value_s[HEAD_DIM:, span] = jnp.where(row == 0, 1.0, 0.0).astype(low)
    if copies > 1:
        out_ref[...] = jnp.zeros_like(out_ref)
        mass_ref[...] = jnp.zeros_like(mass_ref)

    def query_block(turn, _):
        i = turn * copies + share if copies > 1 else turn
        span = pl.ds(pl.multiple_of(i * block, block), block)
        query = query_s[:, span]

        def step(j, current, diagonal):
            peak, sums = current
            keys = pl.ds(pl.multiple_of(j * block, block), block)
            scores = jnp.dot(key_s[keys, :], query, preferred_element_type=full)
            if diagonal:
                scores = causal(scores, 0, 0)
            new_peak = jnp.maximum(peak, jnp.max(scores, axis=0, keepdims=True) * power)
            weights = jnp.exp2(scores * power - new_peak)
            sums = sums * jnp.exp2(peak - new_peak) + jnp.dot(
                value_s[:, keys], weights.astype(low), preferred_element_type=full
            )
            return new_peak, sums

        start = (jnp.full((1, block), masked, full), jnp.zeros((value_s.shape[0], block), full))
        current = lax.fori_loop(0, i, lambda j, now: step(j, now, False), start)
        peak, sums = step(i, current, True)
        mass = sums[HEAD_DIM : HEAD_DIM + 1]
        label = lane_labels(ends_ref, utterances, i * block, 1, block)
        out = (sums[0:HEAD_DIM] * jnp.where(label < utterances, 1.0 / mass, 0.0)).astype(low)
        mass_ref[:, span] = peak + jnp.log2(mass)
        for part in range(block // frames):
            out_ref[i * (block // frames) + part] = out[:, part * frames : (part + 1) * frames]
        return 0

    lax.fori_loop(0, total // block // copies, query_block, 0)


def block_of(total, copies):
    return min(1024, total // copies)


def attn_fwd(ends, rows, copies):
    sources, _, frames = rows.shape
    total = sources * frames
    return pl.pallas_call(
        functools.partial(forward_kernel, block=block_of(total, copies), copies=copies),
        out_shape=(
            jax.ShapeDtypeStruct((sources, HEAD_DIM, frames), low),
            jax.ShapeDtypeStruct((1, total), full),
        ),
        in_specs=[pl.BlockSpec(memory_space=pltpu.SMEM), pl.BlockSpec(memory_space=pltpu.VMEM)],
        out_specs=[pl.BlockSpec(memory_space=pltpu.VMEM)] * 2,
        scratch_shapes=[
            pltpu.VMEM((2 * HEAD_DIM, total), low),
            pltpu.VMEM((total, 2 * HEAD_DIM), low),
            pltpu.VMEM((HEAD_DIM + 16, total), low),
        ],
        compiler_params=pltpu.CompilerParams(vmem_limit_bytes=vmem_bytes),
        cost_estimate=pl.CostEstimate(
            flops=4 * total * total * HEAD_DIM, bytes_accessed=4 * rows.size, transcendentals=total * total // 2
        ),
        name="attention_forward",
    )(ends, rows)


def backward_kernel(
    ends_ref, rows_ref, grad_ref, out_ref, mass_ref, result_ref,
    query_s, key_s, keyt_s, value_s, grad_s, grad_query_s, *, block, copies
):
    sources, _, frames = rows_ref.shape
    utterances = ends_ref.shape[0] - 1
    share = ends_ref[utterances]
    scale = HEAD_DIM**-0.5
    power = scale * log2e
    total = sources * frames
    blocks = total // block
    row = lax.broadcasted_iota(jnp.int32, (HEAD_DIM, frames), 0)
    for source in range(sources):
        span = pl.ds(source * frames, frames)
        stage_scores(ends_ref, rows_ref, source, utterances, query_s, key_s)
        keyt_s[:, span] = rows_ref[source, HEAD_DIM : 2 * HEAD_DIM, :]
        grad = grad_ref[source]
        delta = jnp.sum(grad.astype(full) * out_ref[source].astype(full), axis=0, keepdims=True)
        first = delta.astype(low).astype(full)
        second = (delta - first).astype(low).astype(full)
        third = delta - first - second
        more = jnp.where(row == 0, -first, jnp.where(row == 1, -second, jnp.where(row == 2, -third, 0.0)))
        grad_s[0:HEAD_DIM, span] = grad
        grad_s[HEAD_DIM:, span] = more.astype(low)
        ones = jnp.where(row < 3, 1.0, 0.0).astype(low)
        value_s[span, :] = jnp.concatenate([rows_ref[source, 2 * HEAD_DIM :, :], ones], axis=0).T
    grad_query_s[...] = jnp.zeros_like(grad_query_s)
    across = (((1,), (1,)), ((), ()))

    def key_block(j, _):
        keys = pl.ds(pl.multiple_of(j * block, block), block)

        def step(i, current, diagonal):
            grad_key, grad_value = current
            span = pl.ds(pl.multiple_of(i * block, block), block)
            scores = jnp.dot(key_s[keys, :], query_s[:, span], preferred_element_type=full)
            if diagonal:
                scores = causal(scores, j * block, i * block)
            probs = jnp.exp2(scores * power - mass_ref[:, span])
            shifted = jnp.dot(value_s[keys, :], grad_s[:, span], preferred_element_type=full)
            grad_scores = (probs * shifted).astype(low)
            grad_query_s[:, span] += jnp.dot(keyt_s[:, keys], grad_scores, preferred_element_type=full)
            grad_value = grad_value + lax.dot_general(
                grad_s[0:HEAD_DIM, span], probs.astype(low), across, preferred_element_type=full
            )
            grad_key = grad_key + lax.dot_general(
                query_s[0:HEAD_DIM, span], grad_scores, across, preferred_element_type=full
            )
            return grad_key, grad_value

        zero = jnp.zeros((HEAD_DIM, block), full)
        if copies > 1:
            first = (j - share + copies - 1) // copies
            current = lax.fori_loop(
                first, blocks // copies, lambda turn, now: step(turn * copies + share, now, True), (zero, zero)
            )
        else:
            current = step(j, (zero, zero), True)
            current = lax.fori_loop(j + 1, blocks, lambda i, now: step(i, now, False), current)
        grad_key = (current[0] * scale).astype(low)
        grad_value = current[1].astype(low)
        for part in range(block // frames):
            lanes = slice(part * frames, (part + 1) * frames)
            place = j * (block // frames) + part
            result_ref[place, HEAD_DIM : 2 * HEAD_DIM, :] = grad_key[:, lanes]
            result_ref[place, 2 * HEAD_DIM :, :] = grad_value[:, lanes]
        return 0

    lax.fori_loop(0, blocks, key_block, 0)
    for source in range(sources):
        lanes = slice(source * frames, (source + 1) * frames)
        result_ref[source, 0:HEAD_DIM, :] = (grad_query_s[:, lanes] * scale).astype(low)


def attn_bwd(ends, rows, grads, outs, mass, copies):
    sources, _, frames = rows.shape
    total = sources * frames
    return pl.pallas_call(
        functools.partial(backward_kernel, block=block_of(total, copies), copies=copies),
        out_shape=jax.ShapeDtypeStruct(rows.shape, low),
        in_specs=[pl.BlockSpec(memory_space=pltpu.SMEM)] + [pl.BlockSpec(memory_space=pltpu.VMEM)] * 4,
        out_specs=pl.BlockSpec(memory_space=pltpu.VMEM),
        scratch_shapes=[
            pltpu.VMEM((2 * HEAD_DIM, total), low),
            pltpu.VMEM((total, 2 * HEAD_DIM), low),
            pltpu.VMEM((HEAD_DIM, total), low),
            pltpu.VMEM((total, 2 * HEAD_DIM), low),
            pltpu.VMEM((2 * HEAD_DIM, total), low),
            pltpu.VMEM((HEAD_DIM, total), full),
        ],
        compiler_params=pltpu.CompilerParams(vmem_limit_bytes=vmem_bytes),
        cost_estimate=pl.CostEstimate(
            flops=10 * total * total * HEAD_DIM, bytes_accessed=8 * rows.size, transcendentals=total * total // 2
        ),
        name="attention_backward",
    )(ends, rows, grads, outs, mass)


def norm_parts(inputs):
    centred = inputs - jnp.mean(inputs, axis=-1, keepdims=True)
    spread = jnp.mean(centred * centred, axis=-1, keepdims=True)
    inverse = lax.rsqrt(spread + eps)
    return centred * inverse, inverse


def norm_back(grad, unit, inverse, gain):
    scaled = grad * gain
    along = jnp.mean(scaled, axis=-1, keepdims=True)
    across = jnp.mean(scaled * unit, axis=-1, keepdims=True)
    return inverse * (scaled - along - unit * across)


def other_core(array):
    count = lax.axis_size("items")
    return lax.ppermute(array, "items", [(i, i ^ 1) for i in range(count)])


def to_heads(array):
    size = lax.axis_size("seq")
    copies = size // HEADS
    if copies > 1:
        array = jnp.repeat(array, copies, axis=0)
    return lax.all_to_all(array, "seq", 0, 0, tiled=True)


def to_frames(array):
    size = lax.axis_size("seq")
    copies = size // HEADS
    moved = lax.all_to_all(array, "seq", 0, 0, tiled=True)
    if copies > 1:
        moved = jnp.sum(moved.reshape((HEADS, copies) + moved.shape[1:]).astype(full), axis=1).astype(low)
    return moved


def half_columns(array, which):
    width = array.shape[-1] // 2
    return lax.dynamic_slice_in_dim(array, which * width, width, axis=-1)


def pick(array, index, axis):
    return lax.dynamic_index_in_dim(array, index, axis, keepdims=False)


def flipped(array, bit):
    size = lax.axis_size("seq")
    return lax.ppermute(array, "seq", [(i, i ^ bit) for i in range(size)])


def line_sum(parts):
    size = lax.axis_size("seq")
    lines = size // 4
    mine = lax.axis_index("seq") // 4
    up = down = None
    for step in range(1, lines):
        up_send = pick(parts, jnp.minimum(mine + lines - step, lines - 1), 0)
        down_send = pick(parts, jnp.maximum(mine - (lines - step), 0), 0)
        if up is not None:
            up_send = (up_send.astype(full) + up.astype(full)).astype(low)
            down_send = (down_send.astype(full) + down.astype(full)).astype(low)
        up = lax.ppermute(up_send, "seq", [(i, i + 4) for i in range(4 * step)])
        down = lax.ppermute(down_send, "seq", [(i, i - 4) for i in range(size - 4 * step, size)])
    total = pick(parts, mine, 0).astype(full)
    return total + up.astype(full) + down.astype(full)


def scatter_sum(make, first):
    me = lax.axis_index("seq")
    bits = (me % 2, (me // 2) % 2)
    second = 1 - first
    away = make(first, 1 - bits[first])
    arrived = flipped(away, 1 << first)
    kept = make(first, bits[first])
    mine, theirs = bits[second], 1 - bits[second]
    send = (pick(kept, theirs, 1).astype(full) + pick(arrived, theirs, 1).astype(full)).astype(low)
    came = flipped(send, 1 << second)
    total = (
        pick(kept, mine, 1).astype(full) + pick(arrived, mine, 1).astype(full) + came.astype(full)
    ).astype(low)
    return line_sum(total)


def term_maker(left, right, extra=None):
    lines = lax.axis_size("seq") // 4
    count, wide = left.shape
    rows = wide // (4 * lines)
    grid = left.reshape(count, lines, 2, 2, rows)

    def make(bit, value):
        chosen = pick(grid, value, 3 - bit)
        terms = jnp.einsum("tzbr,tn->zbrn", chosen, right, preferred_element_type=full).astype(low)
        if extra is not None:
            terms = jnp.concatenate([terms, pick(extra, value, 2 - bit)], axis=2)
        return terms

    return make


def gain_block(gain, columns):
    lines = lax.axis_size("seq") // 4
    rows = gain.shape[0] // (4 * lines)
    block = gain.astype(low).reshape(lines, 2, 2, 1, rows)
    return jnp.pad(block, ((0, 0), (0, 0), (0, 0), (0, GAIN_ROWS - 1), (0, columns - rows)))


def over_items(piece):
    count = lax.axis_size("items")
    pieces = lax.all_gather(piece.astype(low), "items", axis=0)
    pieces = pieces.reshape((count // 2, 2) + piece.shape)
    if count > 2:
        return jnp.sum(pieces.astype(full), axis=0)
    return pieces[0].astype(full)


def side_by_side(halves):
    return jnp.concatenate([halves[0], halves[1]], axis=-1)


def on_device(frames, lengths, w_qkv, w_out, w_up, w_down, gain_one, gain_two, cotangent):
    row_count, feature_count = frames.shape[1:]
    me = lax.axis_index("seq")
    core = lax.axis_index("items") % 2
    ends = jnp.cumsum(lengths[0]).astype(jnp.int32)
    places = me * row_count + jnp.arange(row_count, dtype=jnp.int32)
    present = (places < ends[-1]).astype(full)[:, None]

    inputs = frames[0].astype(full)
    unit_one, inverse_one = norm_parts(inputs)
    low_one = (unit_one * gain_one).astype(low)
    packed = jnp.dot(low_one, w_qkv, preferred_element_type=full).astype(low)
    by_head = packed.T.reshape(3, HEADS, HEAD_DIM, row_count).transpose(1, 0, 2, 3).reshape(HEADS, 3 * HEAD_DIM, row_count)
    head_rows = to_heads(by_head)
    copies = lax.axis_size("seq") // HEADS
    control = jnp.concatenate([ends, (me % copies)[None]])
    head_out, log_mass = attn_fwd(control, head_rows, copies)
    attended = to_frames(head_out).reshape(feature_count, row_count).T

    middle = inputs + jnp.dot(attended, w_out, preferred_element_type=full)
    unit_two, inverse_two = norm_parts(middle)
    low_two = (unit_two * gain_two).astype(low)
    hidden = jnp.dot(low_two, w_up, preferred_element_type=full)
    activated, pull_gelu = jax.vjp(jax.nn.gelu, hidden)
    act_low = activated.astype(low)
    mixed = jnp.dot(act_low, w_down, preferred_element_type=full)
    result = (present * (middle + mixed)).astype(low)
    grad_mixed = cotangent[0].astype(full) * present
    grad_mixed_low = grad_mixed.astype(low)
    grad_act = jnp.einsum("td,fd->tf", grad_mixed_low, w_down, preferred_element_type=full)
    grad_hidden = pull_gelu(grad_act)[0].astype(low)
    grad_normed_two = jnp.einsum("tf,df->td", grad_hidden, w_up, preferred_element_type=full)
    grad_gain_two = jnp.sum(grad_normed_two * unit_two, axis=0)
    grad_middle = grad_mixed + norm_back(grad_normed_two, unit_two, inverse_two, gain_two)
    grad_branch = grad_middle.astype(low)
    grad_attended = jnp.einsum("te,de->dt", grad_branch, w_out, preferred_element_type=full).astype(low)
    grad_attended = grad_attended * present[:, 0].astype(low)[None]
    grad_heads = to_heads(grad_attended.reshape(HEADS, HEAD_DIM, row_count))

    def both(left, right):
        lefts = jnp.concatenate([left, other_core(left)], axis=0)
        rights = jnp.concatenate(
            [half_columns(right, core), other_core(half_columns(right, 1 - core))], axis=0
        )
        return lefts, rights

    sum_down = scatter_sum(term_maker(*both(act_low, grad_mixed_low)), 1)
    sum_up = scatter_sum(term_maker(*both(low_two, grad_hidden)), 0)
    extra = gain_block(grad_gain_two, feature_count // 2)
    sum_out = scatter_sum(term_maker(*both(attended, grad_branch), extra), 0)

    grad_rows = attn_bwd(control, head_rows, grad_heads, head_out, log_mass, copies)
    grad_packed = to_frames(grad_rows)
    grad_packed = (
        grad_packed.reshape(HEADS, 3, HEAD_DIM, row_count).transpose(3, 1, 0, 2).reshape(row_count, 3 * feature_count)
    )
    lefts, rights = both(low_one, grad_packed)
    split = rights.shape[1] // 2
    grad_normed_one = jnp.einsum("te,de->td", grad_packed, w_qkv, preferred_element_type=full)
    grad_gain_one = jnp.sum(grad_normed_one * unit_one, axis=0)
    sum_qkv_a = scatter_sum(term_maker(lefts, rights[:, :split]), 0)
    extra = gain_block(grad_gain_one, rights.shape[1] - split)
    sum_qkv_b = scatter_sum(term_maker(lefts, rights[:, split:], extra), 1)
    grad_inputs = grad_middle + norm_back(grad_normed_one, unit_one, inverse_one, gain_one)

    rows_out = sum_up.shape[0]
    out_halves = over_items(sum_out)
    up = side_by_side(over_items(sum_up))
    down = side_by_side(over_items(sum_down))
    out = side_by_side(out_halves[:, :rows_out])
    b_halves = over_items(sum_qkv_b)
    a_halves = over_items(sum_qkv_a)
    qkv = side_by_side(jnp.concatenate([a_halves, b_halves[:, :rows_out]], axis=-1))
    sum_gain_two = jnp.sum(out_halves[:, rows_out, :rows_out], axis=0)
    sum_gain_one = jnp.sum(b_halves[:, rows_out, :rows_out], axis=0)
    return (result[None], grad_inputs[None], qkv, out, up, down, sum_gain_one, sum_gain_two)


def solution(mesh):
    return jax.shard_map(
        on_device,
        mesh=mesh,
        in_specs=(
            P("items", "seq", None),
            P("items", None),
            P(),
            P(),
            P(),
            P(),
            P(),
            P(),
            P("items", "seq", None),
        ),
        out_specs=(
            P("items", "seq", None),
            P("items", "seq", None),
            P("seq", None),
            P("seq", None),
            P("seq", None),
            P("seq", None),
            P("seq"),
            P("seq"),
        ),
        check_vma=False,
    )
```

time: 1960 us -> 475 us (0.24)
  waiting for transfers between devices: 1250 us -> 152 us
  other arithmetic: 159 us -> 38.6 us
  starting transfers between devices: 197 us -> 106 us
  matrix products: 131 us -> 66.4 us
  loops' own time: 60.7 us -> 0 us
  Pallas kernels: 0 us -> 51.9 us
  local copies, waits for them, and re-layouts: 91 us -> 39.3 us
  blocking collectives: 44.9 us -> 10.2 us
    reduce_scatter x4 -> x0, waiting for transfers between devices: 483 us -> none  [the longest x1 182 us: on_device(): lax.psum_scatter(grad_down.astype(jnp.bfloat16), 'seq', scatter_dimension...]
    ppermute x64 -> x48, waiting for transfers between devices: 547 us -> 117 us  [the longest x10 80.9 us: flipped(): return lax.ppermute(array, 'seq', [(i, i ^ bit) for i in range(size)])]
    all_gather x2 -> x0, waiting for transfers between devices: 220 us -> none  [the longest x1 114 us: on_device(): lax.all_gather(value_rows, 'seq', axis=0, tiled=True)]
    ppermute x64 -> x48, starting transfers between devices: 196 us -> 80.3 us  [the longest x15 53.2 us: line_sum(): up = lax.ppermute(up_send, 'seq', [(i, i + 4) for i in range(4 * step)])]
    convert_element_type x73 -> x38, other arithmetic: 117 us -> 19.4 us  [the longest x5 6.11 us: scatter_sum(): (pick(kept, theirs, 1).astype(full) + pick(arrived, theirs, 1).astype(ful...]
    dot_general x19 -> x18, matrix products: 131 us -> 66.4 us  [the longest x10 24.5 us: make(): jnp.einsum('tzbr,tn->zbrn', chosen, right, preferred_element_type=full)]
    another operation x18 -> x0, loops' own time: 60.7 us -> none  [the longest x1 59.5 us: on_device(): final = lax.fori_loop(0, cycle_size, cycle_turn, begin)]
    pallas_call x0 -> x2, Pallas kernels: none -> 51.9 us  [the longest x1 33.8 us: attn_bwd(): pl.pallas_call(functools.partial(backward_kernel, block=block_of(total, c...]
  transfers between devices with their start and end apart: 71 -> 52, of which waited for: 69 -> 16; matrix products, arithmetic and copies ran while one was open for 11% -> 27% of each run, Pallas kernels for 0% -> 11%
where the time goes in v1:
time: 475 us; the launch traced here: 467 us
  waiting for transfers between devices  152 us (32%)
  starting transfers between devices  106 us (22%)
  matrix products  66.4 us (14%)
  Pallas kernels  51.9 us (11%)
  local copies, waits for them, and re-layouts  39.3 us (8%)
  other arithmetic  38.6 us (8%)
  blocking collectives  10.2 us (2%)
    ppermute x10, waiting for transfers between devices, flipped(): return lax.ppermute(array, 'seq', [(i, i ^ bit) for i in range(size)])  80.9 us
    ppermute x15, starting transfers between devices, line_sum(): up = lax.ppermute(up_send, 'seq', [(i, i + 4) for i in range(4 * step)])  53.2 us
    pallas_call x1, Pallas kernels, attn_bwd(): pl.pallas_call(functools.partial(backward_kernel, block=block_of(total, c...  33.8 us
    all_to_all x2, waiting for transfers between devices, to_heads(): return lax.all_to_all(array, 'seq', 0, 0, tiled=True)  32.7 us
    dot_general x10, matrix products, make(): jnp.einsum('tzbr,tn->zbrn', chosen, right, preferred_element_type=full)  24.5 us
    ppermute x15, waiting for transfers between devices, line_sum(): lax.ppermute(down_send, 'seq', [(i, i - 4) for i in range(size - 4 * step...  22.2 us
    pallas_call x1, Pallas kernels, attn_fwd(): pl.pallas_call(functools.partial(forward_kernel, block=block_of(total, co...  18.1 us
    ppermute x15, waiting for transfers between devices, line_sum(): up = lax.ppermute(up_send, 'seq', [(i, i + 4) for i in range(4 * step)])  14 us
  transfers between devices with their start and end apart: 52, of which 16 were waited for; matrix products, arithmetic and copies ran while one was open for 27% of the time, Pallas kernels for 11%

profile of v1, /device:TPU:0, one launch (start us, length us, event | category | flops | bytes accessed | tf_op | source)
XLA Modules:
  0.0 466.9 jit_solution(10670098973049655472)
XLA Ops:
  3.3 2.1 fusion.36
  5.5 5.9 %fusion.7 = bf16[3072,256]{0,1:T(8,128)(2,1)} fusion(bf16[256,1024]{1,0:T(8,128)(2,1)} %fusion.36, bf16[1024,3072]{1,0:T(8,128)(2,1)} %param.11), kind=kOutput, calls=%fused_computation.12 | convolution fusion | flops 1611399168 | bytes 8388608 | tf_op jit(solution)/shard_map/dot_general | solution.py:351
  11.4 2.6 copy.47
  14.0 2.8 copy.48
  16.8 8.5 %all-to-all-start = ((bf16[16,192,256]{2,1,0:T(8,128)(2,1)}), bf16[16,192,256]{2,1,0:T(8,128)(2,1)}, u32[]{:S(2)}, u32[]{:S(2)}) async-start(bf16[16,192,256]{2,1,0:T(8,128)(2,1)} %bitcast.335), calls=%async_computation | async-start | bytes 3145728 | tf_op jit(solution)/shard_map/all_to_all | solution.py:245
  27.4 32.1 %all-to-all-done.rows_ref = bf16[16,192,256]{2,1,0:T(8,128)(2,1)} async-done(((bf16[16,192,256]{2,1,0:T(8,128)(2,1)}), bf16[16,192,256]{2,1,0:T(8,128)(2,1)}, u32[]{:S(2)}, u32[]{:S(2)}) %all-to-all-start) | async-done | bytes 1572896 | tf_op jit(solution)/shard_map/all_to_all | solution.py:245
  59.5 18.1 %attention_forward.1 = (bf16[16,64,256]{2,1,0:T(8,128)(2,1)}, f32[1,4096]{1,0:T(1,128)}) custom-call(s32[4]{0:T(128)} %pad_add_fusion.ends_ref, bf16[16,192,256]{2,1,0:T(8,128)(2,1)} %all-to-all-done.rows_ref), custom_call_target="tpu_custom_call" | custom-call | flops 4294967296 | bytes 3145728 | tf_op jit(solution)/shard_map/attention_forward/pallas_call | solution.py:102
  77.6 7.7 %all-to-all-start.1 = ((bf16[16,64,256]{2,1,0:T(8,128)(2,1)}), bf16[16,64,256]{2,1,0:T(8,128)(2,1)}, u32[]{:S(2)}, u32[]{:S(2)}) async-start(bf16[16,64,256]{2,1,0:T(8,128)(2,1)} %get-tuple-element.10.out_ref), calls=%async_computation.1 | async-start | bytes 1048576 | tf_op jit(solution)/shard_map/all_to_all | solution.py:251
  86.3 7.7 %fusion.137 = f32[256,4096]{1,0:T(8,128)} fusion(bf16[256,1024]{1,0:T(8,128)(2,1)S(1)} %fusion.47, bf16[4096,1024]{1,0:T(8,128)(2,1)} %param.14), kind=kOutput, calls=%fused_computation.263 | convolution fusion | flops 2147483648 | bytes 13107200 | tf_op jit(solution)/shard_map/td,fd->tf/dot_general | solution.py:369
  95.3 1.8 copy.51
  97.1 2.6 all-to-all-done.1
  99.7 2.2 fusion.136
  103.2 10.4 %fusion.6 = (bf16[256,4096]{1,0:T(8,128)(2,1)S(1)}, bf16[256,4096]{1,0:T(8,128)(2,1)}) fusion(f32[256,4096]{1,0:T(8,128)S(1)} %copy-done.23, bf16[256,1024]{1,0:T(8,128)(2,1)} %multiply_convert_fusion.1, bf16[1024,4096]{1,0:T(8,128)(2,1)} %param.13), kind=kOutput, calls=%fused_computation.8 | convolution fusion | flops 2170552320 | bytes 17301504 | tf_op jit(solution)/shard_map/dot_general | solution.py:362
  113.6 2.7 multiply_reduce_fusion
  124.8 6.6 %fusion.35 = bf16[1,256,1024]{2,1,0:T(8,128)(2,1)} fusion(f32[256,1024]{1,0:T(8,128)S(1)} %get-tuple-element.65, bf16[256,4096]{1,0:T(8,128)(2,1)S(1)} %copy-done.14, bf16[4096,1024]{1,0:T(8,128)(2,1)} %param.14, f32[256]{0:T(256)S(1)} %get-tuple-element.68), kind=kOutput, calls=%fused_computation.59 | convolution fusion | flops 2148270080 | bytes 12059648 | tf_op jit(solution)/shard_map/dot_general | solution.py:365
  132.9 8.0 %collective-permute-done.20 = bf16[4,2,80,512]{3,2,0,1:T(8,128)(2,1)S(1)} collective-permute-done((bf16[4,2,80,512]{3,2,0,1:T(8,128)(2,1)S(1)}, bf16[4,2,80,512]{3,2,0,1:T(8,128)(2,1)S(1)}, u32[]{:S(2)}, u32[]{:S(2)}) %collective-permute-start.20) | collective-permute-done | bytes 655392 | tf_op jit(solution)/shard_map/ppermute | solution.py:268
  144.5 4.7 %all-to-all-start.2 = ((bf16[16,64,256]{2,1,0:T(8,128)(2,1)}), bf16[16,64,256]{2,1,0:T(8,128)(2,1)}, u32[]{:S(2)}, u32[]{:S(2)}) async-start(bf16[16,64,256]{2,1,0:T(8,128)(2,1)} %bitcast.12), calls=%async_computation.2 | async-start | bytes 1048576 | tf_op jit(solution)/shard_map/all_to_all | solution.py:245
  152.6 3.2 collective-permute-start.22
  159.0 4.4 collective-permute-start.23
  164.0 33.8 %attention_backward.1 = bf16[16,192,256]{2,1,0:T(8,128)(2,1)} custom-call(s32[4]{0:T(128)} %pad_add_fusion.ends_ref, bf16[16,192,256]{2,1,0:T(8,128)(2,1)} %all-to-all-done.rows_ref, bf16[16,64,256]{2,1,0:T(8,128)(2,1)} %all-to-all-done.2.grad_ref, bf16[16,64,256]{2,1,0:T(8,128)(2,1)} %get-tuple-element.10.out_ref, f32[1,4096]{1,0:T(1,128)} %get-tuple-element.11.mass_ref), custom_call_target="tpu_custom_call" | custom-call | flops 10737418240 | bytes 6291456 | tf_op jit(solution)/shard_map/attention_backward/pallas_call | solution.py:200
  197.8 4.5 all-to-all-start.3
  203.1 3.8 convolution_convert_fusion.1
  206.9 1.7 collective-permute-start.30
  208.7 4.0 collective-permute-start.24
  214.0 3.9 convolution_convert_fusion.2
  218.0 10.5 %collective-permute-done.24 = bf16[80,512]{1,0:T(8,128)(2,1)S(1)} collective-permute-done((bf16[80,512]{1,0:T(8,128)(2,1)S(1)}, bf16[80,512]{1,0:T(8,128)(2,1)S(1)}, u32[]{:S(2)}, u32[]{:S(2)}) %collective-permute-start.24) | collective-permute-done | bytes 81952 | tf_op jit(solution)/shard_map/ppermute | solution.py:282
  228.5 16.4 %collective-permute-done.27 = bf16[80,512]{1,0:T(8,128)(2,1)S(1)} collective-permute-done((bf16[80,512]{1,0:T(8,128)(2,1)S(1)}, bf16[80,512]{1,0:T(8,128)(2,1)S(1)}, u32[]{:S(2)}, u32[]{:S(2)}) %collective-permute-start.27) | collective-permute-done | bytes 81952 | tf_op jit(solution)/shard_map/ppermute | solution.py:283
  244.9 1.9 all-gather.2
  248.1 4.1 pad_maximum_fusion
  252.2 8.0 %reshape.234 = bf16[512,4,2,2,256]{4,3,2,1,0:T(2,128)(2,1)} reshape(bf16[512,4096]{1,0:T(8,128)(2,1)} %pad_maximum_fusion) | data formatting | bytes 8388608 | tf_op jit(solution)/shard_map/reshape | solution.py:308
  260.2 5.1 %constant_dynamic-slice_fusion.2 = (bf16[512,4,1,2,256]{4,3,2,1,0:T(2,128)(2,1)S(1)}, bf16[512,4,2,256]{3,2,1,0:T(2,128)(2,1)S(1)}) fusion(bf16[512,4,2,2,256]{4,3,2,1,0:T(2,128)(2,1)} %reshape.234, s32[]{:T(128)S(6)} %select_n.175, s32[]{:T(128)S(6)} %select_n.177), kind=kLoop, calls=%fused_computation.227 | loop fusion | bytes 8388616 | tf_op jit(solution)/shard_map/jit(dynamic_index_in_dim)/dynamic_slice | solution.py:263
  265.3 3.7 fusion.21
  269.0 2.5 collective-permute-start.40
  271.6 4.6 copy.73
  276.2 3.1 fusion.44
  279.2 3.5 fusion.18
  282.8 1.6 copy.50
  284.4 5.7 %fusion.42 = (bf16[1024]{0:T(1024)(128)(2,1)S(1)}, f32[256]{0:T(256)S(1)}, f32[256]{0:T(256)S(1)}, f32[256,1024]{1,0:T(8,128)}) fusion(bf16[1,256,1024]{2,1,0:T(8,128)(2,1)S(1)} %copy-done.2, f32[256]{0:T(256)S(1)} %add_rsqrt_fusion.1, f32[256]{0:T(256)S(1)} %broadcast_multiply_fusion.5, f32[1024]{0:T(1024)S(1)} %copy-done.21, ...), kind=kOutput, calls=%fused_computation.66 | convolution fusion | flops 1612970496 | bytes 9447424 | tf_op jit(solution)/shard_map/te,de->td/dot_general | solution.py:398
  291.5 48.7 %collective-permute-done.31 = bf16[4,64,2048]{2,1,0:T(8,128)(2,1)S(1)} collective-permute-done((bf16[4,64,2048]{2,1,0:T(8,128)(2,1)}, bf16[4,64,2048]{2,1,0:T(8,128)(2,1)S(1)}, u32[]{:S(2)}, u32[]{:S(2)}) %collective-permute-start.31) | collective-permute-done | bytes 1048608 | tf_op jit(solution)/shard_map/ppermute | solution.py:268
  340.2 1.7 fusion.16
  342.0 4.2 collective-permute-start.32
  346.3 2.3 copy.96
  349.9 1.7 collective-permute-done.32
  352.3 5.1 %collective-permute-start.33 = (bf16[64,2048]{1,0:T(8,128)(2,1)}, bf16[64,2048]{1,0:T(8,128)(2,1)}, u32[]{:S(2)}, u32[]{:S(2)}) collective-permute-start(bf16[64,2048]{1,0:T(8,128)(2,1)} %fusion.69), channel_id=1, source_target_pairs={{0,4},{1,5},{2,6},{3,7},{4,8},{5,9},{6,10},{7,11},{16,20},{17,21},... | collective-permute-start | bytes 786440 | tf_op jit(solution)/shard_map/ppermute | solution.py:282
  357.4 2.6 fusion.41
  361.8 1.9 fusion.45
  367.0 2.1 collective-permute-start.34
  376.2 1.7 convolution_convert_fusion.4
  379.3 10.6 %collective-permute-done.41 = bf16[4,256,512]{2,1,0:T(8,128)(2,1)S(1)} collective-permute-done((bf16[4,256,512]{2,1,0:T(8,128)(2,1)S(1)}, bf16[4,256,512]{2,1,0:T(8,128)(2,1)S(1)}, u32[]{:S(2)}, u32[]{:S(2)}) %collective-permute-start.41) | collective-permute-done | bytes 1048608 | tf_op jit(solution)/shard_map/ppermute | solution.py:268
  389.9 1.6 fusion.11
  393.7 2.2 all-gather.3
  396.0 8.2 %collective-permute-done.2 = bf16[4,2,64,768]{3,2,0,1:T(8,128)(2,1)S(1)} collective-permute-done((bf16[4,2,64,768]{3,2,0,1:T(8,128)(2,1)S(1)}, bf16[4,2,64,768]{3,2,0,1:T(8,128)(2,1)S(1)}, u32[]{:S(2)}, u32[]{:S(2)}) %collective-permute-start.2) | collective-permute-done | bytes 786464 | tf_op jit(solution)/shard_map/ppermute | solution.py:268
  408.1 4.8 %collective-permute-done.3 = bf16[4,64,768]{2,1,0:T(8,128)(2,1)S(1)} collective-permute-done((bf16[4,64,768]{2,1,0:T(8,128)(2,1)S(1)}, bf16[4,64,768]{2,1,0:T(8,128)(2,1)S(1)}, u32[]{:S(2)}, u32[]{:S(2)}) %collective-permute-start.3) | collective-permute-done | bytes 393248 | tf_op jit(solution)/shard_map/ppermute | solution.py:268
  413.1 1.8 collective-permute-start.4
  417.1 4.3 collective-permute-start.5
  423.0 2.3 collective-permute-start.44
  427.5 4.9 %collective-permute-start.6 = (bf16[64,768]{1,0:T(8,128)(2,1)S(1)}, bf16[64,768]{1,0:T(8,128)(2,1)S(1)}, u32[]{:S(2)}, u32[]{:S(2)}) collective-permute-start(bf16[64,768]{1,0:T(8,128)(2,1)S(1)} %get-tuple-element.50), channel_id=1, source_target_pairs={{0,4},{1,5},{2,6},{3,7},{4,8},{5,9},{6,10},{7,11},{8,12},{9,13},{1... | collective-permute-start | bytes 294920 | tf_op jit(solution)/shard_map/ppermute | solution.py:282
  434.0 5.2 %collective-permute-start.12 = (bf16[80,768]{1,0:T(8,128)(2,1)S(1)}, bf16[80,768]{1,0:T(8,128)(2,1)S(1)}, u32[]{:S(2)}, u32[]{:S(2)}) collective-permute-start(bf16[80,768]{1,0:T(8,128)(2,1)S(1)} %get-tuple-element.48), channel_id=1, source_target_pairs={{0,4},{1,5},{2,6},{3,7},{16,20},{17,21},{18,22},{19,23}} | collective-permute-start | bytes 368648 | tf_op jit(solution)/shard_map/ppermute | solution.py:282
  439.9 1.9 all-gather
  442.1 3.9 collective-permute-start.13
  446.0 2.2 all-gather.4
  449.5 5.0 %collective-permute-start.14 = (bf16[80,768]{1,0:T(8,128)(2,1)S(1)}, bf16[80,768]{1,0:T(8,128)(2,1)S(1)}, u32[]{:S(2)}, u32[]{:S(2)}) collective-permute-start(bf16[80,768]{1,0:T(8,128)(2,1)S(1)} %get-tuple-element.46), channel_id=1, source_target_pairs={{0,4},{1,5},{2,6},{3,7},{4,8},{5,9},{6,10},{7,11},{8,12},{9,13},{1... | collective-permute-start | bytes 368648 | tf_op jit(solution)/shard_map/ppermute | solution.py:282
  457.0 5.8 %collective-permute-done.17 = bf16[80,768]{1,0:T(8,128)(2,1)S(1)} collective-permute-done((bf16[80,768]{1,0:T(8,128)(2,1)S(1)}, bf16[80,768]{1,0:T(8,128)(2,1)S(1)}, u32[]{:S(2)}, u32[]{:S(2)}) %collective-permute-start.17) | collective-permute-done | bytes 122912 | tf_op jit(solution)/shard_map/ppermute | solution.py:283
  462.8 2.0 all-gather.1
  (216 shorter events, 69.2 us)
Async XLA Ops:
  0.6 99.1 %copy-start = (bf16[1024,1024]{1,0:T(8,128)(2,1)S(1)}, bf16[1024,1024]{1,0:T(8,128)(2,1)}, u32[]{:S(2)}) copy-start(bf16[1024,1024]{1,0:T(8,128)(2,1)} %param.12) | copy-start | bytes 6291460
  16.8 8.6 %copy-start.22 = (s32[1,3]{1,0:T(1,128)S(1)}, s32[1,3]{1,0:T(1,128)}, u32[]{:S(2)}) copy-start(s32[1,3]{1,0:T(1,128)} %param.10) | copy-start | bytes 40
  16.8 42.7 %all-to-all-start = ((bf16[16,192,256]{2,1,0:T(8,128)(2,1)}), bf16[16,192,256]{2,1,0:T(8,128)(2,1)}, u32[]{:S(2)}, u32[]{:S(2)}) async-start(bf16[16,192,256]{2,1,0:T(8,128)(2,1)} %bitcast.335), calls=%async_computation | async-start | bytes 3145728 | tf_op jit(solution)/shard_map/all_to_all | solution.py:245
  25.3 68.7 %collective-permute-start = (bf16[256,1024]{1,0:T(8,128)(2,1)}, bf16[256,1024]{1,0:T(8,128)(2,1)}, u32[]{:S(2)}, u32[]{:S(2)}) collective-permute-start(bf16[256,1024]{1,0:T(8,128)(2,1)} %fusion.36), channel_id=1, source_target_pairs={{0,16},{16,0},{1,17},{17,1},{2,18},{18,2},{3,19},{19,3},{4,20},{20... | collective-permute-start | bytes 1572872 | tf_op jit(solution)/shard_map/ppermute | solution.py:237
  27.4 58.0 %copy-start.5 = (bf16[1,256,1024]{2,1,0:T(8,128)(2,1)S(1)}, bf16[1,256,1024]{2,1,0:T(8,128)(2,1)}, u32[]{:S(2)}) copy-start(bf16[1,256,1024]{2,1,0:T(8,128)(2,1)} %param.17) | copy-start | bytes 1572868
  77.6 22.0 %all-to-all-start.1 = ((bf16[16,64,256]{2,1,0:T(8,128)(2,1)}), bf16[16,64,256]{2,1,0:T(8,128)(2,1)}, u32[]{:S(2)}, u32[]{:S(2)}) async-start(bf16[16,64,256]{2,1,0:T(8,128)(2,1)} %get-tuple-element.10.out_ref), calls=%async_computation.1 | async-start | bytes 1048576 | tf_op jit(solution)/shard_map/all_to_all | solution.py:251
  86.3 179.1 %collective-permute-start.39 = (bf16[256,512]{1,0:T(8,128)(2,1)}, bf16[256,512]{1,0:T(8,128)(2,1)}, u32[]{:S(2)}, u32[]{:S(2)}) collective-permute-start(bf16[256,512]{1,0:T(8,128)(2,1)} %get-tuple-element.41), channel_id=1, source_target_pairs={{0,16},{16,0},{1,17},{17,1},{2,18},{18,2},{3,19},{19,3},{4,20},{20... | collective-permute-start | bytes 786440 | tf_op jit(solution)/shard_map/ppermute | solution.py:237
  102.2 11.4 %slice-start = ((s8[8388608]{0:T(1024)(128)(4,1)}), s8[4194304]{0:T(1024)(128)(4,1)S(1)}, s32[]{:S(2)}) async-start(s8[8388608]{0:T(1024)(128)(4,1)} %bitcast.357), calls=%async_computation.4 | async-start | bytes 8388608
  103.2 10.4 %slice-start.1 = ((s8[8388608]{0:T(1024)(128)(4,1)}), s8[4194304]{0:T(1024)(128)(4,1)S(1)}, s32[]{:S(2)}) async-start(s8[8388608]{0:T(1024)(128)(4,1)} %bitcast.357), calls=%async_computation.5 | async-start | bytes 8388608
  103.2 52.6 %collective-permute-start.28 = (bf16[256,1024]{1,0:T(8,128)(2,1)}, bf16[256,1024]{1,0:T(8,128)(2,1)}, u32[]{:S(2)}, u32[]{:S(2)}) collective-permute-start(bf16[256,1024]{1,0:T(8,128)(2,1)} %multiply_convert_fusion.1), channel_id=1, source_target_pairs={{0,16},{16,0},{1,17},{17,1},{2,18},{18,2},{3,19},{19,3},{4,20},{20... | collective-permute-start | bytes 1572872 | tf_op jit(solution)/shard_map/ppermute | solution.py:237
  116.3 4.7 %collective-permute-start.18 = (bf16[256,1024]{0,1:T(8,128)(2,1)}, bf16[256,1024]{0,1:T(8,128)(2,1)}, u32[]{:S(2)}, u32[]{:S(2)}) collective-permute-start(bf16[256,1024]{0,1:T(8,128)(2,1)} %bitcast.53), channel_id=1, source_target_pairs={{0,16},{16,0},{1,17},{17,1},{2,18},{18,2},{3,19},{19,3},{4,20},{20... | collective-permute-start | bytes 1572872 | tf_op jit(solution)/shard_map/ppermute | solution.py:237
  119.6 2.7 collective-permute-start.19
  120.8 127.4 %collective-permute-start.38 = (bf16[256,4096]{1,0:T(8,128)(2,1)}, bf16[256,4096]{1,0:T(8,128)(2,1)}, u32[]{:S(2)}, u32[]{:S(2)}) collective-permute-start(bf16[256,4096]{1,0:T(8,128)(2,1)} %get-tuple-element.23), channel_id=1, source_target_pairs={{0,16},{16,0},{1,17},{17,1},{2,18},{18,2},{3,19},{19,3},{4,20},{20... | collective-permute-start | bytes 6291464 | tf_op jit(solution)/shard_map/ppermute | solution.py:237
  123.9 17.0 %collective-permute-start.20 = (bf16[4,2,80,512]{3,2,0,1:T(8,128)(2,1)S(1)}, bf16[4,2,80,512]{3,2,0,1:T(8,128)(2,1)S(1)}, u32[]{:S(2)}, u32[]{:S(2)}) collective-permute-start(bf16[4,2,80,512]{3,2,0,1:T(8,128)(2,1)S(1)} %pad_maximum_fusion.12), channel_id=1, source_target_pairs={{0,1},{1,0},{2,3},{3,2},{4,5},{5,4},{6,7},{7,6},{8,9},{9,8},{10,11... | collective-permute-start | bytes 1966088 | tf_op jit(solution)/shard_map/ppermute | solution.py:268
  131.3 11.4 %copy-start.8 = (bf16[256,1024]{1,0:T(8,128)(2,1)S(1)}, bf16[256,1024]{1,0:T(8,128)(2,1)}, u32[]{:S(2)}) copy-start(bf16[256,1024]{1,0:T(8,128)(2,1)} %copy-done.7) | copy-start | bytes 1572868
  141.9 9.6 %collective-permute-start.21 = (bf16[4,80,512]{2,1,0:T(8,128)(2,1)}, bf16[4,80,512]{2,1,0:T(8,128)(2,1)}, u32[]{:S(2)}, u32[]{:S(2)}) collective-permute-start(bf16[4,80,512]{2,1,0:T(8,128)(2,1)} %fusion.98), channel_id=1, source_target_pairs={{0,2},{1,3},{2,0},{3,1},{4,6},{5,7},{6,4},{7,5},{8,10},{9,11},{10,... | collective-permute-start | bytes 983048 | tf_op jit(solution)/shard_map/ppermute | solution.py:268
  143.5 5.7 %copy-start.11 = (bf16[256,4096]{1,0:T(8,128)(2,1)S(1)}, bf16[256,4096]{1,0:T(8,128)(2,1)}, u32[]{:S(2)}) copy-start(bf16[256,4096]{1,0:T(8,128)(2,1)} %copy-done.10) | copy-start | bytes 6291460
  144.5 19.5 %all-to-all-start.2 = ((bf16[16,64,256]{2,1,0:T(8,128)(2,1)}), bf16[16,64,256]{2,1,0:T(8,128)(2,1)}, u32[]{:S(2)}, u32[]{:S(2)}) async-start(bf16[16,64,256]{2,1,0:T(8,128)(2,1)} %bitcast.12), calls=%async_computation.2 | async-start | bytes 1048576 | tf_op jit(solution)/shard_map/all_to_all | solution.py:245
  150.8 52.3 %collective-permute-start.29 = (bf16[256,2048]{1,0:T(8,128)(2,1)}, bf16[256,2048]{1,0:T(8,128)(2,1)}, u32[]{:S(2)}, u32[]{:S(2)}) collective-permute-start(bf16[256,2048]{1,0:T(8,128)(2,1)} %get-tuple-element.25), channel_id=1, source_target_pairs={{0,16},{16,0},{1,17},{17,1},{2,18},{18,2},{3,19},{19,3},{4,20},{20... | collective-permute-start | bytes 3145736 | tf_op jit(solution)/shard_map/ppermute | solution.py:237
  152.6 6.5 %collective-permute-start.22 = (bf16[80,512]{1,0:T(8,128)(2,1)S(1)}, bf16[80,512]{1,0:T(8,128)(2,1)S(1)}, u32[]{:S(2)}, u32[]{:S(2)}) collective-permute-start(bf16[80,512]{1,0:T(8,128)(2,1)S(1)} %get-tuple-element.58), channel_id=1, source_target_pairs={{0,4},{1,5},{2,6},{3,7},{16,20},{17,21},{18,22},{19,23}} | collective-permute-start | bytes 245768 | tf_op jit(solution)/shard_map/ppermute | solution.py:282
  157.6 44.8 %collective-permute-start.25 = (bf16[80,512]{1,0:T(8,128)(2,1)S(1)}, bf16[80,512]{1,0:T(8,128)(2,1)S(1)}, u32[]{:S(2)}, u32[]{:S(2)}) collective-permute-start(bf16[80,512]{1,0:T(8,128)(2,1)S(1)} %get-tuple-element.59), channel_id=1, source_target_pairs={{12,8},{13,9},{14,10},{15,11},{28,24},{29,25},{30,26},{31,27}} | collective-permute-start | bytes 245768 | tf_op jit(solution)/shard_map/ppermute | solution.py:283
  159.0 43.3 %collective-permute-start.23 = (bf16[80,512]{1,0:T(8,128)(2,1)S(1)}, bf16[80,512]{1,0:T(8,128)(2,1)S(1)}, u32[]{:S(2)}, u32[]{:S(2)}) collective-permute-start(bf16[80,512]{1,0:T(8,128)(2,1)S(1)} %fusion.113), channel_id=1, source_target_pairs={{0,4},{1,5},{2,6},{3,7},{4,8},{5,9},{6,10},{7,11},{16,20},{17,21},... | collective-permute-start | bytes 245768 | tf_op jit(solution)/shard_map/ppermute | solution.py:282
  197.8 84.9 %all-to-all-start.3 = ((bf16[16,192,256]{2,1,0:T(8,128)(2,1)}), bf16[16,192,256]{2,1,0:T(8,128)(2,1)}, u32[]{:S(2)}, u32[]{:S(2)}) async-start(bf16[16,192,256]{2,1,0:T(8,128)(2,1)} %attention_backward.1), calls=%async_computation.3 | async-start | bytes 3145728 | tf_op jit(solution)/shard_map/all_to_all | solution.py:251
  202.4 10.3 %collective-permute-start.26 = (bf16[80,512]{1,0:T(8,128)(2,1)S(1)}, bf16[80,512]{1,0:T(8,128)(2,1)S(1)}, u32[]{:S(2)}, u32[]{:S(2)}) collective-permute-start(bf16[80,512]{1,0:T(8,128)(2,1)S(1)} %get-tuple-element.57), channel_id=1, source_target_pairs={{8,4},{9,5},{10,6},{11,7},{12,8},{13,9},{14,10},{15,11},{24,20},{2... | collective-permute-start | bytes 245768 | tf_op jit(solution)/shard_map/ppermute | solution.py:283
  206.9 69.2 %collective-permute-start.30 = (bf16[4,2,64,2048]{3,2,0,1:T(8,128)(2,1)}, bf16[4,2,64,2048]{3,2,0,1:T(8,128)(2,1)}, u32[]{:S(2)}, u32[]{:S(2)}) collective-permute-start(bf16[4,2,64,2048]{3,2,0,1:T(8,128)(2,1)} %convolution_convert_fusion.1), channel_id=1, source_target_pairs={{0,1},{1,0},{2,3},{3,2},{4,5},{5,4},{6,7},{7,6},{8,9},{9,8},{10,11... | collective-permute-start | bytes 6291464 | tf_op jit(solution)/shard_map/ppermute | solution.py:268
  208.7 19.8 %collective-permute-start.24 = (bf16[80,512]{1,0:T(8,128)(2,1)S(1)}, bf16[80,512]{1,0:T(8,128)(2,1)S(1)}, u32[]{:S(2)}, u32[]{:S(2)}) collective-permute-start(bf16[80,512]{1,0:T(8,128)(2,1)S(1)} %get-tuple-element.56), channel_id=1, source_target_pairs={{0,4},{1,5},{2,6},{3,7},{4,8},{5,9},{6,10},{7,11},{8,12},{9,13},{1... | collective-permute-start | bytes 245768 | tf_op jit(solution)/shard_map/ppermute | solution.py:282
  212.7 32.1 %collective-permute-start.27 = (bf16[80,512]{1,0:T(8,128)(2,1)S(1)}, bf16[80,512]{1,0:T(8,128)(2,1)S(1)}, u32[]{:S(2)}, u32[]{:S(2)}) collective-permute-start(bf16[80,512]{1,0:T(8,128)(2,1)S(1)} %fusion.112), channel_id=1, source_target_pairs={{4,0},{5,1},{6,2},{7,3},{8,4},{9,5},{10,6},{11,7},{12,8},{13,9},{1... | collective-permute-start | bytes 245768 | tf_op jit(solution)/shard_map/ppermute | solution.py:283
  218.0 30.2 %copy-start.15 = (bf16[256,4096]{1,0:T(8,128)(2,1)S(1)}, bf16[256,4096]{1,0:T(8,128)(2,1)}, u32[]{:S(2)}) copy-start(bf16[256,4096]{1,0:T(8,128)(2,1)} %get-tuple-element.23) | copy-start | bytes 6291460
  269.0 92.8 %collective-permute-start.40 = (bf16[4,2,256,512]{3,2,0,1:T(8,128)(2,1)}, bf16[4,2,256,512]{3,2,0,1:T(8,128)(2,1)}, u32[]{:S(2)}, u32[]{:S(2)}) collective-permute-start(bf16[4,2,256,512]{3,2,0,1:T(8,128)(2,1)} %fusion.21), channel_id=1, source_target_pairs={{0,2},{1,3},{2,0},{3,1},{4,6},{5,7},{6,4},{7,5},{8,10},{9,11},{10,... | collective-permute-start | bytes 6291464 | tf_op jit(solution)/shard_map/ppermute | solution.py:268
  279.2 61.0 %collective-permute-start.31 = (bf16[4,64,2048]{2,1,0:T(8,128)(2,1)}, bf16[4,64,2048]{2,1,0:T(8,128)(2,1)S(1)}, u32[]{:S(2)}, u32[]{:S(2)}) collective-permute-start(bf16[4,64,2048]{2,1,0:T(8,128)(2,1)} %fusion.44), channel_id=1, source_target_pairs={{0,2},{1,3},{2,0},{3,1},{4,6},{5,7},{6,4},{7,5},{8,10},{9,11},{10,... | collective-permute-start | bytes 3145736 | tf_op jit(solution)/shard_map/ppermute | solution.py:268
  290.2 50.0 %copy-start.12 = (bf16[4,2,64,2048]{3,2,1,0:T(8,128)(2,1)S(1)}, bf16[4,2,64,2048]{3,2,1,0:T(8,128)(2,1)}, u32[]{:S(2)}) copy-start(bf16[4,2,64,2048]{3,2,1,0:T(8,128)(2,1)} %convolution_convert_fusion.2) | copy-start | bytes 6291460
  342.0 15.5 %copy-start.3 = (f32[256,1024]{1,0:T(8,128)S(1)}, f32[256,1024]{1,0:T(8,128)}, u32[]{:S(2)}) copy-start(f32[256,1024]{1,0:T(8,128)} %get-tuple-element.19) | copy-start | bytes 3145732
  342.0 9.5 %collective-permute-start.32 = (bf16[64,2048]{1,0:T(8,128)(2,1)S(1)}, bf16[64,2048]{1,0:T(8,128)(2,1)S(1)}, u32[]{:S(2)}, u32[]{:S(2)}) collective-permute-start(bf16[64,2048]{1,0:T(8,128)(2,1)S(1)} %get-tuple-element.34), channel_id=1, source_target_pairs={{0,4},{1,5},{2,6},{3,7},{16,20},{17,21},{18,22},{19,23}} | collective-permute-start | bytes 786440 | tf_op jit(solution)/shard_map/ppermute | solution.py:282
  348.5 20.6 %collective-permute-start.1 = (bf16[256,1536]{1,0:T(8,128)(2,1)}, bf16[256,1536]{1,0:T(8,128)(2,1)}, u32[]{:S(2)}, u32[]{:S(2)}) collective-permute-start(bf16[256,1536]{1,0:T(8,128)(2,1)} %copy.96), channel_id=1, source_target_pairs={{0,16},{16,0},{1,17},{17,1},{2,18},{18,2},{3,19},{19,3},{4,20},{20... | collective-permute-start | bytes 2359304 | tf_op jit(solution)/shard_map/ppermute | solution.py:237
  348.5 16.6 %collective-permute-start.35 = (bf16[64,2048]{1,0:T(8,128)(2,1)S(1)}, bf16[64,2048]{1,0:T(8,128)(2,1)}, u32[]{:S(2)}, u32[]{:S(2)}) collective-permute-start(bf16[64,2048]{1,0:T(8,128)(2,1)S(1)} %get-tuple-element.35), channel_id=1, source_target_pairs={{12,8},{13,9},{14,10},{15,11},{28,24},{29,25},{30,26},{31,27}} | collective-permute-start | bytes 786440 | tf_op jit(solution)/shard_map/ppermute | solution.py:283
  352.3 12.8 %collective-permute-start.33 = (bf16[64,2048]{1,0:T(8,128)(2,1)}, bf16[64,2048]{1,0:T(8,128)(2,1)}, u32[]{:S(2)}, u32[]{:S(2)}) collective-permute-start(bf16[64,2048]{1,0:T(8,128)(2,1)} %fusion.69), channel_id=1, source_target_pairs={{0,4},{1,5},{2,6},{3,7},{4,8},{5,9},{6,10},{7,11},{16,20},{17,21},... | collective-permute-start | bytes 786440 | tf_op jit(solution)/shard_map/ppermute | solution.py:282
  361.8 7.4 %copy-start.4 = (bf16[512,1024]{0,1:T(8,128)(2,1)S(1)}, bf16[512,1024]{0,1:T(8,128)(2,1)}, u32[]{:S(2)}) copy-start(bf16[512,1024]{0,1:T(8,128)(2,1)} %copy.51) | copy-start | bytes 3145732
  363.7 26.2 %collective-permute-start.41 = (bf16[4,256,512]{2,1,0:T(8,128)(2,1)S(1)}, bf16[4,256,512]{2,1,0:T(8,128)(2,1)S(1)}, u32[]{:S(2)}, u32[]{:S(2)}) collective-permute-start(bf16[4,256,512]{2,1,0:T(8,128)(2,1)S(1)} %fusion.45), channel_id=1, source_target_pairs={{0,1},{1,0},{2,3},{3,2},{4,5},{5,4},{6,7},{7,6},{8,9},{9,8},{10,11... | collective-permute-start | bytes 3145736 | tf_op jit(solution)/shard_map/ppermute | solution.py:268
  366.4 11.6 %collective-permute-start.36 = (bf16[64,2048]{1,0:T(8,128)(2,1)S(1)}, bf16[64,2048]{1,0:T(8,128)(2,1)S(1)}, u32[]{:S(2)}, u32[]{:S(2)}) collective-permute-start(bf16[64,2048]{1,0:T(8,128)(2,1)S(1)} %get-tuple-element.33), channel_id=1, source_target_pairs={{8,4},{9,5},{10,6},{11,7},{12,8},{13,9},{14,10},{15,11},{24,20},{2... | collective-permute-start | bytes 786440 | tf_op jit(solution)/shard_map/ppermute | solution.py:283
  367.0 25.9 %collective-permute-start.34 = (bf16[64,2048]{1,0:T(8,128)(2,1)S(1)}, bf16[64,2048]{1,0:T(8,128)(2,1)S(1)}, u32[]{:S(2)}, u32[]{:S(2)}) collective-permute-start(bf16[64,2048]{1,0:T(8,128)(2,1)S(1)} %get-tuple-element.32), channel_id=1, source_target_pairs={{0,4},{1,5},{2,6},{3,7},{4,8},{5,9},{6,10},{7,11},{8,12},{9,13},{1... | collective-permute-start | bytes 786440 | tf_op jit(solution)/shard_map/ppermute | solution.py:282
  370.8 33.4 %collective-permute-start.2 = (bf16[4,2,64,768]{3,2,0,1:T(8,128)(2,1)S(1)}, bf16[4,2,64,768]{3,2,0,1:T(8,128)(2,1)S(1)}, u32[]{:S(2)}, u32[]{:S(2)}) collective-permute-start(bf16[4,2,64,768]{3,2,0,1:T(8,128)(2,1)S(1)} %convolution_convert_fusion.5), channel_id=1, source_target_pairs={{0,1},{1,0},{2,3},{3,2},{4,5},{5,4},{6,7},{7,6},{8,9},{9,8},{10,11... | collective-permute-start | bytes 2359304 | tf_op jit(solution)/shard_map/ppermute | solution.py:268
  373.3 48.1 %collective-permute-start.10 = (bf16[4,2,80,768]{3,2,0,1:T(8,128)(2,1)S(1)}, bf16[4,2,80,768]{3,2,0,1:T(8,128)(2,1)S(1)}, u32[]{:S(2)}, u32[]{:S(2)}) collective-permute-start(bf16[4,2,80,768]{3,2,0,1:T(8,128)(2,1)S(1)} %pad_maximum_fusion.9), channel_id=1, source_target_pairs={{0,2},{1,3},{2,0},{3,1},{4,6},{5,7},{6,4},{7,5},{8,10},{9,11},{10,... | collective-permute-start | bytes 2949128 | tf_op jit(solution)/shard_map/ppermute | solution.py:268
  376.2 13.7 %copy-start.9 = (bf16[4,2,256,512]{3,2,1,0:T(8,128)(2,1)S(1)}, bf16[4,2,256,512]{3,2,1,0:T(8,128)(2,1)}, u32[]{:S(2)}) copy-start(bf16[4,2,256,512]{3,2,1,0:T(8,128)(2,1)} %fusion.18) | copy-start | bytes 6291460
  378.0 15.6 %collective-permute-start.37 = (bf16[64,2048]{1,0:T(8,128)(2,1)S(1)}, bf16[64,2048]{1,0:T(8,128)(2,1)S(1)}, u32[]{:S(2)}, u32[]{:S(2)}) collective-permute-start(bf16[64,2048]{1,0:T(8,128)(2,1)S(1)} %fusion.68), channel_id=1, source_target_pairs={{4,0},{5,1},{6,2},{7,3},{8,4},{9,5},{10,6},{11,7},{12,8},{13,9},{1... | collective-permute-start | bytes 786440 | tf_op jit(solution)/shard_map/ppermute | solution.py:283
  391.6 14.9 %collective-permute-start.42 = (bf16[256,512]{1,0:T(8,128)(2,1)S(1)}, bf16[256,512]{1,0:T(8,128)(2,1)S(1)}, u32[]{:S(2)}, u32[]{:S(2)}) collective-permute-start(bf16[256,512]{1,0:T(8,128)(2,1)S(1)} %get-tuple-element.30), channel_id=1, source_target_pairs={{0,4},{1,5},{2,6},{3,7},{16,20},{17,21},{18,22},{19,23}} | collective-permute-start | bytes 786440 | tf_op jit(solution)/shard_map/ppermute | solution.py:282
  392.9 22.0 %collective-permute-start.45 = (bf16[256,512]{1,0:T(8,128)(2,1)S(1)}, bf16[256,512]{1,0:T(8,128)(2,1)S(1)}, u32[]{:S(2)}, u32[]{:S(2)}) collective-permute-start(bf16[256,512]{1,0:T(8,128)(2,1)S(1)} %get-tuple-element.31), channel_id=1, source_target_pairs={{12,8},{13,9},{14,10},{15,11},{28,24},{29,25},{30,26},{31,27}} | collective-permute-start | bytes 786440 | tf_op jit(solution)/shard_map/ppermute | solution.py:283
  404.3 8.6 %collective-permute-start.3 = (bf16[4,64,768]{2,1,0:T(8,128)(2,1)S(1)}, bf16[4,64,768]{2,1,0:T(8,128)(2,1)S(1)}, u32[]{:S(2)}, u32[]{:S(2)}) collective-permute-start(bf16[4,64,768]{2,1,0:T(8,128)(2,1)S(1)} %fusion.91), channel_id=1, source_target_pairs={{0,2},{1,3},{2,0},{3,1},{4,6},{5,7},{6,4},{7,5},{8,10},{9,11},{10,... | collective-permute-start | bytes 1179656 | tf_op jit(solution)/shard_map/ppermute | solution.py:268
  406.6 8.3 %collective-permute-start.43 = (bf16[256,512]{1,0:T(8,128)(2,1)S(1)}, bf16[256,512]{1,0:T(8,128)(2,1)S(1)}, u32[]{:S(2)}, u32[]{:S(2)}) collective-permute-start(bf16[256,512]{1,0:T(8,128)(2,1)S(1)} %fusion.62), channel_id=1, source_target_pairs={{0,4},{1,5},{2,6},{3,7},{4,8},{5,9},{6,10},{7,11},{16,20},{17,21},... | collective-permute-start | bytes 786440 | tf_op jit(solution)/shard_map/ppermute | solution.py:282
  413.1 4.0 collective-permute-start.4
  415.1 11.0 %collective-permute-start.46 = (bf16[256,512]{1,0:T(8,128)(2,1)S(1)}, bf16[256,512]{1,0:T(8,128)(2,1)S(1)}, u32[]{:S(2)}, u32[]{:S(2)}) collective-permute-start(bf16[256,512]{1,0:T(8,128)(2,1)S(1)} %get-tuple-element.29), channel_id=1, source_target_pairs={{8,4},{9,5},{10,6},{11,7},{12,8},{13,9},{14,10},{15,11},{24,20},{2... | collective-permute-start | bytes 786440 | tf_op jit(solution)/shard_map/ppermute | solution.py:283
  415.8 9.6 %collective-permute-start.7 = (bf16[64,768]{1,0:T(8,128)(2,1)S(1)}, bf16[64,768]{1,0:T(8,128)(2,1)S(1)}, u32[]{:S(2)}, u32[]{:S(2)}) collective-permute-start(bf16[64,768]{1,0:T(8,128)(2,1)S(1)} %get-tuple-element.53), channel_id=1, source_target_pairs={{12,8},{13,9},{14,10},{15,11},{28,24},{29,25},{30,26},{31,27}} | collective-permute-start | bytes 294920 | tf_op jit(solution)/shard_map/ppermute | solution.py:283
  417.1 8.2 %collective-permute-start.5 = (bf16[64,768]{1,0:T(8,128)(2,1)S(1)}, bf16[64,768]{1,0:T(8,128)(2,1)S(1)}, u32[]{:S(2)}, u32[]{:S(2)}) collective-permute-start(bf16[64,768]{1,0:T(8,128)(2,1)S(1)} %fusion.107), channel_id=1, source_target_pairs={{0,4},{1,5},{2,6},{3,7},{4,8},{5,9},{6,10},{7,11},{16,20},{17,21},... | collective-permute-start | bytes 294920 | tf_op jit(solution)/shard_map/ppermute | solution.py:282
  421.6 12.2 %collective-permute-start.11 = (bf16[4,80,768]{2,1,0:T(8,128)(2,1)S(1)}, bf16[4,80,768]{2,1,0:T(8,128)(2,1)S(1)}, u32[]{:S(2)}, u32[]{:S(2)}) collective-permute-start(bf16[4,80,768]{2,1,0:T(8,128)(2,1)S(1)} %fusion.90), channel_id=1, source_target_pairs={{0,1},{1,0},{2,3},{3,2},{4,5},{5,4},{6,7},{7,6},{8,9},{9,8},{10,11... | collective-permute-start | bytes 1474568 | tf_op jit(solution)/shard_map/ppermute | solution.py:268
  423.0 18.9 %collective-permute-start.44 = (bf16[256,512]{1,0:T(8,128)(2,1)S(1)}, bf16[256,512]{1,0:T(8,128)(2,1)S(1)}, u32[]{:S(2)}, u32[]{:S(2)}) collective-permute-start(bf16[256,512]{1,0:T(8,128)(2,1)S(1)} %get-tuple-element.28), channel_id=1, source_target_pairs={{0,4},{1,5},{2,6},{3,7},{4,8},{5,9},{6,10},{7,11},{8,12},{9,13},{1... | collective-permute-start | bytes 786440 | tf_op jit(solution)/shard_map/ppermute | solution.py:282
  425.4 7.0 %collective-permute-start.8 = (bf16[64,768]{1,0:T(8,128)(2,1)S(1)}, bf16[64,768]{1,0:T(8,128)(2,1)S(1)}, u32[]{:S(2)}, u32[]{:S(2)}) collective-permute-start(bf16[64,768]{1,0:T(8,128)(2,1)S(1)} %get-tuple-element.51), channel_id=1, source_target_pairs={{8,4},{9,5},{10,6},{11,7},{12,8},{13,9},{14,10},{15,11},{24,20},{2... | collective-permute-start | bytes 294920 | tf_op jit(solution)/shard_map/ppermute | solution.py:283
  426.2 15.8 %collective-permute-start.47 = (bf16[256,512]{1,0:T(8,128)(2,1)S(1)}, bf16[256,512]{1,0:T(8,128)(2,1)S(1)}, u32[]{:S(2)}, u32[]{:S(2)}) collective-permute-start(bf16[256,512]{1,0:T(8,128)(2,1)S(1)} %fusion.61), channel_id=1, source_target_pairs={{4,0},{5,1},{6,2},{7,3},{8,4},{9,5},{10,6},{11,7},{12,8},{13,9},{1... | collective-permute-start | bytes 786440 | tf_op jit(solution)/shard_map/ppermute | solution.py:283
  427.5 11.7 %collective-permute-start.6 = (bf16[64,768]{1,0:T(8,128)(2,1)S(1)}, bf16[64,768]{1,0:T(8,128)(2,1)S(1)}, u32[]{:S(2)}, u32[]{:S(2)}) collective-permute-start(bf16[64,768]{1,0:T(8,128)(2,1)S(1)} %get-tuple-element.50), channel_id=1, source_target_pairs={{0,4},{1,5},{2,6},{3,7},{4,8},{5,9},{6,10},{7,11},{8,12},{9,13},{1... | collective-permute-start | bytes 294920 | tf_op jit(solution)/shard_map/ppermute | solution.py:282
  432.5 7.4 %collective-permute-start.9 = (bf16[64,768]{1,0:T(8,128)(2,1)S(1)}, bf16[64,768]{1,0:T(8,128)(2,1)S(1)}, u32[]{:S(2)}, u32[]{:S(2)}) collective-permute-start(bf16[64,768]{1,0:T(8,128)(2,1)S(1)} %fusion.106), channel_id=1, source_target_pairs={{4,0},{5,1},{6,2},{7,3},{8,4},{9,5},{10,6},{11,7},{12,8},{13,9},{1... | collective-permute-start | bytes 294920 | tf_op jit(solution)/shard_map/ppermute | solution.py:283
  434.0 8.1 %collective-permute-start.12 = (bf16[80,768]{1,0:T(8,128)(2,1)S(1)}, bf16[80,768]{1,0:T(8,128)(2,1)S(1)}, u32[]{:S(2)}, u32[]{:S(2)}) collective-permute-start(bf16[80,768]{1,0:T(8,128)(2,1)S(1)} %get-tuple-element.48), channel_id=1, source_target_pairs={{0,4},{1,5},{2,6},{3,7},{16,20},{17,21},{18,22},{19,23}} | collective-permute-start | bytes 368648 | tf_op jit(solution)/shard_map/ppermute | solution.py:282
  439.2 9.0 %collective-permute-start.15 = (bf16[80,768]{1,0:T(8,128)(2,1)S(1)}, bf16[80,768]{1,0:T(8,128)(2,1)S(1)}, u32[]{:S(2)}, u32[]{:S(2)}) collective-permute-start(bf16[80,768]{1,0:T(8,128)(2,1)S(1)} %get-tuple-element.49), channel_id=1, source_target_pairs={{12,8},{13,9},{14,10},{15,11},{28,24},{29,25},{30,26},{31,27}} | collective-permute-start | bytes 368648 | tf_op jit(solution)/shard_map/ppermute | solution.py:283
  442.1 6.5 %collective-permute-start.13 = (bf16[80,768]{1,0:T(8,128)(2,1)S(1)}, bf16[80,768]{1,0:T(8,128)(2,1)S(1)}, u32[]{:S(2)}, u32[]{:S(2)}) collective-permute-start(bf16[80,768]{1,0:T(8,128)(2,1)S(1)} %fusion.101), channel_id=1, source_target_pairs={{0,4},{1,5},{2,6},{3,7},{4,8},{5,9},{6,10},{7,11},{16,20},{17,21},... | collective-permute-start | bytes 368648 | tf_op jit(solution)/shard_map/ppermute | solution.py:282
  448.7 5.8 %collective-permute-start.16 = (bf16[80,768]{1,0:T(8,128)(2,1)S(1)}, bf16[80,768]{1,0:T(8,128)(2,1)S(1)}, u32[]{:S(2)}, u32[]{:S(2)}) collective-permute-start(bf16[80,768]{1,0:T(8,128)(2,1)S(1)} %get-tuple-element.47), channel_id=1, source_target_pairs={{8,4},{9,5},{10,6},{11,7},{12,8},{13,9},{14,10},{15,11},{24,20},{2... | collective-permute-start | bytes 368648 | tf_op jit(solution)/shard_map/ppermute | solution.py:283
  449.5 7.4 %collective-permute-start.14 = (bf16[80,768]{1,0:T(8,128)(2,1)S(1)}, bf16[80,768]{1,0:T(8,128)(2,1)S(1)}, u32[]{:S(2)}, u32[]{:S(2)}) collective-permute-start(bf16[80,768]{1,0:T(8,128)(2,1)S(1)} %get-tuple-element.46), channel_id=1, source_target_pairs={{0,4},{1,5},{2,6},{3,7},{4,8},{5,9},{6,10},{7,11},{8,12},{9,13},{1... | collective-permute-start | bytes 368648 | tf_op jit(solution)/shard_map/ppermute | solution.py:282
  454.6 8.2 %collective-permute-start.17 = (bf16[80,768]{1,0:T(8,128)(2,1)S(1)}, bf16[80,768]{1,0:T(8,128)(2,1)S(1)}, u32[]{:S(2)}, u32[]{:S(2)}) collective-permute-start(bf16[80,768]{1,0:T(8,128)(2,1)S(1)} %fusion.100), channel_id=1, source_target_pairs={{4,0},{5,1},{6,2},{7,3},{8,4},{9,5},{10,6},{11,7},{12,8},{13,9},{1... | collective-permute-start | bytes 368648 | tf_op jit(solution)/shard_map/ppermute | solution.py:283
  (14 other events, 34.5 us)

commit v2 on v1

--- a/solution.py
+++ b/solution.py
@@ -13,7 +13,6 @@
 masked = -1e30
 log2e = 1.4426950408889634
 vmem_bytes = 56 * 2**20
-GAIN_ROWS = 16
 low = jnp.bfloat16
 full = jnp.float32
 
@@ -114,7 +113,7 @@
         ],
         compiler_params=pltpu.CompilerParams(vmem_limit_bytes=vmem_bytes),
         cost_estimate=pl.CostEstimate(
-            flops=4 * total * total * HEAD_DIM, bytes_accessed=4 * rows.size, transcendentals=total * total // 2
+            flops=20 * total * total * HEAD_DIM, bytes_accessed=4 * rows.size, transcendentals=total * total // 2
         ),
         name="attention_forward",
     )(ends, rows)
@@ -212,7 +211,7 @@
         ],
         compiler_params=pltpu.CompilerParams(vmem_limit_bytes=vmem_bytes),
         cost_estimate=pl.CostEstimate(
-            flops=10 * total * total * HEAD_DIM, bytes_accessed=8 * rows.size, transcendentals=total * total // 2
+            flops=35 * total * total * HEAD_DIM, bytes_accessed=8 * rows.size, transcendentals=total * total // 2
         ),
         name="attention_backward",
     )(ends, rows, grads, outs, mass)
@@ -232,31 +231,389 @@
     return inverse * (scaled - along - unit * across)
 
 
+def project_kernel(frames_ref, gain_ref, query_ref, key_ref, value_ref, rows_ref, low_ref):
+    @pl.when(pl.program_id(0) == 0)
+    def _():
+        unit, _ = norm_parts(frames_ref[...].astype(full))
+        low_ref[...] = (unit * gain_ref[...]).astype(low)
+
+    heads = rows_ref.shape[0]
+    for part, weight_ref in enumerate((query_ref, key_ref, value_ref)):
+        packed = jnp.dot(low_ref[...], weight_ref[...], preferred_element_type=full).astype(low).T
+        for head in range(heads):
+            rows_ref[head, part * HEAD_DIM : (part + 1) * HEAD_DIM, :] = packed[
+                head * HEAD_DIM : (head + 1) * HEAD_DIM
+            ]
+
+
+def thirds(features, wide):
+    count = features // wide
+    return [pl.BlockSpec((features, wide), lambda i, part=part: (0, part * count + i)) for part in range(3)]
+
+
+def project(frames, gain, w_qkv):
+    rows, features = frames.shape
+    wide = 4 * HEAD_DIM
+    return pl.pallas_call(
+        project_kernel,
+        grid=(features // wide,),
+        out_shape=(
+            jax.ShapeDtypeStruct((HEADS, 3 * HEAD_DIM, rows), low),
+            jax.ShapeDtypeStruct((rows, features), low),
+        ),
+        in_specs=[
+            pl.BlockSpec((rows, features), lambda i: (0, 0)),
+            pl.BlockSpec((1, features), lambda i: (0, 0)),
+        ]
+        + thirds(features, wide),
+        out_specs=[
+            pl.BlockSpec((4, 3 * HEAD_DIM, rows), lambda i: (i, 0, 0)),
+            pl.BlockSpec((rows, features), lambda i: (0, 0)),
+        ],
+        compiler_params=pltpu.CompilerParams(vmem_limit_bytes=vmem_bytes),
+        cost_estimate=pl.CostEstimate(
+            flops=6 * rows * features * features, bytes_accessed=8 * features * features, transcendentals=0
+        ),
+        name="norm_and_project",
+    )(frames, gain[None], w_qkv, w_qkv, w_qkv)
+
+
+def middle_kernel(
+    control_ref, frames_ref, att_ref, cot_ref, gain_ref, out_weight_ref, up_ref, down_ref,
+    result_ref, grad_middle_ref, branch_ref, branch_away_ref, grad_att_ref, low_two_ref, act_ref,
+    grad_hidden_ref, grad_hidden_away_ref, mixed_ref, mixed_away_ref,
+    unit_s, inverse_s, sum_s, back_s, low_two_s, mixed_s,
+):
+    step = pl.program_id(0)
+    steps = pl.num_programs(0)
+    core = control_ref[0]
+    valid = control_ref[1]
+    rows, features = frames_ref.shape
+    root = 0.7978845608028654
+    cubic = 0.044715
+    across = (((1,), (1,)), ((), ()))
+    present = (lax.broadcasted_iota(jnp.int32, (rows, 1), 0) < valid).astype(full)
+
+    def by_core(array, own_ref, away_ref):
+        halves = (array[:, : features // 2], array[:, features // 2 :])
+        for value in range(2):
+
+            @pl.when(core == value)
+            def _():
+                own_ref[...] = halves[value]
+                away_ref[...] = halves[1 - value]
+
+    @pl.when(step == 0)
+    def _():
+        middle = frames_ref[...].astype(full) + jnp.dot(
+            att_ref[...].T, out_weight_ref[...], preferred_element_type=full
+        )
+        unit, inverse = norm_parts(middle)
+        unit_s[...] = unit
+        inverse_s[...] = inverse
+        low_two_s[...] = (unit * gain_ref[...]).astype(low)
+        low_two_ref[...] = low_two_s[...].T
+        mixed_s[...] = (cot_ref[...].astype(full) * present).astype(low)
+        by_core(mixed_s[...], mixed_ref, mixed_away_ref)
+        sum_s[...] = middle
+        back_s[...] = jnp.zeros_like(back_s)
+
+    hidden = jnp.dot(low_two_s[...], up_ref[...], preferred_element_type=full)
+    grad_act = lax.dot_general(mixed_s[...], down_ref[...], across, preferred_element_type=full)
+    square = hidden * hidden
+    bent = jnp.tanh(root * hidden * (1.0 + cubic * square))
+    half = 0.5 * (1.0 + bent)
+    act = (hidden * half).astype(low)
+    slope = half + (0.5 * root) * hidden * (1.0 - bent * bent) * (1.0 + (3.0 * cubic) * square)
+    grad_hidden = (slope * grad_act).astype(low)
+    act_ref[...] = act.T
+
+    @pl.when(step < steps // 2)
+    def _():
+        grad_hidden_ref[...] = grad_hidden
+
+    @pl.when(step >= steps // 2)
+    def _():
+        grad_hidden_away_ref[...] = grad_hidden
+
+    sum_s[...] += jnp.dot(act, down_ref[...], preferred_element_type=full)
+    back_s[...] += lax.dot_general(grad_hidden, up_ref[...], across, preferred_element_type=full)
+
+    @pl.when(step == steps - 1)
+    def _():
+        result_ref[...] = (present * sum_s[...]).astype(low)
+        grad_middle = mixed_s[...].astype(full) + norm_back(
+            back_s[...], unit_s[...], inverse_s[...], gain_ref[...]
+        )
+        grad_middle_ref[...] = grad_middle
+        branch = grad_middle.astype(low)
+        by_core(branch, branch_ref, branch_away_ref)
+        grad_att = lax.dot_general(out_weight_ref[...], branch, across, preferred_element_type=full)
+        lane = (lax.broadcasted_iota(jnp.int32, (1, rows), 1) < valid).astype(full)
+        grad_att_ref[...] = (grad_att * lane).astype(low)
+
+
+def middle_part(core, valid, frames, att, cot, gain, w_out, w_up, w_down):
+    rows, features = frames.shape
+    hidden = w_up.shape[1]
+    wide = 512
+    steps = hidden // wide
+    here = lambda i, s: (i + s[0] * (steps // 2)) % steps
+    whole = lambda *shape: pl.BlockSpec(shape, lambda i, s: (0,) * len(shape))
+    square = (rows, features)
+    turned = (features, rows)
+    halved = (rows, features // 2)
+    outs = [
+        (square, low, None),
+        (square, full, None),
+        (halved, low, None),
+        (halved, low, None),
+        (turned, low, None),
+        (turned, low, None),
+        ((hidden, rows), low, pl.BlockSpec((wide, rows), lambda i, s: (here(i, s), 0))),
+        ((rows, hidden // 2), low, pl.BlockSpec((rows, wide), lambda i, s: (0, jnp.minimum(i, steps // 2 - 1)))),
+        ((rows, hidden // 2), low, pl.BlockSpec((rows, wide), lambda i, s: (0, jnp.maximum(i - steps // 2, 0)))),
+        (halved, low, None),
+        (halved, low, None),
+    ]
+    return pl.pallas_call(
+        middle_kernel,
+        grid_spec=pltpu.PrefetchScalarGridSpec(
+            num_scalar_prefetch=1,
+            grid=(steps,),
+            in_specs=[
+                whole(*square),
+                whole(*turned),
+                whole(*square),
+                whole(1, features),
+                whole(features, features),
+                pl.BlockSpec((features, wide), lambda i, s: (0, here(i, s))),
+                pl.BlockSpec((wide, features), lambda i, s: (here(i, s), 0)),
+            ],
+            out_specs=[spec or whole(*shape) for shape, _, spec in outs],
+            scratch_shapes=[
+                pltpu.VMEM(square, full),
+                pltpu.VMEM((rows, 1), full),
+                pltpu.VMEM(square, full),
+                pltpu.VMEM(square, full),
+                pltpu.VMEM(square, low),
+                pltpu.VMEM(square, low),
+            ],
+        ),
+        out_shape=[jax.ShapeDtypeStruct(shape, kind) for shape, kind, _ in outs],
+        compiler_params=pltpu.CompilerParams(vmem_limit_bytes=vmem_bytes),
+        cost_estimate=pl.CostEstimate(
+            flops=8 * rows * features * hidden + 4 * rows * features * features,
+            bytes_accessed=4 * features * hidden + 2 * features * features,
+            transcendentals=rows * hidden,
+        ),
+        name="middle",
+    )(jnp.stack([core, valid]), frames, att, cot, gain[None], w_out, w_up, w_down)
+
+
+def finish_kernel(frames_ref, middle_ref, gain_ref, rows_ref, query_ref, key_ref, value_ref, result_ref, back_s):
+    step = pl.program_id(0)
+    heads, _, rows = rows_ref.shape
+
+    @pl.when(step == 0)
+    def _():
+        back_s[...] = jnp.zeros_like(back_s)
+
+    total = back_s[...]
+    for part, weight_ref in enumerate((query_ref, key_ref, value_ref)):
+        grads = rows_ref[:, part * HEAD_DIM : (part + 1) * HEAD_DIM, :].reshape(heads * HEAD_DIM, rows)
+        total = total + jnp.dot(weight_ref[...], grads, preferred_element_type=full)
+    back_s[...] = total
+
+    @pl.when(step == pl.num_programs(0) - 1)
+    def _():
+        unit, inverse = norm_parts(frames_ref[...].astype(full))
+        result_ref[...] = middle_ref[...] + norm_back(back_s[...].T, unit, inverse, gain_ref[...])
+
+
+def finish(frames, grad_middle, gain, grad_rows, w_qkv):
+    rows, features = frames.shape
+    wide = 4 * HEAD_DIM
+    whole = lambda *shape: pl.BlockSpec(shape, lambda i: (0,) * len(shape))
+    return pl.pallas_call(
+        finish_kernel,
+        grid=(features // wide,),
+        out_shape=jax.ShapeDtypeStruct((rows, features), full),
+        in_specs=[
+            whole(rows, features),
+            whole(rows, features),
+            whole(1, features),
+            pl.BlockSpec((4, 3 * HEAD_DIM, rows), lambda i: (i, 0, 0)),
+        ]
+        + thirds(features, wide),
+        out_specs=whole(rows, features),
+        scratch_shapes=[pltpu.VMEM((features, rows), full)],
+        compiler_params=pltpu.CompilerParams(vmem_limit_bytes=vmem_bytes),
+        cost_estimate=pl.CostEstimate(
+            flops=6 * rows * features * features, bytes_accessed=8 * features * features, transcendentals=0
+        ),
+        name="input_gradient",
+    )(frames, grad_middle, gain[None], grad_rows, w_qkv, w_qkv, w_qkv)
+
+
+def terms_kernel(pick_ref, *refs, spans, needs, added):
+    step = pl.program_id(0)
+    refs = list(refs)
+    take = lambda count: [refs.pop(0) for _ in range(count)]
+    lefts = [{kind: take(2) for kind in kinds} for kinds in needs]
+    rights = [take(2) for _ in range(3)]
+    came = take(3) if added else [None] * 3
+    outs = [take(2) if added else take(1) for _ in range(3)]
+    for group, parts in enumerate(spans):
+        at = 0
+        for kind, start, stop in parts:
+            own_ref, other_ref = lefts[group][kind]
+            right_own_ref, right_other_ref = rights[kind]
+            rows, frames = own_ref.shape[-2:]
+            for block in range(start, stop) if kind == 2 else (None,):
+                if block is None:
+                    own, other = own_ref[...], other_ref[...]
+                    right_own, right_other = right_own_ref[:, start:stop], right_other_ref[:, start:stop]
+                else:
+                    own, other = own_ref[:, 0, :, 0, :, block], other_ref[:, 0, :, 0, :, block]
+                    right_own, right_other = right_own_ref[...], right_other_ref[...]
+                total = jnp.dot(own.reshape(-1, frames), right_own, preferred_element_type=full)
+                total = total + jnp.dot(other.reshape(-1, frames), right_other, preferred_element_type=full)
+                wide = total.shape[1]
+                total = total.reshape(-1, rows, wide)
+                if not added:
+                    outs[group][0][:, :, at : at + wide] = total.astype(low)
+                else:
+                    total = (total + came[group][:, :, at : at + wide].astype(full)).astype(low)
+
+                    @pl.when(step == 0)
+                    def _():
+                        outs[group][0][:, :, at : at + wide] = total
+
+                    @pl.when(step == 1)
+                    def _():
+                        outs[group][1][:, :, at : at + wide] = total
+                at += wide
+
+
+def terms_by_piece(spans, kept, bits, two, att, act, hidden, branch, mixed, came=None):
+    size = lax.axis_size("seq")
+    features, frames = two[0].shape
+    rows = features // size
+    blocks = act[0].shape[0] // features
+    wide = mixed[0].shape[1]
+    quarter = size // 4
+    widths = [sum((stop - start) * (wide if kind == 2 else 1) for kind, start, stop in parts) for parts in spans]
+    needs = [sorted({kind for kind, _, _ in parts}) for parts in spans]
+    lefts, specs = [], []
+    for group in range(3):
+        after = (group + 1) % 3
+        upper, lower = max(group, after), min(group, after)
+        cut = (size >> (upper + 1), 2, 1 << (upper - lower - 1), 2, 1 << lower)
+
+        def place(i, s, group=group, after=after, upper=upper):
+            value = s[group] if kept else 1 - s[group]
+            beyond = s[after] ^ (1 - i)
+            return (value, beyond) if upper == group else (beyond, value)
+
+        for kind in needs[group]:
+            extra = (blocks, rows, frames) if kind == 2 else (rows, frames)
+
+            def index(i, s, place=place, extra=extra):
+                first, second = place(i, s)
+                return (0, first, 0, second, 0) + (0,) * len(extra)
+
+            lefts += [a.reshape(cut + extra) for a in (two, att, act)[kind]]
+            specs += [pl.BlockSpec((cut[0], 1, cut[2], 1, cut[4]) + extra, index)] * 2
+    rights = (*hidden, *branch, *mixed)
+    specs += [pl.BlockSpec(a.shape, lambda i, s: (0, 0)) for a in rights]
+    half = lambda width: pl.BlockSpec((None, quarter, rows, width), lambda i, s: (i, 0, 0, 0))
+    if came is None:
+        outs = [half(width) for width in widths]
+        shapes = [jax.ShapeDtypeStruct((2, quarter, rows, width), low) for width in widths]
+    else:
+        specs += [half(width) for width in widths]
+        outs = [pl.BlockSpec((quarter, rows, width), lambda i, s: (0, 0, 0)) for width in widths for _ in range(2)]
+        shapes = [jax.ShapeDtypeStruct((quarter, rows, width), low) for width in widths for _ in range(2)]
+    return pl.pallas_call(
+        functools.partial(terms_kernel, spans=spans, needs=needs, added=came is not None),
+        grid_spec=pltpu.PrefetchScalarGridSpec(num_scalar_prefetch=1, grid=(2,), in_specs=specs, out_specs=outs),
+        out_shape=shapes,
+        compiler_params=pltpu.CompilerParams(vmem_limit_bytes=vmem_bytes),
+        cost_estimate=pl.CostEstimate(
+            flops=2 * frames * features * sum(widths), bytes_accessed=2 * features * sum(widths), transcendentals=0
+        ),
+        name="terms_by_piece",
+    )(jnp.stack(bits), *lefts, *rights, *(came or ()))
+
+
+def plane_terms_kernel(core_ref, rows_ref, low_ref, keep_ref, send_ref, sum_s, turn_s):
+    step = pl.program_id(0)
+    lines, columns, frames = rows_ref.shape
+
+    @pl.when(step == 0)
+    def _():
+        sum_s[...] = jnp.zeros_like(sum_s)
+
+    total = sum_s[...] + jnp.dot(
+        rows_ref[...].reshape(lines * columns, frames), low_ref[...], preferred_element_type=full
+    )
+    sum_s[...] = total
+
+    @pl.when(step == pl.num_programs(0) - 1)
+    def _():
+        turn_s[...] = total.T.reshape(turn_s.shape)
+        core = core_ref[0]
+        keep_ref[...] = turn_s[:, :, core].reshape(keep_ref.shape)
+        send_ref[...] = turn_s[:, :, 1 - core].astype(low).reshape(send_ref.shape)
+
+
+def plane_terms(core, line_rows, low_plane):
+    lines, count, columns, frames = line_rows.shape
+    features = low_plane.shape[-1]
+    rows = features // lines // count // 2
+    shape = (lines, count * rows, lines * columns)
+    whole = pl.BlockSpec(shape, lambda i: (0, 0, 0))
+    return pl.pallas_call(
+        plane_terms_kernel,
+        grid=(count,),
+        in_specs=[
+            pl.BlockSpec(memory_space=pltpu.SMEM),
+            pl.BlockSpec((lines, None, columns, frames), lambda i: (0, i, 0, 0)),
+            pl.BlockSpec((None, frames, features), lambda i: (i, 0, 0)),
+        ],
+        out_specs=[whole, whole],
+        out_shape=(jax.ShapeDtypeStruct(shape, full), jax.ShapeDtypeStruct(shape, low)),
+        scratch_shapes=[
+            pltpu.VMEM((lines * columns, features), full),
+            pltpu.VMEM((lines, count, 2, rows, lines * columns), full),
+        ],
+        compiler_params=pltpu.CompilerParams(vmem_limit_bytes=vmem_bytes),
+        cost_estimate=pl.CostEstimate(
+            flops=2 * lines * count * columns * frames * features, bytes_accessed=8 * line_rows.size, transcendentals=0
+        ),
+        name="plane_terms",
+    )(core[None], line_rows, low_plane)
+
+
 def other_core(array):
     count = lax.axis_size("items")
     return lax.ppermute(array, "items", [(i, i ^ 1) for i in range(count)])
 
 
 def to_heads(array):
-    size = lax.axis_size("seq")
-    copies = size // HEADS
+    copies = lax.axis_size("seq") // HEADS
     if copies > 1:
         array = jnp.repeat(array, copies, axis=0)
     return lax.all_to_all(array, "seq", 0, 0, tiled=True)
 
 
-def to_frames(array):
-    size = lax.axis_size("seq")
-    copies = size // HEADS
-    moved = lax.all_to_all(array, "seq", 0, 0, tiled=True)
-    if copies > 1:
-        moved = jnp.sum(moved.reshape((HEADS, copies) + moved.shape[1:]).astype(full), axis=1).astype(low)
-    return moved
-
-
-def half_columns(array, which):
-    width = array.shape[-1] // 2
-    return lax.dynamic_slice_in_dim(array, which * width, width, axis=-1)
+def by_head(array, axis):
+    copies = array.shape[axis] // HEADS
+    if copies == 1:
+        return array
+    shape = array.shape[:axis] + (HEADS, copies) + array.shape[axis + 1 :]
+    return jnp.sum(array.reshape(shape).astype(full), axis=axis + 1).astype(low)
 
 
 def pick(array, index, axis):
@@ -264,154 +621,137 @@
 
 
 def flipped(array, bit):
-    size = lax.axis_size("seq")
-    return lax.ppermute(array, "seq", [(i, i ^ bit) for i in range(size)])
-
-
-def line_sum(parts):
-    size = lax.axis_size("seq")
-    lines = size // 4
-    mine = lax.axis_index("seq") // 4
-    up = down = None
-    for step in range(1, lines):
-        up_send = pick(parts, jnp.minimum(mine + lines - step, lines - 1), 0)
-        down_send = pick(parts, jnp.maximum(mine - (lines - step), 0), 0)
-        if up is not None:
-            up_send = (up_send.astype(full) + up.astype(full)).astype(low)
-            down_send = (down_send.astype(full) + down.astype(full)).astype(low)
-        up = lax.ppermute(up_send, "seq", [(i, i + 4) for i in range(4 * step)])
-        down = lax.ppermute(down_send, "seq", [(i, i - 4) for i in range(size - 4 * step, size)])
-    total = pick(parts, mine, 0).astype(full)
-    return total + up.astype(full) + down.astype(full)
-
-
-def scatter_sum(make, first):
-    me = lax.axis_index("seq")
-    bits = (me % 2, (me // 2) % 2)
-    second = 1 - first
-    away = make(first, 1 - bits[first])
-    arrived = flipped(away, 1 << first)
-    kept = make(first, bits[first])
-    mine, theirs = bits[second], 1 - bits[second]
-    send = (pick(kept, theirs, 1).astype(full) + pick(arrived, theirs, 1).astype(full)).astype(low)
-    came = flipped(send, 1 << second)
-    total = (
-        pick(kept, mine, 1).astype(full) + pick(arrived, mine, 1).astype(full) + came.astype(full)
-    ).astype(low)
-    return line_sum(total)
-
-
-def term_maker(left, right, extra=None):
-    lines = lax.axis_size("seq") // 4
-    count, wide = left.shape
-    rows = wide // (4 * lines)
-    grid = left.reshape(count, lines, 2, 2, rows)
-
-    def make(bit, value):
-        chosen = pick(grid, value, 3 - bit)
-        terms = jnp.einsum("tzbr,tn->zbrn", chosen, right, preferred_element_type=full).astype(low)
-        if extra is not None:
-            terms = jnp.concatenate([terms, pick(extra, value, 2 - bit)], axis=2)
-        return terms
-
-    return make
-
-
-def gain_block(gain, columns):
-    lines = lax.axis_size("seq") // 4
-    rows = gain.shape[0] // (4 * lines)
-    block = gain.astype(low).reshape(lines, 2, 2, 1, rows)
-    return jnp.pad(block, ((0, 0), (0, 0), (0, 0), (0, GAIN_ROWS - 1), (0, columns - rows)))
+    return lax.ppermute(array, "seq", [(i, i ^ (1 << bit)) for i in range(lax.axis_size("seq"))])
+
+
+def split_terms(terms, bit, left):
+    axis = left.index(bit)
+    mine = (lax.axis_index("seq") >> bit) & 1
+    terms = [a.reshape((2,) * len(left) + a.shape[-2:]) for a in terms]
+
+    def part(value):
+        chosen = [pick(a, value, axis) for a in terms]
+        return chosen[0] if len(chosen) == 1 else (chosen[0].astype(full) + chosen[1].astype(full)).astype(low)
+
+    left.remove(bit)
+    return part(1 - mine), part(mine)
+
+
+def together(first, second):
+    return (first.astype(full) + second.astype(full)).astype(low)
 
 
 def over_items(piece):
     count = lax.axis_size("items")
-    pieces = lax.all_gather(piece.astype(low), "items", axis=0)
-    pieces = pieces.reshape((count // 2, 2) + piece.shape)
-    if count > 2:
-        return jnp.sum(pieces.astype(full), axis=0)
-    return pieces[0].astype(full)
-
-
-def side_by_side(halves):
-    return jnp.concatenate([halves[0], halves[1]], axis=-1)
+    if count == 2:
+        other = other_core(piece)
+        first = lax.axis_index("items") == 0
+        return jnp.stack([jnp.where(first, piece, other), jnp.where(first, other, piece)]).astype(full)
+    pieces = lax.all_gather(piece, "items", axis=0)
+    return jnp.sum(pieces.reshape((count // 2, 2) + piece.shape).astype(full), axis=0)
+
+
+def my_rows(array, rows):
+    return lax.dynamic_slice_in_dim(array, lax.axis_index("seq") * rows, rows, axis=0)
 
 
 def on_device(frames, lengths, w_qkv, w_out, w_up, w_down, gain_one, gain_two, cotangent):
-    row_count, feature_count = frames.shape[1:]
+    row_count, features = frames.shape[1:]
+    hidden_count = w_up.shape[1]
+    size = lax.axis_size("seq")
+    depth = size.bit_length() - 1
     me = lax.axis_index("seq")
     core = lax.axis_index("items") % 2
+    copies = size // HEADS
     ends = jnp.cumsum(lengths[0]).astype(jnp.int32)
-    places = me * row_count + jnp.arange(row_count, dtype=jnp.int32)
-    present = (places < ends[-1]).astype(full)[:, None]
-
-    inputs = frames[0].astype(full)
-    unit_one, inverse_one = norm_parts(inputs)
-    low_one = (unit_one * gain_one).astype(low)
-    packed = jnp.dot(low_one, w_qkv, preferred_element_type=full).astype(low)
-    by_head = packed.T.reshape(3, HEADS, HEAD_DIM, row_count).transpose(1, 0, 2, 3).reshape(HEADS, 3 * HEAD_DIM, row_count)
-    head_rows = to_heads(by_head)
-    copies = lax.axis_size("seq") // HEADS
+    valid = jnp.clip(ends[-1] - me * row_count, 0, row_count)
     control = jnp.concatenate([ends, (me % copies)[None]])
+    rows_out = features // size
+
+    head_parts, low_one = project(frames[0], gain_one, w_qkv)
+    head_rows = to_heads(head_parts)
+    lines = size // 4
+    fours = [list(range(at, at + 4)) for at in range(0, size, 4)]
+    columns = [list(range(at, size, 4)) for at in range(4)]
+    low_plane = lax.all_gather(low_one, "seq", axis=0, axis_index_groups=fours)
     head_out, log_mass = attn_fwd(control, head_rows, copies)
-    attended = to_frames(head_out).reshape(feature_count, row_count).T
-
-    middle = inputs + jnp.dot(attended, w_out, preferred_element_type=full)
-    unit_two, inverse_two = norm_parts(middle)
-    low_two = (unit_two * gain_two).astype(low)
-    hidden = jnp.dot(low_two, w_up, preferred_element_type=full)
-    activated, pull_gelu = jax.vjp(jax.nn.gelu, hidden)
-    act_low = activated.astype(low)
-    mixed = jnp.dot(act_low, w_down, preferred_element_type=full)
-    result = (present * (middle + mixed)).astype(low)
-    grad_mixed = cotangent[0].astype(full) * present
-    grad_mixed_low = grad_mixed.astype(low)
-    grad_act = jnp.einsum("td,fd->tf", grad_mixed_low, w_down, preferred_element_type=full)
-    grad_hidden = pull_gelu(grad_act)[0].astype(low)
-    grad_normed_two = jnp.einsum("tf,df->td", grad_hidden, w_up, preferred_element_type=full)
-    grad_gain_two = jnp.sum(grad_normed_two * unit_two, axis=0)
-    grad_middle = grad_mixed + norm_back(grad_normed_two, unit_two, inverse_two, gain_two)
-    grad_branch = grad_middle.astype(low)
-    grad_attended = jnp.einsum("te,de->dt", grad_branch, w_out, preferred_element_type=full).astype(low)
-    grad_attended = grad_attended * present[:, 0].astype(low)[None]
+    head_out, low_plane = lax.optimization_barrier((head_out, low_plane))
+    moved = lax.all_to_all(head_out, "seq", 0, 0, tiled=True)
+    attended = by_head(moved, 0).reshape(features, row_count)
+    att = (attended, other_core(attended))
+
+    result, grad_middle, branch, branch_away, grad_attended, two, act, hidden, hidden_away, mixed, mixed_away = (
+        middle_part(core, valid, frames[0], attended, cotangent[0], gain_two, w_out, w_up, w_down)
+    )
     grad_heads = to_heads(grad_attended.reshape(HEADS, HEAD_DIM, row_count))
 
-    def both(left, right):
-        lefts = jnp.concatenate([left, other_core(left)], axis=0)
-        rights = jnp.concatenate(
-            [half_columns(right, core), other_core(half_columns(right, 1 - core))], axis=0
-        )
-        return lefts, rights
-
-    sum_down = scatter_sum(term_maker(*both(act_low, grad_mixed_low)), 1)
-    sum_up = scatter_sum(term_maker(*both(low_two, grad_hidden)), 0)
-    extra = gain_block(grad_gain_two, feature_count // 2)
-    sum_out = scatter_sum(term_maker(*both(attended, grad_branch), extra), 0)
+    pairs = (
+        (two, other_core(two)),
+        att,
+        (act, other_core(act)),
+        (hidden, other_core(hidden_away)),
+        (branch, other_core(branch_away)),
+        (mixed, other_core(mixed_away)),
+    )
+    half = features // 2
+    split = hidden_count // 2
+    third = (split + half) * 3 // 5
+    spans = (
+        ((0, 0, third),),
+        ((0, third, split), (1, 0, half), (2, 0, 1)),
+        ((2, 1, hidden_count // features),),
+    )
+    bits = [(me >> bit) & 1 for bit in range(3)]
+    came = terms_by_piece(spans, False, bits, *pairs)
+    came = [flipped(a, bit) for bit, a in enumerate(came)]
 
     grad_rows = attn_bwd(control, head_rows, grad_heads, head_out, log_mass, copies)
-    grad_packed = to_frames(grad_rows)
-    grad_packed = (
-        grad_packed.reshape(HEADS, 3, HEAD_DIM, row_count).transpose(3, 1, 0, 2).reshape(row_count, 3 * feature_count)
-    )
-    lefts, rights = both(low_one, grad_packed)
-    split = rights.shape[1] // 2
-    grad_normed_one = jnp.einsum("te,de->td", grad_packed, w_qkv, preferred_element_type=full)
-    grad_gain_one = jnp.sum(grad_normed_one * unit_one, axis=0)
-    sum_qkv_a = scatter_sum(term_maker(lefts, rights[:, :split]), 0)
-    extra = gain_block(grad_gain_one, rights.shape[1] - split)
-    sum_qkv_b = scatter_sum(term_maker(lefts, rights[:, split:], extra), 1)
-    grad_inputs = grad_middle + norm_back(grad_normed_one, unit_one, inverse_one, gain_one)
-
-    rows_out = sum_up.shape[0]
-    out_halves = over_items(sum_out)
-    up = side_by_side(over_items(sum_up))
-    down = side_by_side(over_items(sum_down))
-    out = side_by_side(out_halves[:, :rows_out])
-    b_halves = over_items(sum_qkv_b)
-    a_halves = over_items(sum_qkv_a)
-    qkv = side_by_side(jnp.concatenate([a_halves, b_halves[:, :rows_out]], axis=-1))
-    sum_gain_two = jnp.sum(out_halves[:, rows_out, :rows_out], axis=0)
-    sum_gain_one = jnp.sum(b_halves[:, rows_out, :rows_out], axis=0)
+    grad_rows, *came = lax.optimization_barrier((grad_rows, *came))
+    across = lambda array, groups: lax.all_to_all(array, "seq", 0, 0, tiled=True, axis_index_groups=groups)
+    line_rows = across(grad_rows.reshape(lines, 4, 3 * HEAD_DIM, row_count), columns)
+
+    parts = terms_by_piece(spans, True, bits, *pairs, came=came)
+    came = [flipped(parts[2 * g], (g + 1) % 3) for g in range(3)]
+    left = [[bit for bit in range(depth - 1, -1, -1) if bit not in (g, (g + 1) % 3)] for g in range(3)]
+    line_rows, *came = lax.optimization_barrier((line_rows, *came))
+    terms = [(parts[2 * g + 1], came[g]) for g in range(3)]
+
+    def halve(terms, turn):
+        sent = []
+        for g in range(3):
+            bit = (g + turn) % 3 if turn < 3 else turn
+            send, keep = split_terms(terms[g], bit, left[g])
+            sent.append((keep, flipped(send, bit)))
+        return sent
+
+    terms = halve(terms, 2)
+    grad_packed = across(line_rows.transpose(1, 0, 2, 3), fours)
+    keep, send = plane_terms(core, line_rows, low_plane)
+    both = (keep + other_core(send).astype(full)).astype(low)
+    both, *came = lax.optimization_barrier((both, *[came for _, came in terms]))
+    terms = [(kept, came[g]) for g, (kept, _) in enumerate(terms)]
+    for turn in range(3, depth):
+        terms = halve(terms, turn)
+
+    pieces = lax.all_to_all(both.reshape(size, rows_out // 2, lines * 3 * HEAD_DIM), "seq", 0, 0, tiled=True)
+    grad_packed = by_head(grad_packed.transpose(1, 0, 2, 3).reshape(size, 3 * HEAD_DIM, row_count), 0)
+    grad_inputs = finish(frames[0], grad_middle, gain_one, grad_packed, w_qkv)
+    grad_inputs, pieces, *came = lax.optimization_barrier((grad_inputs, pieces, *[came for _, came in terms]))
+    terms = [(kept, came[g]) for g, (kept, _) in enumerate(terms)]
+    sums = jnp.concatenate([together(*pair) for pair in terms], axis=-1)
+
+    pieces = jnp.sum(pieces.reshape((lines, 4) + pieces.shape[1:]).astype(full), axis=0).astype(low)
+    pieces = pieces.reshape(4, rows_out // 2, lines, 3, HEAD_DIM).transpose(1, 3, 2, 0, 4)
+    pieces = by_head(pieces.reshape(rows_out // 2, 3, size, HEAD_DIM), 2)
+    qkv = over_items(pieces.reshape(rows_out // 2, 3 * features)).reshape(rows_out, 3 * features)
+    sums = over_items(sums)
+    side = lambda start, stop: jnp.concatenate([sums[0, :, start:stop], sums[1, :, start:stop]], axis=-1)
+    up = side(0, split)
+    out = side(split, split + half)
+    start = split + half
+    down = jnp.concatenate([side(at, at + half) for at in range(start, start + split, half)], axis=0)
+    sum_gain_one = jnp.sum(my_rows(w_qkv, rows_out).astype(full) * qkv, axis=1) / my_rows(gain_one, rows_out)
+    sum_gain_two = jnp.sum(my_rows(w_up, rows_out).astype(full) * up, axis=1) / my_rows(gain_two, rows_out)
     return (result[None], grad_inputs[None], qkv, out, up, down, sum_gain_one, sum_gain_two)
 
 

time: 475 us -> 332 us (0.70); the launches traced: 467 us -> 331 us
  matrix products: 66.4 us -> 0 us
  Pallas kernels: 51.9 us -> 114 us
  starting transfers between devices: 106 us -> 54.3 us
  waiting for transfers between devices: 152 us -> 115 us
  local copies, waits for them, and re-layouts: 39.3 us -> 11.1 us
  other arithmetic: 38.6 us -> 21.4 us
  between operations: 2.26 us -> 15.1 us
  blocking collectives: 10.2 us -> 0 us
    dot_general x18 -> x0, matrix products: 66.4 us -> none  [the longest x10 24.5 us: make(): jnp.einsum('tzbr,tn->zbrn', chosen, right, preferred_element_type=full)]
    pallas_call x0 -> x6, Pallas kernels: none -> 62.3 us  [the longest x1 22.2 us: middle_part(): pl.pallas_call(middle_kernel, grid_spec=pltpu.PrefetchScalarGridSpec(num_...]
    ppermute x40 -> x12, starting transfers between devices: 79.4 us -> 18.3 us  [flipped(): lax.ppermute(array, 'seq', [(i, i ^ 1 << bit) for i in range(lax.axis_siz...]
    ppermute x40 -> x12, waiting for transfers between devices: 117 us -> 66.6 us  [flipped(): lax.ppermute(array, 'seq', [(i, i ^ 1 << bit) for i in range(lax.axis_siz...]
    dynamic_slice x12 -> x0, local copies, waits for them, and re-layouts: 15.2 us -> none  [the longest x8 10.7 us: pick(): return lax.dynamic_index_in_dim(array, index, axis, keepdims=False)]
    all_gather x5 -> x0, blocking collectives: 10.2 us -> none  [over_items(): pieces = lax.all_gather(piece.astype(low), 'items', axis=0)]
    concatenate x10 -> x3, other arithmetic: 11.7 us -> 1.82 us  [the longest x1 1.06 us: on_device(): jnp.concatenate([side(at, at + half) for at in range(start, start + split...]
    all_to_all x2 -> x4, waiting for transfers between devices: 2.63 us -> 12.4 us  [the longest x1 12.4 us: on_device(): moved = lax.all_to_all(head_out, 'seq', 0, 0, tiled=True)]
  transfers between devices with their start and end apart: 52 -> 28, of which waited for: 16 -> 12; matrix products, arithmetic and copies ran while one was open for 27% -> 5% of each run, Pallas kernels for 11% -> 26%
where the time goes in v2:
time: 332 us; the launch traced here: 331 us
  waiting for transfers between devices  115 us (35%)
  Pallas kernels  114 us (34%)
  starting transfers between devices  54.3 us (16%)
  other arithmetic  21.4 us (6%)
  between operations  15.1 us (5%)
  local copies, waits for them, and re-layouts  11.1 us (3%)
    ppermute x12, waiting for transfers between devices, flipped(): lax.ppermute(array, 'seq', [(i, i ^ 1 << bit) for i in range(lax.axis_siz...  66.6 us
    pallas_call x1, Pallas kernels, attn_bwd(): pl.pallas_call(functools.partial(backward_kernel, block=block_of(total, c...  33.9 us
    all_to_all x2, waiting for transfers between devices, to_heads(): return lax.all_to_all(array, 'seq', 0, 0, tiled=True)  32.6 us
    pallas_call x1, Pallas kernels, middle_part(): pl.pallas_call(middle_kernel, grid_spec=pltpu.PrefetchScalarGridSpec(num_...  22.2 us
    pallas_call x2, Pallas kernels, terms_by_piece(): pl.pallas_call(functools.partial(terms_kernel, spans=spans, needs=needs,...  19.2 us
    ppermute x12, starting transfers between devices, flipped(): lax.ppermute(array, 'seq', [(i, i ^ 1 << bit) for i in range(lax.axis_siz...  18.3 us
    pallas_call x1, Pallas kernels, attn_fwd(): pl.pallas_call(functools.partial(forward_kernel, block=block_of(total, co...  18.1 us
    all_to_all x2, starting transfers between devices, to_heads(): return lax.all_to_all(array, 'seq', 0, 0, tiled=True)  12.9 us
  transfers between devices with their start and end apart: 28, of which 12 were waited for; matrix products, arithmetic and copies ran while one was open for 5% of the time, Pallas kernels for 26%

profile of v2, /device:TPU:0, one launch (start us, length us, event | category | flops | bytes accessed | tf_op | source)
XLA Modules:
  0.0 331.0 jit_solution(7045069407273087362)
XLA Ops:
  7.2 6.5 %norm_and_project.1 = (bf16[16,192,256]{2,1,0:T(8,128)(2,1)}, bf16[256,1024]{1,0:T(8,128)(2,1)}) custom-call(bf16[256,1024]{1,0:T(8,128)(2,1)} %bitcast.148, f32[1,1024]{1,0:T(1,128)} %bitcast.159, bf16[1024,3072]{1,0:T(8,128)(2,1)} %value_ref.3, bf16[1024,3072]{1,0:T(8,128)(2,1)} %value_ref.3, bf16[1024,3072]{1,0:T(8,128)(2,1)} %value_ref.3), custom_call_target="tpu_custom_call" | custom-call | flops 1610612736 | bytes 8388608 | tf_op jit(solution)/shard_map/norm_and_project/pallas_call | solution.py:257
  13.7 8.4 %all-to-all-start = ((bf16[16,192,256]{2,1,0:T(8,128)(2,1)}), bf16[16,192,256]{2,1,0:T(8,128)(2,1)S(1)}, u32[]{:S(2)}, u32[]{:S(2)}) async-start(bf16[16,192,256]{2,1,0:T(8,128)(2,1)} %get-tuple-element.53), calls=%async_computation | async-start | bytes 3145728 | tf_op jit(solution)/shard_map/all_to_all | solution.py:608
  22.2 0.7 all-gather.3.cloned.1.call-update
  23.0 0.7 pad_add_fusion.1.ends_ref
  23.7 32.6 %all-to-all-done.rows_ref = bf16[16,192,256]{2,1,0:T(8,128)(2,1)S(1)} async-done(((bf16[16,192,256]{2,1,0:T(8,128)(2,1)}), bf16[16,192,256]{2,1,0:T(8,128)(2,1)S(1)}, u32[]{:S(2)}, u32[]{:S(2)}) %all-to-all-start) | async-done | bytes 1572896 | tf_op jit(solution)/shard_map/all_to_all | solution.py:608
  56.3 1.2 copy-done.5
  57.5 18.1 %attention_forward.1 = (bf16[16,64,256]{2,1,0:T(8,128)(2,1)}, f32[1,4096]{1,0:T(1,128)}) custom-call(s32[4]{0:T(128)} %pad_add_fusion.1.ends_ref, bf16[16,192,256]{2,1,0:T(8,128)(2,1)} %copy-done.5), custom_call_target="tpu_custom_call" | custom-call | flops 21474836480 | bytes 3145728 | tf_op jit(solution)/shard_map/attention_forward/pallas_call | solution.py:101
  75.6 7.9 %all-to-all-start.1 = ((bf16[16,64,256]{2,1,0:T(8,128)(2,1)}), bf16[16,64,256]{2,1,0:T(8,128)(2,1)S(1)}, u32[]{:S(2)}, u32[]{:S(2)}) async-start(bf16[16,64,256]{2,1,0:T(8,128)(2,1)} %get-tuple-element.56.out_ref), calls=%async_computation.1 | async-start | bytes 1048576 | tf_op jit(solution)/shard_map/all_to_all | solution.py:679
  83.5 0.6 slice.40
  84.8 0.6 pad_add_fusion.control_ref
  85.4 12.4 %all-to-all-done.1 = bf16[16,64,256]{2,1,0:T(8,128)(2,1)S(1)} async-done(((bf16[16,64,256]{2,1,0:T(8,128)(2,1)}), bf16[16,64,256]{2,1,0:T(8,128)(2,1)S(1)}, u32[]{:S(2)}, u32[]{:S(2)}) %all-to-all-start.1) | async-done | bytes 524320 | tf_op jit(solution)/shard_map/all_to_all | solution.py:679
  97.8 0.8 copy-done.3
  98.6 22.2 %middle.1 = (bf16[256,1024]{1,0:T(8,128)(2,1)}, f32[256,1024]{1,0:T(8,128)}, bf16[256,512]{1,0:T(8,128)(2,1)}, bf16[256,512]{1,0:T(8,128)(2,1)}, bf16[1024,256]{...) custom-call(s32[2]{0:T(128)} %pad_add_fusion.control_ref, ...), custom_call_target="tpu_custom_call" | custom-call | flops 9663676416 | bytes 18874368 | tf_op jit(solution)/shard_map/middle/pallas_call | solution.py:379
  121.4 4.4 %all-to-all-start.2 = ((bf16[16,64,256]{2,1,0:T(8,128)(2,1)}), bf16[16,64,256]{2,1,0:T(8,128)(2,1)}, u32[]{:S(2)}, u32[]{:S(2)}) async-start(bf16[16,64,256]{2,1,0:T(8,128)(2,1)} %bitcast.158), calls=%async_computation.2 | async-start | bytes 1048576 | tf_op jit(solution)/shard_map/all_to_all | solution.py:608
  126.4 1.2 collective-permute-done.4.refs_13_
  127.7 0.6 pad_add_fusion.2.pick_ref
  128.3 1.3 collective-permute-done.5.refs_15_
  129.7 0.7 copy-done.1
  130.6 0.7 copy-done
  131.3 7.4 %terms_by_piece.2 = (bf16[2,4,64,1536]{3,2,1,0:T(8,128)(2,1)}, bf16[2,4,64,1536]{3,2,1,0:T(8,128)(2,1)}, bf16[2,4,64,1536]{3,2,1,0:T(8,128)(2,1)}) custom-call(s32[3]{0:T(128)} %pad_add_fusion.2.pick_ref, bf16[4,2,1,2,1,64,256]{6,5,4,3,2,1,0:T(8,128)(2,1)} %bitcast.129, bf16[4,2,1,2,1,64,256]{6,5,4,3,2,1,0:T(8,128)(2,1)} %bitcast.133, ...), custom_call_target="tpu_custom_call" | custom-call | flops 2415919104 | bytes 9437184 | tf_op jit(solution)/shard_map/terms_by_piece/pallas_call | solution.py:538
  138.7 1.6 collective-permute-start.6
  140.4 1.5 collective-permute-start.7
  141.8 1.5 collective-permute-start.8
  143.3 33.9 %attention_backward.1 = bf16[16,192,256]{2,1,0:T(8,128)(2,1)} custom-call(s32[4]{0:T(128)} %pad_add_fusion.1.ends_ref, bf16[16,192,256]{2,1,0:T(8,128)(2,1)} %copy-done.5, bf16[16,64,256]{2,1,0:T(8,128)(2,1)} %all-to-all-done.2.grad_ref, bf16[16,64,256]{2,1,0:T(8,128)(2,1)} %get-tuple-element.56.out_ref, f32[1,4096]{1,0:T(1,128)} %get-tuple-element.60.mass_ref), custom_call_target="tpu_custom_call" | custom-call | flops 37580963840 | bytes 6291456 | tf_op jit(solution)/shard_map/attention_backward/pallas_call | solution.py:199
  177.3 0.8 collective-permute-done.8.refs_18_
  178.9 3.7 %all-to-all-start.3 = ((bf16[4,4,192,256]{3,2,1,0:T(8,128)(2,1)}), bf16[4,4,192,256]{3,2,1,0:T(8,128)(2,1)S(1)}, u32[]{:S(2)}, u32[]{:S(2)}) async-start(bf16[4,4,192,256]{3,2,1,0:T(8,128)(2,1)} %bitcast.151), calls=%async_computation.3 | async-start | bytes 3145728 | tf_op jit(solution)/shard_map/all_to_all | solution.py:710
  182.6 11.8 %terms_by_piece.3 = (bf16[4,64,1536]{2,1,0:T(8,128)(2,1)}, bf16[4,64,1536]{2,1,0:T(8,128)(2,1)}, bf16[4,64,1536]{2,1,0:T(8,128)(2,1)}, bf16[4,64,1536]{2,1,0:T(8...) custom-call(s32[3]{0:T(128)} %pad_add_fusion.2.pick_ref, ...), custom_call_target="tpu_custom_call" | custom-call | flops 2415919104 | bytes 9437184 | tf_op jit(solution)/shard_map/terms_by_piece/pallas_call | solution.py:538
  194.4 1.5 collective-permute-start.9
  195.9 2.0 collective-permute-start.10
  197.9 0.8 collective-permute-start.11
  198.7 14.7 %collective-permute-done.9 = bf16[4,64,1536]{2,1,0:T(8,128)(2,1)} collective-permute-done((bf16[4,64,1536]{2,1,0:T(8,128)(2,1)}, bf16[4,64,1536]{2,1,0:T(8,128)(2,1)}, u32[]{:S(2)}, u32[]{:S(2)}) %collective-permute-start.9) | collective-permute-done | bytes 786464 | tf_op jit(solution)/shard_map/ppermute | solution.py:624
  213.4 13.3 %collective-permute-done.10 = bf16[4,64,1536]{2,1,0:T(8,128)(2,1)S(1)} collective-permute-done((bf16[4,64,1536]{2,1,0:T(8,128)(2,1)}, bf16[4,64,1536]{2,1,0:T(8,128)(2,1)S(1)}, u32[]{:S(2)}, u32[]{:S(2)}) %collective-permute-start.10) | collective-permute-done | bytes 786464 | tf_op jit(solution)/shard_map/ppermute | solution.py:624
  226.7 1.4 copy.18
  228.3 0.5 copy-done.2
  228.8 3.8 %all-to-all-start.4 = ((bf16[4,4,192,256]{3,2,1,0:T(8,128)(2,1)}), bf16[4,4,192,256]{3,2,1,0:T(8,128)(2,1)S(1)}, u32[]{:S(2)}, u32[]{:S(2)}) async-start(bf16[4,4,192,256]{3,2,1,0:T(8,128)(2,1)} %copy.18), calls=%async_computation.4 | async-start | bytes 3145728 | tf_op jit(solution)/shard_map/all_to_all | solution.py:710
  232.6 6.8 %plane_terms.1 = (f32[4,128,768]{2,1,0:T(8,128)}, bf16[4,128,768]{2,1,0:T(8,128)(2,1)}) custom-call(s32[1]{0:T(128)} %bitcast.core_ref, bf16[4,4,192,256]{3,2,1,0:T(8,128)(2,1)} %copy-done.2, bf16[4,256,1024]{2,1,0:T(8,128)(2,1)} %bitcast.162), custom_call_target="tpu_custom_call" | custom-call | flops 1610612736 | bytes 6291456 | tf_op jit(solution)/shard_map/plane_terms/pallas_call | solution.py:577
  239.5 1.4 add_convert_fusion.3
  241.6 1.8 collective-permute-start.14
  243.6 1.5 collective-permute-start.15
  245.1 1.1 add_convert_fusion
  246.2 6.2 %collective-permute-done.13 = bf16[2,64,1536]{2,1,0:T(8,128)(2,1)S(1)} collective-permute-done((bf16[2,64,1536]{2,1,0:T(8,128)(2,1)S(1)}, bf16[2,64,1536]{2,1,0:T(8,128)(2,1)S(1)}, u32[]{:S(2)}, u32[]{:S(2)}) %collective-permute-start.13) | collective-permute-done | bytes 393248 | tf_op jit(solution)/shard_map/ppermute | solution.py:624
  252.4 6.3 %collective-permute-done.14 = bf16[2,64,1536]{2,1,0:T(8,128)(2,1)S(1)} collective-permute-done((bf16[2,64,1536]{2,1,0:T(8,128)(2,1)S(1)}, bf16[2,64,1536]{2,1,0:T(8,128)(2,1)S(1)}, u32[]{:S(2)}, u32[]{:S(2)}) %collective-permute-start.14) | collective-permute-done | bytes 393248 | tf_op jit(solution)/shard_map/ppermute | solution.py:624
  258.7 0.7 copy-done.19
  259.4 0.7 copy-done.21
  260.2 5.6 %all-to-all-start.5 = ((bf16[16,32,768]{2,1,0:T(8,128)(2,1)}), bf16[16,32,768]{2,1,0:T(8,128)(2,1)S(1)}, u32[]{:S(2)}, u32[]{:S(2)}) async-start(bf16[16,32,768]{2,1,0:T(8,128)(2,1)} %bitcast.39), calls=%async_computation.5 | async-start | bytes 1572864 | tf_op jit(solution)/shard_map/all_to_all | solution.py:736
  265.8 1.6 fusion.12
  267.5 2.8 collective-permute-start.16
  270.3 1.6 fusion.13
  272.0 1.6 fusion.14
  273.7 2.8 collective-permute-start.18
  276.5 1.3 copy.19
  277.8 7.5 %input_gradient.1 = f32[256,1024]{1,0:T(8,128)} custom-call(bf16[256,1024]{1,0:T(8,128)(2,1)} %bitcast.150, f32[256,1024]{1,0:T(8,128)} %get-tuple-element.58.middle_ref, f32[1,1024]{1,0:T(1,128)} %bitcast.160, bf16[16,192,256]{2,1,0:T(8,128)(2,1)} %bitcast.139, bf16[1024,3072]{1,0:T(8,128)(2,1)} %value_ref.3, bf16[1024,3072]{1,0:T(8,128)(2,1)} %value_ref.3, ...), custom_call_target="tpu_custom_call" | custom-call | flops 1610612736 | bytes 8388608 | tf_op jit(solution)/shard_map/input_gradient/pallas_call | solution.py:438
  285.4 18.0 %collective-permute-done.16 = bf16[64,1536]{1,0:T(8,128)(2,1)} collective-permute-done((bf16[64,1536]{1,0:T(8,128)(2,1)}, bf16[64,1536]{1,0:T(8,128)(2,1)}, u32[]{:S(2)}, u32[]{:S(2)}) %collective-permute-start.16) | collective-permute-done | bytes 196640 | tf_op jit(solution)/shard_map/ppermute | solution.py:624
  303.3 4.2 %collective-permute-done.17 = bf16[64,1536]{1,0:T(8,128)(2,1)} collective-permute-done((bf16[64,1536]{1,0:T(8,128)(2,1)}, bf16[64,1536]{1,0:T(8,128)(2,1)}, u32[]{:S(2)}, u32[]{:S(2)}) %collective-permute-start.17) | collective-permute-done | bytes 196640 | tf_op jit(solution)/shard_map/ppermute | solution.py:624
  307.5 3.1 collective-permute-done.18
  311.9 1.0 fusion.7
  313.0 1.2 fusion.3
  314.2 0.5 collective-permute-start.20
  314.8 2.1 multiply_reduce_fusion.1
  316.9 1.3 dynamic-slice_divide_fusion.1
  318.8 2.2 multiply_reduce_fusion
  321.0 1.3 dynamic-slice_divide_fusion
  322.3 0.7 pad_maximum_fusion.3
  323.0 1.1 maximum_maximum_fusion
  (83 shorter events, 5.7 us)
Async XLA Ops:
  13.7 9.2 %copy-start.23 = (s32[1,3]{1,0:T(1,128)S(1)}, s32[1,3]{1,0:T(1,128)}, u32[]{:S(2)}) copy-start(s32[1,3]{1,0:T(1,128)} %param.10) | copy-start | bytes 40
  13.7 42.6 %all-to-all-start = ((bf16[16,192,256]{2,1,0:T(8,128)(2,1)}), bf16[16,192,256]{2,1,0:T(8,128)(2,1)S(1)}, u32[]{:S(2)}, u32[]{:S(2)}) async-start(bf16[16,192,256]{2,1,0:T(8,128)(2,1)} %get-tuple-element.53), calls=%async_computation | async-start | bytes 3145728 | tf_op jit(solution)/shard_map/all_to_all | solution.py:608
  22.1 53.5 %all-gather.3.cloned.1.call-start = ((), (), s32[]{:S(2)}) async-start(), calls=%async_computation.6 | async-start | bytes 2621440 | tf_op jit(solution)/shard_map/all_gather | solution.py:676
  56.3 1.2 copy-start.5
  75.6 22.2 %all-to-all-start.1 = ((bf16[16,64,256]{2,1,0:T(8,128)(2,1)}), bf16[16,64,256]{2,1,0:T(8,128)(2,1)S(1)}, u32[]{:S(2)}, u32[]{:S(2)}) async-start(bf16[16,64,256]{2,1,0:T(8,128)(2,1)} %get-tuple-element.56.out_ref), calls=%async_computation.1 | async-start | bytes 1048576 | tf_op jit(solution)/shard_map/all_to_all | solution.py:679
  97.8 0.8 copy-start.3
  120.8 8.9 %collective-permute-start.2 = (bf16[4096,256]{1,0:T(8,128)(2,1)}, bf16[4096,256]{1,0:T(8,128)(2,1)S(1)}, u32[]{:S(2)}, u32[]{:S(2)}) collective-permute-start(bf16[4096,256]{1,0:T(8,128)(2,1)} %get-tuple-element.62), channel_id=1, source_target_pairs={{0,16},{16,0},{1,17},{17,1},{2,18},{18,2},{3,19},{19,3},{4,20},{20... | collective-permute-start | bytes 6291464 | tf_op jit(solution)/shard_map/ppermute | solution.py:601
  120.9 8.8 %collective-permute-start.3 = (bf16[256,2048]{1,0:T(8,128)(2,1)}, bf16[256,2048]{1,0:T(8,128)(2,1)}, u32[]{:S(2)}, u32[]{:S(2)}) collective-permute-start(bf16[256,2048]{1,0:T(8,128)(2,1)} %get-tuple-element.64), channel_id=1, source_target_pairs={{0,16},{16,0},{1,17},{17,1},{2,18},{18,2},{3,19},{19,3},{4,20},{20... | collective-permute-start | bytes 3145736 | tf_op jit(solution)/shard_map/ppermute | solution.py:601
  121.4 22.0 %all-to-all-start.2 = ((bf16[16,64,256]{2,1,0:T(8,128)(2,1)}), bf16[16,64,256]{2,1,0:T(8,128)(2,1)}, u32[]{:S(2)}, u32[]{:S(2)}) async-start(bf16[16,64,256]{2,1,0:T(8,128)(2,1)} %bitcast.158), calls=%async_computation.2 | async-start | bytes 1048576 | tf_op jit(solution)/shard_map/all_to_all | solution.py:608
  125.8 1.8 collective-permute-start.4
  125.9 3.7 %collective-permute-start = (bf16[1024,256]{1,0:T(8,128)(2,1)}, bf16[1024,256]{1,0:T(8,128)(2,1)S(1)}, u32[]{:S(2)}, u32[]{:S(2)}) collective-permute-start(bf16[1024,256]{1,0:T(8,128)(2,1)} %get-tuple-element.61), channel_id=1, source_target_pairs={{0,16},{16,0},{1,17},{17,1},{2,18},{18,2},{3,19},{19,3},{4,20},{20... | collective-permute-start | bytes 1572872 | tf_op jit(solution)/shard_map/ppermute | solution.py:601
  126.4 3.2 collective-permute-start.1
  127.6 2.1 copy-start.9
  127.6 2.0 collective-permute-start.5
  129.6 0.8 copy-start.1
  129.6 1.0 copy-start.4
  129.6 1.6 copy-start
  138.7 38.5 %collective-permute-start.6 = (bf16[2,4,64,1536]{3,2,1,0:T(8,128)(2,1)}, bf16[2,4,64,1536]{3,2,1,0:T(8,128)(2,1)S(1)}, u32[]{:S(2)}, u32[]{:S(2)}) collective-permute-start(bf16[2,4,64,1536]{3,2,1,0:T(8,128)(2,1)} %get-tuple-element.69), channel_id=1, source_target_pairs={{0,1},{1,0},{2,3},{3,2},{4,5},{5,4},{6,7},{7,6},{8,9},{9,8},{10,11... | collective-permute-start | bytes 4718600 | tf_op jit(solution)/shard_map/ppermute | solution.py:624
  140.4 36.9 %collective-permute-start.7 = (bf16[2,4,64,1536]{3,2,1,0:T(8,128)(2,1)}, bf16[2,4,64,1536]{3,2,1,0:T(8,128)(2,1)S(1)}, u32[]{:S(2)}, u32[]{:S(2)}) collective-permute-start(bf16[2,4,64,1536]{3,2,1,0:T(8,128)(2,1)} %get-tuple-element.70), channel_id=1, source_target_pairs={{0,2},{1,3},{2,0},{3,1},{4,6},{5,7},{6,4},{7,5},{8,10},{9,11},{10,... | collective-permute-start | bytes 4718600 | tf_op jit(solution)/shard_map/ppermute | solution.py:624
  141.8 36.2 %collective-permute-start.8 = (bf16[2,4,64,1536]{3,2,1,0:T(8,128)(2,1)}, bf16[2,4,64,1536]{3,2,1,0:T(8,128)(2,1)}, u32[]{:S(2)}, u32[]{:S(2)}) collective-permute-start(bf16[2,4,64,1536]{3,2,1,0:T(8,128)(2,1)} %get-tuple-element.71), channel_id=1, source_target_pairs={{0,4},{1,5},{2,6},{3,7},{4,0},{5,1},{6,2},{7,3},{8,12},{9,13},{10,... | collective-permute-start | bytes 4718600 | tf_op jit(solution)/shard_map/ppermute | solution.py:624
  177.2 1.7 copy-start.7
  177.2 1.2 copy-start.8
  178.9 47.8 %all-to-all-start.3 = ((bf16[4,4,192,256]{3,2,1,0:T(8,128)(2,1)}), bf16[4,4,192,256]{3,2,1,0:T(8,128)(2,1)S(1)}, u32[]{:S(2)}, u32[]{:S(2)}) async-start(bf16[4,4,192,256]{3,2,1,0:T(8,128)(2,1)} %bitcast.151), calls=%async_computation.3 | async-start | bytes 3145728 | tf_op jit(solution)/shard_map/all_to_all | solution.py:710
  194.4 19.0 %collective-permute-start.9 = (bf16[4,64,1536]{2,1,0:T(8,128)(2,1)}, bf16[4,64,1536]{2,1,0:T(8,128)(2,1)}, u32[]{:S(2)}, u32[]{:S(2)}) collective-permute-start(bf16[4,64,1536]{2,1,0:T(8,128)(2,1)} %get-tuple-element.76), channel_id=1, source_target_pairs={{0,2},{1,3},{2,0},{3,1},{4,6},{5,7},{6,4},{7,5},{8,10},{9,11},{10,... | collective-permute-start | bytes 2359304 | tf_op jit(solution)/shard_map/ppermute | solution.py:624
  195.9 30.8 %collective-permute-start.10 = (bf16[4,64,1536]{2,1,0:T(8,128)(2,1)}, bf16[4,64,1536]{2,1,0:T(8,128)(2,1)S(1)}, u32[]{:S(2)}, u32[]{:S(2)}) collective-permute-start(bf16[4,64,1536]{2,1,0:T(8,128)(2,1)} %get-tuple-element.77), channel_id=1, source_target_pairs={{0,4},{1,5},{2,6},{3,7},{4,0},{5,1},{6,2},{7,3},{8,12},{9,13},{10,... | collective-permute-start | bytes 2359304 | tf_op jit(solution)/shard_map/ppermute | solution.py:624
  197.9 28.8 %collective-permute-start.11 = (bf16[4,64,1536]{2,1,0:T(8,128)(2,1)}, bf16[4,64,1536]{2,1,0:T(8,128)(2,1)S(1)}, u32[]{:S(2)}, u32[]{:S(2)}) collective-permute-start(bf16[4,64,1536]{2,1,0:T(8,128)(2,1)} %get-tuple-element.78), channel_id=1, source_target_pairs={{0,1},{1,0},{2,3},{3,2},{4,5},{5,4},{6,7},{7,6},{8,9},{9,8},{10,11... | collective-permute-start | bytes 2359304 | tf_op jit(solution)/shard_map/ppermute | solution.py:624
  226.7 1.4 copy-start.15
  226.7 1.6 copy-start.13
  226.7 2.2 copy-start.2
  228.8 30.6 %all-to-all-start.4 = ((bf16[4,4,192,256]{3,2,1,0:T(8,128)(2,1)}), bf16[4,4,192,256]{3,2,1,0:T(8,128)(2,1)S(1)}, u32[]{:S(2)}, u32[]{:S(2)}) async-start(bf16[4,4,192,256]{3,2,1,0:T(8,128)(2,1)} %copy.18), calls=%async_computation.4 | async-start | bytes 3145728 | tf_op jit(solution)/shard_map/all_to_all | solution.py:710
  232.6 6.9 %copy-start.12 = (bf16[4,64,1536]{2,1,0:T(8,128)(2,1)S(1)}, bf16[4,64,1536]{2,1,0:T(8,128)(2,1)}, u32[]{:S(2)}) copy-start(bf16[4,64,1536]{2,1,0:T(8,128)(2,1)} %get-tuple-element.83) | copy-start | bytes 2359300
  239.5 1.9 copy-start.11
  239.5 1.9 copy-start.16
  239.5 5.6 %collective-permute-start.12 = (bf16[4,128,768]{2,1,0:T(8,128)(2,1)}, bf16[4,128,768]{2,1,0:T(8,128)(2,1)S(1)}, u32[]{:S(2)}, u32[]{:S(2)}) collective-permute-start(bf16[4,128,768]{2,1,0:T(8,128)(2,1)} %get-tuple-element.82), channel_id=1, source_target_pairs={{0,16},{16,0},{1,17},{17,1},{2,18},{18,2},{3,19},{19,3},{4,20},{20... | collective-permute-start | bytes 2359304 | tf_op jit(solution)/shard_map/ppermute | solution.py:601
  240.9 2.5 copy-start.10
  240.9 2.5 copy-start.14
  241.0 11.5 %collective-permute-start.13 = (bf16[2,64,1536]{2,1,0:T(8,128)(2,1)S(1)}, bf16[2,64,1536]{2,1,0:T(8,128)(2,1)S(1)}, u32[]{:S(2)}, u32[]{:S(2)}) collective-permute-start(bf16[2,64,1536]{2,1,0:T(8,128)(2,1)S(1)} %get-tuple-element.109), channel_id=1, source_target_pairs={{0,4},{1,5},{2,6},{3,7},{4,0},{5,1},{6,2},{7,3},{8,12},{9,13},{10,... | collective-permute-start | bytes 1179656 | tf_op jit(solution)/shard_map/ppermute | solution.py:624
  241.6 3.6 %copy-start.6 = (f32[4,128,768]{2,1,0:T(8,128)S(1)}, f32[4,128,768]{2,1,0:T(8,128)}, u32[]{:S(2)}) copy-start(f32[4,128,768]{2,1,0:T(8,128)} %get-tuple-element.81) | copy-start | bytes 4718596
  241.6 17.1 %collective-permute-start.14 = (bf16[2,64,1536]{2,1,0:T(8,128)(2,1)S(1)}, bf16[2,64,1536]{2,1,0:T(8,128)(2,1)S(1)}, u32[]{:S(2)}, u32[]{:S(2)}) collective-permute-start(bf16[2,64,1536]{2,1,0:T(8,128)(2,1)S(1)} %get-tuple-element.107), channel_id=1, source_target_pairs={{0,1},{1,0},{2,3},{3,2},{4,5},{5,4},{6,7},{7,6},{8,9},{9,8},{10,11... | collective-permute-start | bytes 1179656 | tf_op jit(solution)/shard_map/ppermute | solution.py:624
  243.6 15.8 %collective-permute-start.15 = (bf16[2,64,1536]{2,1,0:T(8,128)(2,1)S(1)}, bf16[2,64,1536]{2,1,0:T(8,128)(2,1)S(1)}, u32[]{:S(2)}, u32[]{:S(2)}) collective-permute-start(bf16[2,64,1536]{2,1,0:T(8,128)(2,1)S(1)} %get-tuple-element.105), channel_id=1, source_target_pairs={{0,2},{1,3},{2,0},{3,1},{4,6},{5,7},{6,4},{7,5},{8,10},{9,11},{10,... | collective-permute-start | bytes 1179656 | tf_op jit(solution)/shard_map/ppermute | solution.py:624
  252.4 6.3 %copy-start.17 = (bf16[2,64,1536]{2,1,0:T(8,128)(2,1)}, bf16[2,64,1536]{2,1,0:T(8,128)(2,1)S(1)}, u32[]{:S(2)}) copy-start(bf16[2,64,1536]{2,1,0:T(8,128)(2,1)S(1)} %collective-permute-done.13) | copy-start | bytes 1179652
  258.7 0.8 copy-start.19
  259.4 0.7 copy-start.21
  260.2 50.5 %all-to-all-start.5 = ((bf16[16,32,768]{2,1,0:T(8,128)(2,1)}), bf16[16,32,768]{2,1,0:T(8,128)(2,1)S(1)}, u32[]{:S(2)}, u32[]{:S(2)}) async-start(bf16[16,32,768]{2,1,0:T(8,128)(2,1)} %bitcast.39), calls=%async_computation.5 | async-start | bytes 1572864 | tf_op jit(solution)/shard_map/all_to_all | solution.py:736
  267.5 35.8 %collective-permute-start.16 = (bf16[64,1536]{1,0:T(8,128)(2,1)}, bf16[64,1536]{1,0:T(8,128)(2,1)}, u32[]{:S(2)}, u32[]{:S(2)}) collective-permute-start(bf16[64,1536]{1,0:T(8,128)(2,1)} %fusion.12), channel_id=1, source_target_pairs={{0,8},{1,9},{2,10},{3,11},{4,12},{5,13},{6,14},{7,15},{8,0},{9,1},... | collective-permute-start | bytes 589832 | tf_op jit(solution)/shard_map/ppermute | solution.py:624
  271.9 35.6 %collective-permute-start.17 = (bf16[64,1536]{1,0:T(8,128)(2,1)}, bf16[64,1536]{1,0:T(8,128)(2,1)}, u32[]{:S(2)}, u32[]{:S(2)}) collective-permute-start(bf16[64,1536]{1,0:T(8,128)(2,1)} %fusion.13), channel_id=1, source_target_pairs={{0,8},{1,9},{2,10},{3,11},{4,12},{5,13},{6,14},{7,15},{8,0},{9,1},... | collective-permute-start | bytes 589832 | tf_op jit(solution)/shard_map/ppermute | solution.py:624
  273.7 37.0 %collective-permute-start.18 = (bf16[64,1536]{1,0:T(8,128)(2,1)}, bf16[64,1536]{1,0:T(8,128)(2,1)}, u32[]{:S(2)}, u32[]{:S(2)}) collective-permute-start(bf16[64,1536]{1,0:T(8,128)(2,1)} %fusion.14), channel_id=1, source_target_pairs={{0,8},{1,9},{2,10},{3,11},{4,12},{5,13},{6,14},{7,15},{8,0},{9,1},... | collective-permute-start | bytes 589832 | tf_op jit(solution)/shard_map/ppermute | solution.py:624
  310.7 1.2 copy-start.18
  310.8 2.1 copy-start.20
  310.8 2.1 copy-start.22
  311.8 2.9 collective-permute-start.19
  314.2 4.0 %collective-permute-start.20 = (bf16[64,4608]{1,0:T(8,128)(2,1)S(1)}, bf16[64,4608]{1,0:T(8,128)(2,1)S(1)}, u32[]{:S(2)}, u32[]{:S(2)}) collective-permute-start(bf16[64,4608]{1,0:T(8,128)(2,1)S(1)} %pad_maximum_fusion.1), channel_id=1, source_target_pairs={{0,16},{16,0},{1,17},{17,1},{2,18},{18,2},{3,19},{19,3},{4,20},{20... | collective-permute-start | bytes 1769480 | tf_op jit(solution)/shard_map/ppermute | solution.py:601
Sparse Core Ops, SparseCore 0:
  25.4 48.0 all-gather.2
